TPU v7x, 256 devices: a whole 4x4x8 slice. The times are simulated.
256 devices in a mesh: tm: 8 (over y, core), mp: 4 (over z_lo), tok: 8 (over z_hi, x).
Axes of the slice: x: 4, y: 4, z: 8 (z_hi: 2, z_lo: 4; z = z_hi * 4 + z_lo), core: 2. Of those that a mesh axis runs over, the one named last changes fastest.
Arguments:
- features: bfloat16 [1024, 3584], P('tok'), may hold values from -6 to 6
- spike_mask: int32 [8, 1024, 3584], P('tm', 'tok'), may hold values 0 or 1
- gate_weight: bfloat16 [3584, 7168], P(('tm', 'tok'), 'mp'), may hold values from -0.09375 to 0.09375
- threshold: float32 [7168], P('mp'), may hold values from 0.5 to 2
Outputs:
- rates: float32 [1024, 7168], P('tok', 'mp')
- grad_threshold: float32 [7168], P('mp')
All inputs are finite; a program needn't handle non-finite values. No bound on the sum of `spike_mask` on one device may be relied on, other than what follows from the above.
Results may differ from a plain program's by a relative error of at most 0.00035.
Values may be sent and summed in bfloat16 or wider, within the bound.
No kernel may reach another device: no remote copies, remote signals or barrier semaphores. Data moves between devices by JAX's collectives and lax.ppermute only.
A program may use at most 64 MiB of HBM per device.

v0:
```python
import jax
import jax.numpy as jnp
from jax import lax
from jax.sharding import PartitionSpec as P

SHARP = 2.0


def passed_along(x, axis, by):
    peers = lax.axis_size(axis)
    pairs = [(i, i + by) for i in range(peers) if 0 <= i + by < peers]
    return lax.ppermute(x, axis, pairs)


def on_device(features, spike_mask, gate_weight, threshold):
    steps = lax.axis_size("tm")
    step_index = lax.axis_index("tm")
    tokens_all = features.shape[0] * lax.axis_size("tok")
    rows = features.shape[0]
    width = gate_weight.shape[1]
    driven = jnp.where(spike_mask[0] > 0, features, jnp.zeros_like(features))
    piece = lax.all_gather(gate_weight, ("tm", "tok"), axis=0, tiled=True)
    student = jnp.dot(driven, piece, preferred_element_type=jnp.float32)
    teacher = jnp.dot(features, piece, preferred_element_type=jnp.float32)
    current = 2.0 * student
    target = jax.nn.silu(teacher)
    blocks = 1
    size = rows // blocks
    turns = steps + blocks - 1

    def forward_turn(turn, carry):
        incoming, spikes = carry
        block = turn - step_index
        active = (block >= 0) & (block < blocks)
        rising = incoming + current
        fired = jax.nn.sigmoid(SHARP * (rising - threshold))
        leaving = rising - threshold * fired
        older = spikes
        spikes = jnp.where(active, fired, older)
        passed = passed_along(leaving, "tm", 1)
        return (passed, spikes)

    block_zero = jnp.zeros((size, width), jnp.float32)
    unused, spikes = lax.fori_loop(
        0, turns, forward_turn, (block_zero, jnp.zeros((rows, width), jnp.float32))
    )
    total = lax.psum(spikes, "tm")
    rates = threshold * total / steps
    error = (rates - target) / tokens_all

    def backward_turn(turn, carry):
        incoming, grad_sum = carry
        block = turn - (steps - 1 - step_index)
        active = (block >= 0) & (block < blocks)
        dspike = error * threshold / steps - threshold * incoming
        dwide = dspike * SHARP * spikes * (1.0 - spikes)
        term = jnp.sum(-dwide - spikes * incoming + error * spikes / steps, axis=0)
        grad_sum = grad_sum + jnp.where(active, term, jnp.zeros_like(term))
        passed = passed_along((incoming + dwide).astype(jnp.bfloat16), "tm", -1).astype(jnp.float32)
        return (passed, grad_sum)

    unused_cot, grad_local = lax.fori_loop(
        0, turns, backward_turn, (block_zero, jnp.zeros((width,), jnp.float32))
    )
    grad_threshold = lax.psum(grad_local, ("tm", "tok"))
    return (rates, grad_threshold)


def solution(mesh):
    return jax.shard_map(
        on_device,
        mesh=mesh,
        in_specs=(P("tok", None), P("tm", "tok", None), P(("tm", "tok"), "mp"), P("mp")),
        out_specs=(P("tok", "mp"), P("mp")),
        check_vma=False,
    )
```

profile of v0, /device:TPU:32, one launch (start us, length us, event | category | flops | bytes accessed | tf_op | source)
XLA Modules:
  0.0 676.2 jit_solution(10581541776726929995)
XLA Ops:
  8.0 140.1 %all-gather.2.cloned.1.call-done = bf16[3584,1792]{1,0:T(8,128)(2,1)} async-done(((bf16[56,1792]{1,0:T(8,128)(2,1)}), bf16[3584,1792]{1,0:T(8,128)(2,1)}) %all-gather.2.cloned.1.call-update) | async-done | bytes 12845072 | tf_op jit(solution)/shard_map/all_gather | solution.py:22
  148.0 7.4 %convolution_multiply_fusion = f32[128,1792]{1,0:T(8,128)S(1)} fusion(bf16[3584,1792]{1,0:T(8,128)(2,1)} %all-gather.2.cloned.1.call-done, bf16[128,3584]{1,0:T(8,128)(2,1)} %param.8, s32[1,128,3584]{2,1,0:T(8,128)} %param.9), kind=kOutput, calls=%fused_computation.8 | convolution fusion | flops 1645314048 | bytes 16515072 | tf_op jit(solution)/shard_map/dot_general | solution.py:23
  155.5 120.2 %while.34 = (s32[]{:T(128)}, f32[128,1792]{1,0:T(8,128)S(1)}, f32[128,1792]{1,0:T(8,128)S(1)}, f32[128,1792]{1,0:T(8,128)S(1)}, f32[1792]{0:T(1024)S(1)}, /*index=5*/s32[]{:T(128)}, s32[]{:T(128)}, s32[]{:T(128)}) while((s32[]{:T(128)}, f32[128,1792]{1,0:T(8,128)S(1)}, f32[128,1792]{1,0:T(8,128)S(1)}, f32[128,1792]{1,0:T(8,128)S(1)}, ...), condition=%wide.region_1.2_spmd.clone, body=%wide.region_0.1_spmd.clone.sunk | while | flops 2293767 | bytes 8264873 | solution.py:44
  155.5 1.5 select_select_fusion.2
  157.1 2.2 collective-permute-start
  159.3 2.2 collective-permute-done
  163.1 11.6 %collective-permute-start = (f32[128,1792]{1,0:T(8,128)}, f32[128,1792]{1,0:T(8,128)S(1)}, u32[]{:S(2)}, u32[]{:S(2)}) collective-permute-start(f32[128,1792]{1,0:T(8,128)} %get-tuple-element.455), channel_id=1, source_target_pairs={{0,32},{32,64},{64,96},{96,128},{128,160},{160,192},{192,224},{1,3... | collective-permute-start | bytes 2752520 | tf_op jit(solution)/shard_map/while/body/eval_jaxpr/ppermute | solution.py:12
  174.7 2.2 collective-permute-done
  176.9 1.5 select_select_fusion.2
  178.4 12.7 %collective-permute-start = (f32[128,1792]{1,0:T(8,128)}, f32[128,1792]{1,0:T(8,128)S(1)}, u32[]{:S(2)}, u32[]{:S(2)}) collective-permute-start(f32[128,1792]{1,0:T(8,128)} %get-tuple-element.455), channel_id=1, source_target_pairs={{0,32},{32,64},{64,96},{96,128},{128,160},{160,192},{192,224},{1,3... | collective-permute-start | bytes 2752520 | tf_op jit(solution)/shard_map/while/body/eval_jaxpr/ppermute | solution.py:12
  191.1 2.2 collective-permute-done
  194.9 12.7 %collective-permute-start = (f32[128,1792]{1,0:T(8,128)}, f32[128,1792]{1,0:T(8,128)S(1)}, u32[]{:S(2)}, u32[]{:S(2)}) collective-permute-start(f32[128,1792]{1,0:T(8,128)} %get-tuple-element.455), channel_id=1, source_target_pairs={{0,32},{32,64},{64,96},{96,128},{128,160},{160,192},{192,224},{1,3... | collective-permute-start | bytes 2752520 | tf_op jit(solution)/shard_map/while/body/eval_jaxpr/ppermute | solution.py:12
  207.6 2.2 collective-permute-done
  211.4 12.7 %collective-permute-start = (f32[128,1792]{1,0:T(8,128)}, f32[128,1792]{1,0:T(8,128)S(1)}, u32[]{:S(2)}, u32[]{:S(2)}) collective-permute-start(f32[128,1792]{1,0:T(8,128)} %get-tuple-element.455), channel_id=1, source_target_pairs={{0,32},{32,64},{64,96},{96,128},{128,160},{160,192},{192,224},{1,3... | collective-permute-start | bytes 2752520 | tf_op jit(solution)/shard_map/while/body/eval_jaxpr/ppermute | solution.py:12
  224.0 2.2 collective-permute-done
  227.8 12.7 %collective-permute-start = (f32[128,1792]{1,0:T(8,128)}, f32[128,1792]{1,0:T(8,128)S(1)}, u32[]{:S(2)}, u32[]{:S(2)}) collective-permute-start(f32[128,1792]{1,0:T(8,128)} %get-tuple-element.455), channel_id=1, source_target_pairs={{0,32},{32,64},{64,96},{96,128},{128,160},{160,192},{192,224},{1,3... | collective-permute-start | bytes 2752520 | tf_op jit(solution)/shard_map/while/body/eval_jaxpr/ppermute | solution.py:12
  240.5 2.2 collective-permute-done
  244.3 12.7 %collective-permute-start = (f32[128,1792]{1,0:T(8,128)}, f32[128,1792]{1,0:T(8,128)S(1)}, u32[]{:S(2)}, u32[]{:S(2)}) collective-permute-start(f32[128,1792]{1,0:T(8,128)} %get-tuple-element.455), channel_id=1, source_target_pairs={{0,32},{32,64},{64,96},{96,128},{128,160},{160,192},{192,224},{1,3... | collective-permute-start | bytes 2752520 | tf_op jit(solution)/shard_map/while/body/eval_jaxpr/ppermute | solution.py:12
  256.9 2.2 collective-permute-done
  260.7 12.7 %collective-permute-start = (f32[128,1792]{1,0:T(8,128)}, f32[128,1792]{1,0:T(8,128)S(1)}, u32[]{:S(2)}, u32[]{:S(2)}) collective-permute-start(f32[128,1792]{1,0:T(8,128)} %get-tuple-element.455), channel_id=1, source_target_pairs={{0,32},{32,64},{64,96},{96,128},{128,160},{160,192},{192,224},{1,3... | collective-permute-start | bytes 2752520 | tf_op jit(solution)/shard_map/while/body/eval_jaxpr/ppermute | solution.py:12
  273.4 2.2 collective-permute-done
  276.7 74.4 %all-reduce.2.cloned.1.call-done = f32[128,1792]{1,0:T(8,128)} async-done(((f32[128,1792]{1,0:T(8,128)}), f32[128,1792]{1,0:T(8,128)}) %all-reduce.2.cloned.1.call-update) | async-done | bytes 917520 | tf_op jit(solution)/shard_map/psum | solution.py:47
  351.1 8.4 %fusion.4 = (f32[128,1792]{1,0:T(8,128)S(1)}, f32[128,1792]{1,0:T(8,128)S(1)}, f32[128,1792]{1,0:T(8,128)}) fusion(f32[128,1792]{1,0:T(8,128)} %copy-done, f32[128,1792]{1,0:T(8,128)} %all-reduce.2.cloned.1.call-done, f32[1792]{0:T(1024)S(1)} %get-tuple-element.528, bf16[128,3584]{1,0:T(8,128)(2,1)} %param.8, ...), kind=kOutput, calls=%fused_computation.16 | convolution fusion | flops 1646231552 | bytes 18357248 | tf_op jit(solution)/shard_map/dot_general | solution.py:24
  359.4 99.1 %while.35 = (s32[]{:T(128)}, f32[128,1792]{1,0:T(8,128)}, f32[1792]{0:T(1024)S(1)}, f32[1792]{0:T(1024)S(1)}, f32[128,1792]{1,0:T(8,128)S(1)}, /*index=5*/f32[12...) while((s32[]{:T(128)}, f32[128,1792]{1,0:T(8,128)}, ...), condition=%wide.region_5.6_spmd.clone, body=%wide.region_3.5_spmd.clone.sunk | while | flops 4132359 | bytes 7376058 | solution.py:62
  361.3 2.5 collective-permute-done.1
  363.8 2.0 convert_element_type.22
  365.8 1.7 add_reduce_fusion.2
  368.8 5.9 collective-permute-done.1
  374.7 2.0 convert_element_type.22
  376.8 1.7 add_reduce_fusion.2
  379.8 8.6 %collective-permute-done.1 = bf16[128,1792]{1,0:T(8,128)(2,1)} collective-permute-done((bf16[128,1792]{1,0:T(8,128)(2,1)S(1)}, bf16[128,1792]{1,0:T(8,128)(2,1)}, u32[]{:S(2)}, u32[]{:S(2)}) %collective-permute-start.1) | collective-permute-done | bytes 458784 | tf_op jit(solution)/shard_map/while/body/eval_jaxpr/ppermute | solution.py:12
  388.4 2.0 convert_element_type.22
  390.4 1.7 add_reduce_fusion.2
  393.4 8.6 %collective-permute-done.1 = bf16[128,1792]{1,0:T(8,128)(2,1)} collective-permute-done((bf16[128,1792]{1,0:T(8,128)(2,1)S(1)}, bf16[128,1792]{1,0:T(8,128)(2,1)}, u32[]{:S(2)}, u32[]{:S(2)}) %collective-permute-start.1) | collective-permute-done | bytes 458784 | tf_op jit(solution)/shard_map/while/body/eval_jaxpr/ppermute | solution.py:12
  402.0 2.0 convert_element_type.22
  404.0 1.7 add_reduce_fusion.2
  407.0 8.6 %collective-permute-done.1 = bf16[128,1792]{1,0:T(8,128)(2,1)} collective-permute-done((bf16[128,1792]{1,0:T(8,128)(2,1)S(1)}, bf16[128,1792]{1,0:T(8,128)(2,1)}, u32[]{:S(2)}, u32[]{:S(2)}) %collective-permute-start.1) | collective-permute-done | bytes 458784 | tf_op jit(solution)/shard_map/while/body/eval_jaxpr/ppermute | solution.py:12
  415.6 2.0 convert_element_type.22
  417.6 1.7 add_reduce_fusion.2
  420.7 8.6 %collective-permute-done.1 = bf16[128,1792]{1,0:T(8,128)(2,1)} collective-permute-done((bf16[128,1792]{1,0:T(8,128)(2,1)S(1)}, bf16[128,1792]{1,0:T(8,128)(2,1)}, u32[]{:S(2)}, u32[]{:S(2)}) %collective-permute-start.1) | collective-permute-done | bytes 458784 | tf_op jit(solution)/shard_map/while/body/eval_jaxpr/ppermute | solution.py:12
  429.2 2.0 convert_element_type.22
  431.3 1.7 add_reduce_fusion.2
  434.3 8.6 %collective-permute-done.1 = bf16[128,1792]{1,0:T(8,128)(2,1)} collective-permute-done((bf16[128,1792]{1,0:T(8,128)(2,1)S(1)}, bf16[128,1792]{1,0:T(8,128)(2,1)}, u32[]{:S(2)}, u32[]{:S(2)}) %collective-permute-start.1) | collective-permute-done | bytes 458784 | tf_op jit(solution)/shard_map/while/body/eval_jaxpr/ppermute | solution.py:12
  442.9 2.0 convert_element_type.22
  444.9 1.7 add_reduce_fusion.2
  447.9 8.6 %collective-permute-done.1 = bf16[128,1792]{1,0:T(8,128)(2,1)} collective-permute-done((bf16[128,1792]{1,0:T(8,128)(2,1)S(1)}, bf16[128,1792]{1,0:T(8,128)(2,1)}, u32[]{:S(2)}, u32[]{:S(2)}) %collective-permute-start.1) | collective-permute-done | bytes 458784 | tf_op jit(solution)/shard_map/while/body/eval_jaxpr/ppermute | solution.py:12
  456.5 2.0 convert_element_type.22
  458.5 210.8 %psum.15 = f32[1792]{0:T(1024)} all-reduce(f32[1792]{0:T(1024)S(1)} %get-tuple-element.289), channel_id=1, replica_groups=mesh['tm'=8,'mp'=4,'tok'=8] {'tm','tok'}, use_global_device_ids=true, to_apply=%region_6.7 | all-reduce | flops 1792 | bytes 14336 | tf_op jit(solution)/shard_map/psum | solution.py:65
  (37 shorter events, 22.0 us)
Async XLA Ops:
  7.2 140.9 %all-gather.2.cloned.1.call-start = ((), (), s32[]{:S(2)}) async-start(), calls=%async_computation | async-start | bytes 13045760 | tf_op jit(solution)/shard_map/all_gather | solution.py:22
  7.9 343.2 %all-reduce.2.cloned.1.call-start = ((), (), s32[]{:S(2)}) async-start(), calls=%async_computation.1 | async-start | bytes 1835008 | tf_op jit(solution)/shard_map/psum | solution.py:47
  8.0 147.5 %copy-start.2 = (f32[1792]{0:T(1024)S(1)}, f32[1792]{0:T(1024)}, u32[]{:S(2)}) copy-start(f32[1792]{0:T(1024)} %param.11) | copy-start | bytes 21508
  157.1 4.5 collective-permute-start
  163.1 13.8 %collective-permute-start = (f32[128,1792]{1,0:T(8,128)}, f32[128,1792]{1,0:T(8,128)S(1)}, u32[]{:S(2)}, u32[]{:S(2)}) collective-permute-start(f32[128,1792]{1,0:T(8,128)} %get-tuple-element.455), channel_id=1, source_target_pairs={{0,32},{32,64},{64,96},{96,128},{128,160},{160,192},{192,224},{1,3... | collective-permute-start | bytes 2752520 | tf_op jit(solution)/shard_map/while/body/eval_jaxpr/ppermute | solution.py:12
  178.4 14.9 %collective-permute-start = (f32[128,1792]{1,0:T(8,128)}, f32[128,1792]{1,0:T(8,128)S(1)}, u32[]{:S(2)}, u32[]{:S(2)}) collective-permute-start(f32[128,1792]{1,0:T(8,128)} %get-tuple-element.455), channel_id=1, source_target_pairs={{0,32},{32,64},{64,96},{96,128},{128,160},{160,192},{192,224},{1,3... | collective-permute-start | bytes 2752520 | tf_op jit(solution)/shard_map/while/body/eval_jaxpr/ppermute | solution.py:12
  194.9 14.9 %collective-permute-start = (f32[128,1792]{1,0:T(8,128)}, f32[128,1792]{1,0:T(8,128)S(1)}, u32[]{:S(2)}, u32[]{:S(2)}) collective-permute-start(f32[128,1792]{1,0:T(8,128)} %get-tuple-element.455), channel_id=1, source_target_pairs={{0,32},{32,64},{64,96},{96,128},{128,160},{160,192},{192,224},{1,3... | collective-permute-start | bytes 2752520 | tf_op jit(solution)/shard_map/while/body/eval_jaxpr/ppermute | solution.py:12
  211.4 14.9 %collective-permute-start = (f32[128,1792]{1,0:T(8,128)}, f32[128,1792]{1,0:T(8,128)S(1)}, u32[]{:S(2)}, u32[]{:S(2)}) collective-permute-start(f32[128,1792]{1,0:T(8,128)} %get-tuple-element.455), channel_id=1, source_target_pairs={{0,32},{32,64},{64,96},{96,128},{128,160},{160,192},{192,224},{1,3... | collective-permute-start | bytes 2752520 | tf_op jit(solution)/shard_map/while/body/eval_jaxpr/ppermute | solution.py:12
  227.8 14.9 %collective-permute-start = (f32[128,1792]{1,0:T(8,128)}, f32[128,1792]{1,0:T(8,128)S(1)}, u32[]{:S(2)}, u32[]{:S(2)}) collective-permute-start(f32[128,1792]{1,0:T(8,128)} %get-tuple-element.455), channel_id=1, source_target_pairs={{0,32},{32,64},{64,96},{96,128},{128,160},{160,192},{192,224},{1,3... | collective-permute-start | bytes 2752520 | tf_op jit(solution)/shard_map/while/body/eval_jaxpr/ppermute | solution.py:12
  244.3 14.9 %collective-permute-start = (f32[128,1792]{1,0:T(8,128)}, f32[128,1792]{1,0:T(8,128)S(1)}, u32[]{:S(2)}, u32[]{:S(2)}) collective-permute-start(f32[128,1792]{1,0:T(8,128)} %get-tuple-element.455), channel_id=1, source_target_pairs={{0,32},{32,64},{64,96},{96,128},{128,160},{160,192},{192,224},{1,3... | collective-permute-start | bytes 2752520 | tf_op jit(solution)/shard_map/while/body/eval_jaxpr/ppermute | solution.py:12
  260.7 14.9 %collective-permute-start = (f32[128,1792]{1,0:T(8,128)}, f32[128,1792]{1,0:T(8,128)S(1)}, u32[]{:S(2)}, u32[]{:S(2)}) collective-permute-start(f32[128,1792]{1,0:T(8,128)} %get-tuple-element.455), channel_id=1, source_target_pairs={{0,32},{32,64},{64,96},{96,128},{128,160},{160,192},{192,224},{1,3... | collective-permute-start | bytes 2752520 | tf_op jit(solution)/shard_map/while/body/eval_jaxpr/ppermute | solution.py:12
  275.6 1.0 copy-start
  276.7 82.8 %copy-start.1 = (f32[128,1792]{1,0:T(8,128)S(1)}, f32[128,1792]{1,0:T(8,128)}, u32[]{:S(2)}) copy-start(f32[128,1792]{1,0:T(8,128)} %copy-done) | copy-start | bytes 2752516
  360.0 3.8 collective-permute-start.1
  367.5 7.2 %collective-permute-start.1 = (bf16[128,1792]{1,0:T(8,128)(2,1)S(1)}, bf16[128,1792]{1,0:T(8,128)(2,1)}, u32[]{:S(2)}, u32[]{:S(2)}) collective-permute-start(bf16[128,1792]{1,0:T(8,128)(2,1)S(1)} %get-tuple-element.465), channel_id=1, source_target_pairs={{32,0},{64,32},{96,64},{128,96},{160,128},{192,160},{224,192},{33,... | collective-permute-start | bytes 1376264 | tf_op jit(solution)/shard_map/while/body/eval_jaxpr/ppermute | solution.py:12
  378.5 9.9 %collective-permute-start.1 = (bf16[128,1792]{1,0:T(8,128)(2,1)S(1)}, bf16[128,1792]{1,0:T(8,128)(2,1)}, u32[]{:S(2)}, u32[]{:S(2)}) collective-permute-start(bf16[128,1792]{1,0:T(8,128)(2,1)S(1)} %get-tuple-element.465), channel_id=1, source_target_pairs={{32,0},{64,32},{96,64},{128,96},{160,128},{192,160},{224,192},{33,... | collective-permute-start | bytes 1376264 | tf_op jit(solution)/shard_map/while/body/eval_jaxpr/ppermute | solution.py:12
  392.1 9.9 %collective-permute-start.1 = (bf16[128,1792]{1,0:T(8,128)(2,1)S(1)}, bf16[128,1792]{1,0:T(8,128)(2,1)}, u32[]{:S(2)}, u32[]{:S(2)}) collective-permute-start(bf16[128,1792]{1,0:T(8,128)(2,1)S(1)} %get-tuple-element.465), channel_id=1, source_target_pairs={{32,0},{64,32},{96,64},{128,96},{160,128},{192,160},{224,192},{33,... | collective-permute-start | bytes 1376264 | tf_op jit(solution)/shard_map/while/body/eval_jaxpr/ppermute | solution.py:12
  405.7 9.9 %collective-permute-start.1 = (bf16[128,1792]{1,0:T(8,128)(2,1)S(1)}, bf16[128,1792]{1,0:T(8,128)(2,1)}, u32[]{:S(2)}, u32[]{:S(2)}) collective-permute-start(bf16[128,1792]{1,0:T(8,128)(2,1)S(1)} %get-tuple-element.465), channel_id=1, source_target_pairs={{32,0},{64,32},{96,64},{128,96},{160,128},{192,160},{224,192},{33,... | collective-permute-start | bytes 1376264 | tf_op jit(solution)/shard_map/while/body/eval_jaxpr/ppermute | solution.py:12
  419.3 9.9 %collective-permute-start.1 = (bf16[128,1792]{1,0:T(8,128)(2,1)S(1)}, bf16[128,1792]{1,0:T(8,128)(2,1)}, u32[]{:S(2)}, u32[]{:S(2)}) collective-permute-start(bf16[128,1792]{1,0:T(8,128)(2,1)S(1)} %get-tuple-element.465), channel_id=1, source_target_pairs={{32,0},{64,32},{96,64},{128,96},{160,128},{192,160},{224,192},{33,... | collective-permute-start | bytes 1376264 | tf_op jit(solution)/shard_map/while/body/eval_jaxpr/ppermute | solution.py:12
  433.0 9.9 %collective-permute-start.1 = (bf16[128,1792]{1,0:T(8,128)(2,1)S(1)}, bf16[128,1792]{1,0:T(8,128)(2,1)}, u32[]{:S(2)}, u32[]{:S(2)}) collective-permute-start(bf16[128,1792]{1,0:T(8,128)(2,1)S(1)} %get-tuple-element.465), channel_id=1, source_target_pairs={{32,0},{64,32},{96,64},{128,96},{160,128},{192,160},{224,192},{33,... | collective-permute-start | bytes 1376264 | tf_op jit(solution)/shard_map/while/body/eval_jaxpr/ppermute | solution.py:12
  446.6 9.9 %collective-permute-start.1 = (bf16[128,1792]{1,0:T(8,128)(2,1)S(1)}, bf16[128,1792]{1,0:T(8,128)(2,1)}, u32[]{:S(2)}, u32[]{:S(2)}) collective-permute-start(bf16[128,1792]{1,0:T(8,128)(2,1)S(1)} %get-tuple-element.465), channel_id=1, source_target_pairs={{32,0},{64,32},{96,64},{128,96},{160,128},{192,160},{224,192},{33,... | collective-permute-start | bytes 1376264 | tf_op jit(solution)/shard_map/while/body/eval_jaxpr/ppermute | solution.py:12
Sparse Core Ops, SparseCore 0:
  11.7 136.3 all-gather.1
  276.8 74.2 all-reduce.1
where the time goes:
time: 677 us; the launch traced here: 676 us
  waiting for transfers between devices  293 us (43%)
  blocking collectives  211 us (31%)
  starting transfers between devices  100 us (15%)
  other arithmetic  41 us (6%)
  matrix products  15.7 us (2%)
  between operations  14.1 us (2%)
    psum x1, blocking collectives, on_device(): grad_threshold = lax.psum(grad_local, ('tm', 'tok'))  211 us
    all_gather x1, waiting for transfers between devices, on_device(): piece = lax.all_gather(gate_weight, ('tm', 'tok'), axis=0, tiled=True)  140 us
    ppermute x16, starting transfers between devices, passed_along(): return lax.ppermute(x, axis, pairs)  100 us
    ppermute x16, waiting for transfers between devices, passed_along(): return lax.ppermute(x, axis, pairs)  77.7 us
    psum x1, waiting for transfers between devices, on_device(): total = lax.psum(spikes, 'tm')  74.4 us
    convert_element_type x8, other arithmetic, backward_turn(): passed_along((incoming + dwide).astype(jnp.bfloat16), 'tm', -1)  16.3 us
  transfers between devices with their start and end apart: 18, of which 18 were waited for; matrix products, arithmetic and copies ran while one was open for 0% of the time, Pallas kernels for 0%

commit v1 on v0

v1 whole, which is shorter than its diff:
```python
import functools
import jax
import jax.numpy as jnp
from jax import lax
from jax.experimental import pallas as pl
from jax.experimental.pallas import tpu as pltpu
from jax.sharding import Mesh, PartitionSpec as P

SHARP = 2.0
STARTS = (0, 384, 896, 1280)
WIDE = 512
Y, CORE, Z, X = 4, 2, 2, 4
STEPS = Y * CORE


def around(x, axis, by):
    n = lax.axis_size(axis)
    return lax.ppermute(x, axis, [(i, (i + by) % n) for i in range(n)])


def student_kernel(core_ref, driven_ref, features_ref, mine_ref, other_ref, threshold_ref, rates_ref, grad_ref, current_ref, teacher_ref, *, tokens_all):
    rows = features_ref.shape[0]
    depth = mine_ref.shape[1]
    first = core_ref[0] == 0
    chunk = 2 * depth
    for n in range(0, WIDE, 256):
        total = jnp.zeros((STEPS * rows, 256), jnp.float32)
        teacher = jnp.zeros((rows, 256), jnp.float32)
        for y in range(Y):
            mine = mine_ref[y, :, n : n + 256]
            other = other_ref[y, :, n : n + 256]
            weight = jnp.concatenate(
                [jnp.where(first, mine, other), jnp.where(first, other, mine)], axis=0
            )
            left = driven_ref[:, :, y * chunk : (y + 1) * chunk].reshape(STEPS * rows, chunk)
            total = total + jnp.dot(left, weight, preferred_element_type=jnp.float32)
            teacher = teacher + jnp.dot(
                features_ref[:, y * chunk : (y + 1) * chunk], weight, preferred_element_type=jnp.float32
            )
        current_ref[:, :, n : n + 256] = total.reshape(STEPS, rows, 256)
        teacher_ref[:, n : n + 256] = teacher
    threshold = threshold_ref[...]
    tall = 8

    def strip(i, grad_sum):
        at = pl.ds(pl.multiple_of(i * tall, tall), tall)
        potential = jnp.zeros((tall, WIDE), jnp.float32)
        spikes = []
        for t in range(STEPS):
            rising = potential + 2.0 * current_ref[t, at, :]
            fired = jax.nn.sigmoid(SHARP * (rising - threshold))
            potential = rising - threshold * fired
            spikes.append(fired)
        total = spikes[0]
        for t in range(1, STEPS):
            total = total + spikes[t]
        rates = threshold * total / STEPS
        rates_ref[at, :] = rates
        v = teacher_ref[at, :]
        error = (rates - v * jax.nn.sigmoid(v)) / tokens_all
        cotangent = jnp.zeros((tall, WIDE), jnp.float32)
        for t in reversed(range(STEPS)):
            fired = spikes[t]
            dspike = error * threshold / STEPS - threshold * cotangent
            dwide = dspike * SHARP * fired * (1.0 - fired)
            grad_sum = grad_sum + (-dwide - fired * cotangent + error * fired / STEPS)
            cotangent = cotangent + dwide
        return grad_sum

    grad_sum = lax.fori_loop(0, rows // tall, strip, jnp.zeros((tall, WIDE), jnp.float32))
    grad_ref[...] = jnp.sum(grad_sum, axis=0, keepdims=True)


def place_kernel(at_ref, *refs):
    out_ref = refs[-1]
    half = out_ref.shape[0] // 2
    core, y = at_ref[0], at_ref[1]
    for j in range(Y):
        source = (y + j) % Y
        start = pl.multiple_of(jnp.where(source < 2, 0, 896) + jnp.where(source % 2 == 1, 384, 0), 128)
        for k in range(CORE):
            row = pl.multiple_of(((core + k) % CORE) * half, half)
            piece = refs[CORE * j + k]

            @pl.when(source % 2 == 0)
            def _():
                out_ref[pl.ds(row, half), pl.ds(start, WIDE)] = piece[...]

            @pl.when(source % 2 == 1)
            def _():
                out_ref[pl.ds(row, half), pl.ds(start + 128, WIDE - 128)] = piece[:, 128:]


def on_device(features, spike_mask, gate_weight, threshold):
    core, y, x = lax.axis_index("core"), lax.axis_index("y"), lax.axis_index("x")
    rows, deep = features.shape
    tokens_all = rows * Z * X
    half = rows // CORE
    part, width = gate_weight.shape

    def other_core(v):
        return around(v, "core", 1)

    def tokens_of(v, which):
        return lax.dynamic_slice_in_dim(v, which * half, half, axis=0)

    mine_f = tokens_of(features, core)

    def drive(which):
        return jnp.where(tokens_of(spike_mask[0], which) > 0, tokens_of(features, which), jnp.zeros((), features.dtype))

    give = drive(1 - core)
    keep = drive(core)

    windows = jnp.stack([gate_weight[:, s : s + WIDE] for s in STARTS])
    payload = jnp.concatenate([windows] * Z)
    landed = lax.all_to_all(payload, ("z", "y"), 0, 0, tiled=True)
    wa, wb = landed[:Y], landed[Y:]

    got = other_core(give)
    keep_p, keep_m = around(keep, "y", 1), around(keep, "y", -1)
    got_p, got_m = around(got, "y", 1), around(got, "y", -1)
    keep_f = around(keep_p, "y", 1)
    got_f = around(got_m, "y", -1)

    wa_p, wa_m = around(wa, "x", 1), around(wa, "x", -1)
    wb_p, wb_m = around(wb, "x", 1), around(wb, "x", -1)
    wa_f = around(wa_p, "x", 1)
    wb_f = around(wb_m, "x", -1)

    driven = jnp.zeros((STEPS, half, deep), features.dtype)
    for piece, dy, dc in (
        (keep, 0, 0), (got, 0, 1), (keep_p, -1, 0), (got_p, -1, 1),
        (keep_m, 1, 0), (got_m, 1, 1), (keep_f, 2, 0), (got_f, 2, 1),
    ):
        step = lax.rem(y + dy + Y, Y) * CORE + lax.rem(core + dc, CORE)
        driven = lax.dynamic_update_slice(driven, piece[None], (step, 0, 0))

    mine = jnp.zeros((Y, Z, X, part, WIDE), gate_weight.dtype)
    theirs = jnp.zeros((Y, Z, X, part, WIDE), gate_weight.dtype)
    for piece, z, dx in (
        (wa, 0, 0), (wb, 1, 0), (wa_p, 0, -1), (wb_p, 1, -1),
        (wa_m, 0, 1), (wb_m, 1, 1), (wa_f, 0, 2), (wb_f, 1, 2),
    ):
        at = (0, z, lax.rem(x + dx + X, X), 0, 0)
        mine = lax.dynamic_update_slice(mine, piece[:, None, None], at)
        theirs = lax.dynamic_update_slice(theirs, other_core(piece)[:, None, None], at)
    mine = mine.reshape(Y, Z * X * part, WIDE)
    theirs = theirs.reshape(Y, Z * X * part, WIDE)

    start = jnp.asarray(STARTS, jnp.int32)[y]
    own_threshold = lax.dynamic_slice_in_dim(threshold, start, WIDE)[None]

    smem = pl.BlockSpec(memory_space=pltpu.SMEM)
    vmem = pl.BlockSpec(memory_space=pltpu.VMEM)
    rates, grad = pl.pallas_call(
        functools.partial(student_kernel, tokens_all=tokens_all),
        out_shape=(
            jax.ShapeDtypeStruct((half, WIDE), jnp.float32),
            jax.ShapeDtypeStruct((1, WIDE), jnp.float32),
        ),
        in_specs=[smem] + [vmem] * 5,
        out_specs=(vmem, vmem),
        scratch_shapes=[
            pltpu.VMEM((STEPS, half, WIDE), jnp.float32),
            pltpu.VMEM((half, WIDE), jnp.float32),
        ],
        compiler_params=pltpu.CompilerParams(vmem_limit_bytes=32 * 1024 * 1024),
        cost_estimate=pl.CostEstimate(
            flops=2 * 9 * half * deep * WIDE, bytes_accessed=8 * 1024 * 1024, transcendentals=18 * half * WIDE
        ),
        name="student",
    )(core[None], driven, mine_f, mine, theirs, own_threshold)

    grads = lax.all_to_all(
        jnp.broadcast_to(grad, (Y * CORE * Z * X, WIDE)), ("y", "core", "z", "x"), 0, 0, tiled=True
    )

    quarter = half // 2
    r_p, r_m = around(rates, "y", 1), around(rates, "y", -1)
    r_f = jnp.concatenate([around(r_p[:quarter], "y", 1), around(r_m[quarter:], "y", -1)])
    pieces = []
    for piece in (rates, r_m, r_f, r_p):
        pieces += [piece, other_core(piece)]
    rates_out = pl.pallas_call(
        place_kernel,
        out_shape=jax.ShapeDtypeStruct((rows, width), jnp.float32),
        in_specs=[smem] + [vmem] * 8,
        out_specs=vmem,
        name="place",
    )(jnp.stack([core, y]), *pieces)

    sums = jnp.sum(grads.reshape(Y, CORE * Z * X, WIDE), axis=1)
    grad_out = jnp.concatenate([sums[0], sums[1, 128:], sums[2], sums[3, 128:]])
    return rates_out, grad_out


def solution(mesh):
    grid = mesh.devices.reshape(Y, CORE, mesh.shape["mp"], Z, X)
    fine = Mesh(grid, ("y", "core", "mp", "z", "x"))
    tm, tok = ("y", "core"), ("z", "x")
    return jax.shard_map(
        on_device,
        mesh=fine,
        in_specs=(P(tok, None), P(tm, tok, None), P(tm + tok, "mp"), P("mp")),
        out_specs=(P(tok, "mp"), P("mp")),
        check_vma=False,
    )
```

time: 677 us -> 108 us (0.16)
  the two profiles are of different devices: /device:TPU:32 before, /device:TPU:1 now
where the time goes in v1:
time: 108 us; the launch traced here: 106 us
  starting transfers between devices  51 us (47%)
  waiting for transfers between devices  20.4 us (19%)
  local copies, waits for them, and re-layouts  19.9 us (18%)
  Pallas kernels  9.02 us (8%)
  other arithmetic  3.14 us (3%)
  between operations  3.01 us (3%)
    ppermute x29, starting transfers between devices, around(): return lax.ppermute(x, axis, [(i, (i + by) % n) for i in range(n)])  33.4 us
    ppermute x29, waiting for transfers between devices, around(): return lax.ppermute(x, axis, [(i, (i + by) % n) for i in range(n)])  12.1 us
    all_to_all x1, starting transfers between devices, on_device(): lax.all_to_all(jnp.broadcast_to(grad, (Y * CORE * Z * X, WIDE)), ('y', 'c...  9.69 us
    all_to_all x1, starting transfers between devices, on_device(): landed = lax.all_to_all(payload, ('z', 'y'), 0, 0, tiled=True)  7.87 us
    dynamic_update_slice x7, local copies, waits for them, and re-layouts, on_device(): driven = lax.dynamic_update_slice(driven, piece[None], (step, 0, 0))  7.7 us
    pallas_call x1, Pallas kernels, on_device(): pl.pallas_call(functools.partial(student_kernel, tokens_all=tokens_all),...  6.64 us
    unnamed x33, local copies, waits for them, and re-layouts  6.61 us
    all_to_all x1, waiting for transfers between devices, on_device(): lax.all_to_all(jnp.broadcast_to(grad, (Y * CORE * Z * X, WIDE)), ('y', 'c...  5.05 us
  transfers between devices with their start and end apart: 31, of which 9 were waited for; matrix products, arithmetic and copies ran while one was open for 17% of the time, Pallas kernels for 0%

profile of v1, /device:TPU:1, one launch (start us, length us, event | category | flops | bytes accessed | tf_op | source)
XLA Modules:
  0.0 106.5 jit_solution(12461403720832416922)
XLA Ops:
  0.7 2.1 %broadcast_in_dim.89 = bf16[8,64,3584]{2,1,0:T(8,128)(2,1)} broadcast(bf16[]{:T(256)} %constant.58.clone.1), dimensions={} | broadcast | bytes 3670018 | tf_op jit(solution)/shard_map/broadcast_in_dim | solution.py:131
  2.8 0.9 copy-done.2
  3.7 1.0 bitcast_dynamic-update-slice_fusion.7
  4.7 2.1 %collective-permute-start.1 = (bf16[64,3584]{1,0:T(8,128)(2,1)}, bf16[64,3584]{1,0:T(8,128)(2,1)}, u32[]{:S(2)}, u32[]{:S(2)}) collective-permute-start(bf16[64,3584]{1,0:T(8,128)(2,1)} %get-tuple-element.9), channel_id=1, source_target_pairs={{0,64},{64,128},{128,192},{192,0},{1,65},{65,129},{129,193},{193,1... | collective-permute-start | bytes 1376264 | tf_op jit(solution)/shard_map/ppermute | solution.py:18
  6.8 1.4 %collective-permute-start.3 = (bf16[64,3584]{1,0:T(8,128)(2,1)}, bf16[64,3584]{1,0:T(8,128)(2,1)}, u32[]{:S(2)}, u32[]{:S(2)}) collective-permute-start(bf16[64,3584]{1,0:T(8,128)(2,1)} %get-tuple-element.9), channel_id=1, source_target_pairs={{0,192},{64,0},{128,64},{192,128},{1,193},{65,1},{129,65},{193,129... | collective-permute-start | bytes 1376264 | tf_op jit(solution)/shard_map/ppermute | solution.py:18
  8.3 0.9 constant_dynamic-slice_fusion
  9.2 2.9 %collective-permute-start = (bf16[64,3584]{1,0:T(8,128)(2,1)}, bf16[64,3584]{1,0:T(8,128)(2,1)S(1)}, u32[]{:S(2)}, u32[]{:S(2)}) collective-permute-start(bf16[64,3584]{1,0:T(8,128)(2,1)} %get-tuple-element.11), channel_id=1, source_target_pairs={{0,32},{32,0},{1,33},{33,1},{2,34},{34,2},{3,35},{35,3},{4,36},{36... | collective-permute-start | bytes 1376264 | tf_op jit(solution)/shard_map/ppermute | solution.py:18
  12.1 0.6 bitcast_dynamic-update-slice_fusion.30
  12.7 0.6 bitcast_dynamic-update-slice_fusion.28
  13.3 0.6 bitcast_dynamic-update-slice_fusion.26
  14.0 0.6 bitcast_dynamic-update-slice_fusion.24
  14.6 0.6 bitcast_dynamic-update-slice_fusion.31
  17.1 7.9 %all-to-all-start = ((bf16[8,56,512]{2,1,0:T(8,128)(2,1)}), bf16[8,56,512]{2,1,0:T(8,128)(2,1)S(1)}, u32[]{:S(2)}, u32[]{:S(2)}) async-start(bf16[8,56,512]{2,1,0:T(8,128)(2,1)} %bitcast_dynamic-update-slice_fusion.25), calls=%async_computation | async-start | bytes 917504 | tf_op jit(solution)/shard_map/all_to_all | solution.py:117
  27.5 0.8 dynamic_slice.24
  28.3 1.5 %collective-permute-start.2 = (bf16[64,3584]{1,0:T(8,128)(2,1)S(1)}, bf16[64,3584]{1,0:T(8,128)(2,1)S(1)}, u32[]{:S(2)}, u32[]{:S(2)}) collective-permute-start(bf16[64,3584]{1,0:T(8,128)(2,1)S(1)} %collective-permute-done), channel_id=1, source_target_pairs={{0,64},{64,128},{128,192},{192,0},{1,65},{65,129},{129,193},{193,1... | collective-permute-start | bytes 1376264 | tf_op jit(solution)/shard_map/ppermute | solution.py:18
  29.8 1.3 %collective-permute-start.4 = (bf16[64,3584]{1,0:T(8,128)(2,1)S(1)}, bf16[64,3584]{1,0:T(8,128)(2,1)S(1)}, u32[]{:S(2)}, u32[]{:S(2)}) collective-permute-start(bf16[64,3584]{1,0:T(8,128)(2,1)S(1)} %collective-permute-done), channel_id=1, source_target_pairs={{0,192},{64,0},{128,64},{192,128},{1,193},{65,1},{129,65},{193,129... | collective-permute-start | bytes 1376264 | tf_op jit(solution)/shard_map/ppermute | solution.py:18
  31.2 0.8 bitcast_dynamic-update-slice_fusion.6
  32.0 1.8 %bitcast_dynamic-update-slice_fusion.5 = bf16[8,64,3584]{2,1,0:T(8,128)(2,1)} fusion(bf16[8,64,3584]{2,1,0:T(8,128)(2,1)} %bitcast_dynamic-update-slice_fusion.6, s32[]{:T(128)S(6)} %select_n.76, bf16[64,3584]{1,0:T(8,128)(2,1)} %collective-permute-done.1), kind=kLoop, calls=%fused_computation.11 | loop fusion | bytes 917508 | tf_op jit(solution)/shard_map/dynamic_update_slice | solution.py:137
  33.9 3.2 %all-to-all-done = bf16[8,56,512]{2,1,0:T(8,128)(2,1)S(1)} async-done(((bf16[8,56,512]{2,1,0:T(8,128)(2,1)}), bf16[8,56,512]{2,1,0:T(8,128)(2,1)S(1)}, u32[]{:S(2)}, u32[]{:S(2)}) %all-to-all-start) | async-done | bytes 458784 | tf_op jit(solution)/shard_map/all_to_all | solution.py:117
  37.1 1.3 %collective-permute-start.7 = (bf16[4,56,512]{2,1,0:T(8,128)(2,1)S(1)}, bf16[4,56,512]{2,1,0:T(8,128)(2,1)S(1)}, u32[]{:S(2)}, u32[]{:S(2)}) collective-permute-start(bf16[4,56,512]{2,1,0:T(8,128)(2,1)S(1)} %get-tuple-element.13), channel_id=1, source_target_pairs={{0,1},{1,2},{2,3},{3,0},{4,5},{5,6},{6,7},{7,4},{8,9},{9,10},{10,1... | collective-permute-start | bytes 688136 | tf_op jit(solution)/shard_map/ppermute | solution.py:18
  38.6 5.2 %collective-permute-done.2 = bf16[64,3584]{1,0:T(8,128)(2,1)S(1)} collective-permute-done((bf16[64,3584]{1,0:T(8,128)(2,1)S(1)}, bf16[64,3584]{1,0:T(8,128)(2,1)S(1)}, u32[]{:S(2)}, u32[]{:S(2)}) %collective-permute-start.2) | collective-permute-done | bytes 458784 | tf_op jit(solution)/shard_map/ppermute | solution.py:18
  43.8 2.5 %collective-permute-start.9 = (bf16[4,56,512]{2,1,0:T(8,128)(2,1)S(1)}, bf16[4,56,512]{2,1,0:T(8,128)(2,1)S(1)}, u32[]{:S(2)}, u32[]{:S(2)}) collective-permute-start(bf16[4,56,512]{2,1,0:T(8,128)(2,1)S(1)} %get-tuple-element.13), channel_id=1, source_target_pairs={{0,3},{1,0},{2,1},{3,2},{4,7},{5,4},{6,5},{7,6},{8,11},{9,8},{10,9... | collective-permute-start | bytes 688136 | tf_op jit(solution)/shard_map/ppermute | solution.py:18
  46.3 0.8 bitcast_dynamic-update-slice_fusion.4
  47.1 1.8 %bitcast_dynamic-update-slice_fusion.3 = bf16[8,64,3584]{2,1,0:T(8,128)(2,1)} fusion(bf16[8,64,3584]{2,1,0:T(8,128)(2,1)} %bitcast_dynamic-update-slice_fusion.4, s32[]{:T(128)S(6)} %select_n.78, bf16[64,3584]{1,0:T(8,128)(2,1)} %collective-permute-done.3), kind=kLoop, calls=%fused_computation.9 | loop fusion | bytes 917508 | tf_op jit(solution)/shard_map/dynamic_update_slice | solution.py:137
  49.0 2.7 %collective-permute-start.10 = (bf16[4,56,512]{2,1,0:T(8,128)(2,1)S(1)}, bf16[4,56,512]{2,1,0:T(8,128)(2,1)S(1)}, u32[]{:S(2)}, u32[]{:S(2)}) collective-permute-start(bf16[4,56,512]{2,1,0:T(8,128)(2,1)S(1)} %get-tuple-element.12), channel_id=1, source_target_pairs={{0,3},{1,0},{2,1},{3,2},{4,7},{5,4},{6,5},{7,6},{8,11},{9,8},{10,9... | collective-permute-start | bytes 688136 | tf_op jit(solution)/shard_map/ppermute | solution.py:18
  51.6 0.8 bitcast_dynamic-update-slice_fusion.2
  52.5 1.2 %collective-permute-done.5 = bf16[64,3584]{1,0:T(8,128)(2,1)S(1)} collective-permute-done((bf16[64,3584]{1,0:T(8,128)(2,1)}, bf16[64,3584]{1,0:T(8,128)(2,1)S(1)}, u32[]{:S(2)}, u32[]{:S(2)}) %collective-permute-start.5) | collective-permute-done | bytes 458784 | tf_op jit(solution)/shard_map/ppermute | solution.py:18
  53.6 1.4 %collective-permute-start.13 = (bf16[4,56,512]{2,1,0:T(8,128)(2,1)S(1)}, bf16[4,56,512]{2,1,0:T(8,128)(2,1)S(1)}, u32[]{:S(2)}, u32[]{:S(2)}) collective-permute-start(bf16[4,56,512]{2,1,0:T(8,128)(2,1)S(1)} %get-tuple-element.13), channel_id=1, source_target_pairs={{0,32},{32,0},{1,33},{33,1},{2,34},{34,2},{3,35},{35,3},{4,36},{36... | collective-permute-start | bytes 688136 | tf_op jit(solution)/shard_map/ppermute | solution.py:18
  55.1 0.8 bitcast_dynamic-update-slice_fusion.1
  55.9 1.8 %collective-permute-start.6 = (bf16[64,3584]{1,0:T(8,128)(2,1)S(1)}, bf16[64,3584]{1,0:T(8,128)(2,1)S(1)}, u32[]{:S(2)}, u32[]{:S(2)}) collective-permute-start(bf16[64,3584]{1,0:T(8,128)(2,1)S(1)} %collective-permute-done.4), channel_id=1, source_target_pairs={{0,192},{64,0},{128,64},{192,128},{1,193},{65,1},{129,65},{193,129... | collective-permute-start | bytes 1376264 | tf_op jit(solution)/shard_map/ppermute | solution.py:18
  57.8 0.7 collective-permute-start.11
  58.5 2.1 %collective-permute-start.12 = (bf16[4,56,512]{2,1,0:T(8,128)(2,1)S(1)}, bf16[4,56,512]{2,1,0:T(8,128)(2,1)S(1)}, u32[]{:S(2)}, u32[]{:S(2)}) collective-permute-start(bf16[4,56,512]{2,1,0:T(8,128)(2,1)S(1)} %collective-permute-done.10), channel_id=1, source_target_pairs={{0,3},{1,0},{2,1},{3,2},{4,7},{5,4},{6,5},{7,6},{8,11},{9,8},{10,9... | collective-permute-start | bytes 688136 | tf_op jit(solution)/shard_map/ppermute | solution.py:18
  60.6 1.4 %collective-permute-start.15 = (bf16[4,56,512]{2,1,0:T(8,128)(2,1)S(1)}, bf16[4,56,512]{2,1,0:T(8,128)(2,1)S(1)}, u32[]{:S(2)}, u32[]{:S(2)}) collective-permute-start(bf16[4,56,512]{2,1,0:T(8,128)(2,1)S(1)} %collective-permute-done.7), channel_id=1, source_target_pairs={{0,32},{32,0},{1,33},{33,1},{2,34},{34,2},{3,35},{35,3},{4,36},{36... | collective-permute-start | bytes 688136 | tf_op jit(solution)/shard_map/ppermute | solution.py:18
  62.4 3.1 %collective-permute-done.11 = bf16[4,56,512]{2,1,0:T(8,128)(2,1)S(1)} collective-permute-done((bf16[4,56,512]{2,1,0:T(8,128)(2,1)S(1)}, bf16[4,56,512]{2,1,0:T(8,128)(2,1)S(1)}, u32[]{:S(2)}, u32[]{:S(2)}) %collective-permute-start.11) | collective-permute-done | bytes 229408 | tf_op jit(solution)/shard_map/ppermute | solution.py:18
  65.5 1.7 %collective-permute-start.17 = (bf16[4,56,512]{2,1,0:T(8,128)(2,1)S(1)}, bf16[4,56,512]{2,1,0:T(8,128)(2,1)S(1)}, u32[]{:S(2)}, u32[]{:S(2)}) collective-permute-start(bf16[4,56,512]{2,1,0:T(8,128)(2,1)S(1)} %collective-permute-done.9), channel_id=1, source_target_pairs={{0,32},{32,0},{1,33},{33,1},{2,34},{34,2},{3,35},{35,3},{4,36},{36... | collective-permute-start | bytes 688136 | tf_op jit(solution)/shard_map/ppermute | solution.py:18
  68.8 0.8 bitcast_dynamic-update-slice_fusion.driven_ref
  69.6 6.6 %student.1 = (f32[64,512]{1,0:T(8,128)S(1)}, f32[1,512]{1,0:T(1,128)S(1)}) custom-call(s32[1]{0:T(128)} %bitcast.core_ref, bf16[8,64,3584]{2,1,0:T(8,128)(2,1)} %bitcast_dynamic-update-slice_fusion.driven_ref, bf16[64,3584]{1,0:T(8,128)(2,1)S(1)} %get-tuple-element.10.features_ref, bf16[4,448,512]{2,1,0:T(8,128)(2,1)S(1)} %bitcast.112, ...), custom_call_target="tpu_custom_call" | custom-call | flops 2113929216 | bytes 8388608 | tf_op jit(solution)/shard_map/student/pallas_call | solution.py:156
  76.4 2.7 %collective-permute-start.22 = (f32[64,512]{1,0:T(8,128)S(1)}, f32[64,512]{1,0:T(8,128)S(1)}, u32[]{:S(2)}, u32[]{:S(2)}) collective-permute-start(f32[64,512]{1,0:T(8,128)S(1)} %get-tuple-element.4.refs_0_), channel_id=1, source_target_pairs={{0,192},{64,0},{128,64},{192,128},{1,193},{65,1},{129,65},{193,129... | collective-permute-start | bytes 393224 | tf_op jit(solution)/shard_map/ppermute | solution.py:18
  79.0 0.7 broadcast_in_dim.116
  79.8 9.7 %all-to-all-start.1 = ((f32[64,1,512]{2,1,0:T(1,128)}), f32[64,1,512]{2,1,0:T(1,128)S(1)}, u32[]{:S(2)}, u32[]{:S(2)}) async-start(f32[64,1,512]{2,1,0:T(1,128)} %broadcast_in_dim.116), calls=%async_computation.1 | async-start | bytes 262144 | tf_op jit(solution)/shard_map/all_to_all | solution.py:175
  89.5 1.5 %collective-permute-start.25 = (f32[32,512]{1,0:T(8,128)S(1)}, f32[32,512]{1,0:T(8,128)S(1)}, u32[]{:S(2)}, u32[]{:S(2)}) collective-permute-start(f32[32,512]{1,0:T(8,128)S(1)} %slice.50), channel_id=1, source_target_pairs={{0,64},{64,128},{128,192},{192,0},{1,65},{65,129},{129,193},{193,1... | collective-permute-start | bytes 196616 | tf_op jit(solution)/shard_map/ppermute | solution.py:18
  91.5 0.6 collective-permute-start.21
  92.2 1.5 %collective-permute-start.26 = (f32[32,512]{1,0:T(8,128)S(1)}, f32[32,512]{1,0:T(8,128)S(1)}, u32[]{:S(2)}, u32[]{:S(2)}) collective-permute-start(f32[32,512]{1,0:T(8,128)S(1)} %slice.51), channel_id=1, source_target_pairs={{0,192},{64,0},{128,64},{192,128},{1,193},{65,1},{129,65},{193,129... | collective-permute-start | bytes 196616 | tf_op jit(solution)/shard_map/ppermute | solution.py:18
  94.6 1.5 %collective-permute-done.26 = f32[32,512]{1,0:T(8,128)S(1)} collective-permute-done((f32[32,512]{1,0:T(8,128)S(1)}, f32[32,512]{1,0:T(8,128)S(1)}, u32[]{:S(2)}, u32[]{:S(2)}) %collective-permute-start.26) | collective-permute-done | bytes 65568 | tf_op jit(solution)/shard_map/ppermute | solution.py:18
  96.1 0.8 collective-permute-start.27
  96.9 5.0 %all-to-all-done.1 = f32[64,1,512]{2,1,0:T(1,128)S(1)} async-done(((f32[64,1,512]{2,1,0:T(1,128)}), f32[64,1,512]{2,1,0:T(1,128)S(1)}, u32[]{:S(2)}, u32[]{:S(2)}) %all-to-all-start.1) | async-done | bytes 131104 | tf_op jit(solution)/shard_map/all_to_all | solution.py:175
  103.4 0.6 copy-done.10
  104.1 2.4 %place.1 = f32[128,1792]{1,0:T(8,128)} custom-call(s32[2]{0:T(128)} %pad_add_fusion.at_ref, f32[64,512]{1,0:T(8,128)} %copy-done, f32[64,512]{1,0:T(8,128)} %copy-done.7, f32[64,512]{1,0:T(8,128)} %copy-done.5, f32[64,512]{1,0:T(8,128)} %copy-done.8, f32[64,512]{1,0:T(8,128)} %copy-done.6, f32[64,512]{1,0:T(8,128)} %copy-done.10, f32[64,512]{1,0:T(8,128)} %copy-done.4, ...), custom_call_target="tpu_custom_call" | custom-call | tf_op jit(solution)/shard_map/place/pallas_call | solution.py:185
  (90 shorter events, 8.0 us)
Async XLA Ops:
  0.6 2.2 %copy-start.1 = (bf16[128,3584]{1,0:T(8,128)(2,1)S(1)}, bf16[128,3584]{1,0:T(8,128)(2,1)}, u32[]{:S(2)}) copy-start(bf16[128,3584]{1,0:T(8,128)(2,1)} %param.5) | copy-start | bytes 2752516
  0.7 3.0 %copy-start.2 = (s32[1,128,3584]{2,1,0:T(8,128)S(1)}, s32[1,128,3584]{2,1,0:T(8,128)}, u32[]{:S(2)}) copy-start(s32[1,128,3584]{2,1,0:T(8,128)} %param.6) | copy-start | bytes 5505028
  4.7 7.4 %copy-start.3 = (bf16[56,1792]{1,0:T(8,128)(2,1)S(1)}, bf16[56,1792]{1,0:T(8,128)(2,1)}, u32[]{:S(2)}) copy-start(bf16[56,1792]{1,0:T(8,128)(2,1)} %param.7) | copy-start | bytes 602116
  4.7 26.4 %collective-permute-start.1 = (bf16[64,3584]{1,0:T(8,128)(2,1)}, bf16[64,3584]{1,0:T(8,128)(2,1)}, u32[]{:S(2)}, u32[]{:S(2)}) collective-permute-start(bf16[64,3584]{1,0:T(8,128)(2,1)} %get-tuple-element.9), channel_id=1, source_target_pairs={{0,64},{64,128},{128,192},{192,0},{1,65},{65,129},{129,193},{193,1... | collective-permute-start | bytes 1376264 | tf_op jit(solution)/shard_map/ppermute | solution.py:18
  6.8 40.3 %collective-permute-start.3 = (bf16[64,3584]{1,0:T(8,128)(2,1)}, bf16[64,3584]{1,0:T(8,128)(2,1)}, u32[]{:S(2)}, u32[]{:S(2)}) collective-permute-start(bf16[64,3584]{1,0:T(8,128)(2,1)} %get-tuple-element.9), channel_id=1, source_target_pairs={{0,192},{64,0},{128,64},{192,128},{1,193},{65,1},{129,65},{193,129... | collective-permute-start | bytes 1376264 | tf_op jit(solution)/shard_map/ppermute | solution.py:18
  8.3 16.7 %copy-start.11 = (s32[4]{0:T(128)S(1)}, s32[4]{0:T(128)}, u32[]{:S(2)}) copy-start(s32[4]{0:T(128)} %constant.71.clone) | copy-start | bytes 52
  9.2 19.1 %collective-permute-start = (bf16[64,3584]{1,0:T(8,128)(2,1)}, bf16[64,3584]{1,0:T(8,128)(2,1)S(1)}, u32[]{:S(2)}, u32[]{:S(2)}) collective-permute-start(bf16[64,3584]{1,0:T(8,128)(2,1)} %get-tuple-element.11), channel_id=1, source_target_pairs={{0,32},{32,0},{1,33},{33,1},{2,34},{34,2},{3,35},{35,3},{4,36},{36... | collective-permute-start | bytes 1376264 | tf_op jit(solution)/shard_map/ppermute | solution.py:18
  17.1 20.0 %all-to-all-start = ((bf16[8,56,512]{2,1,0:T(8,128)(2,1)}), bf16[8,56,512]{2,1,0:T(8,128)(2,1)S(1)}, u32[]{:S(2)}, u32[]{:S(2)}) async-start(bf16[8,56,512]{2,1,0:T(8,128)(2,1)} %bitcast_dynamic-update-slice_fusion.25), calls=%async_computation | async-start | bytes 917504 | tf_op jit(solution)/shard_map/all_to_all | solution.py:117
  28.3 15.5 %collective-permute-start.2 = (bf16[64,3584]{1,0:T(8,128)(2,1)S(1)}, bf16[64,3584]{1,0:T(8,128)(2,1)S(1)}, u32[]{:S(2)}, u32[]{:S(2)}) collective-permute-start(bf16[64,3584]{1,0:T(8,128)(2,1)S(1)} %collective-permute-done), channel_id=1, source_target_pairs={{0,64},{64,128},{128,192},{192,0},{1,65},{65,129},{129,193},{193,1... | collective-permute-start | bytes 1376264 | tf_op jit(solution)/shard_map/ppermute | solution.py:18
  29.8 19.2 %collective-permute-start.4 = (bf16[64,3584]{1,0:T(8,128)(2,1)S(1)}, bf16[64,3584]{1,0:T(8,128)(2,1)S(1)}, u32[]{:S(2)}, u32[]{:S(2)}) collective-permute-start(bf16[64,3584]{1,0:T(8,128)(2,1)S(1)} %collective-permute-done), channel_id=1, source_target_pairs={{0,192},{64,0},{128,64},{192,128},{1,193},{65,1},{129,65},{193,129... | collective-permute-start | bytes 1376264 | tf_op jit(solution)/shard_map/ppermute | solution.py:18
  31.1 22.6 %collective-permute-start.5 = (bf16[64,3584]{1,0:T(8,128)(2,1)}, bf16[64,3584]{1,0:T(8,128)(2,1)S(1)}, u32[]{:S(2)}, u32[]{:S(2)}) collective-permute-start(bf16[64,3584]{1,0:T(8,128)(2,1)} %collective-permute-done.1), channel_id=1, source_target_pairs={{0,64},{64,128},{128,192},{192,0},{1,65},{65,129},{129,193},{193,1... | collective-permute-start | bytes 1376264 | tf_op jit(solution)/shard_map/ppermute | solution.py:18
  37.1 18.8 %collective-permute-start.7 = (bf16[4,56,512]{2,1,0:T(8,128)(2,1)S(1)}, bf16[4,56,512]{2,1,0:T(8,128)(2,1)S(1)}, u32[]{:S(2)}, u32[]{:S(2)}) collective-permute-start(bf16[4,56,512]{2,1,0:T(8,128)(2,1)S(1)} %get-tuple-element.13), channel_id=1, source_target_pairs={{0,1},{1,2},{2,3},{3,0},{4,5},{5,6},{6,7},{7,4},{8,9},{9,10},{10,1... | collective-permute-start | bytes 688136 | tf_op jit(solution)/shard_map/ppermute | solution.py:18
  43.8 14.0 %collective-permute-start.9 = (bf16[4,56,512]{2,1,0:T(8,128)(2,1)S(1)}, bf16[4,56,512]{2,1,0:T(8,128)(2,1)S(1)}, u32[]{:S(2)}, u32[]{:S(2)}) collective-permute-start(bf16[4,56,512]{2,1,0:T(8,128)(2,1)S(1)} %get-tuple-element.13), channel_id=1, source_target_pairs={{0,3},{1,0},{2,1},{3,2},{4,7},{5,4},{6,5},{7,6},{8,11},{9,8},{10,9... | collective-permute-start | bytes 688136 | tf_op jit(solution)/shard_map/ppermute | solution.py:18
  47.1 8.8 %collective-permute-start.8 = (bf16[4,56,512]{2,1,0:T(8,128)(2,1)S(1)}, bf16[4,56,512]{2,1,0:T(8,128)(2,1)S(1)}, u32[]{:S(2)}, u32[]{:S(2)}) collective-permute-start(bf16[4,56,512]{2,1,0:T(8,128)(2,1)S(1)} %get-tuple-element.12), channel_id=1, source_target_pairs={{0,1},{1,2},{2,3},{3,0},{4,5},{5,6},{6,7},{7,4},{8,9},{9,10},{10,1... | collective-permute-start | bytes 688136 | tf_op jit(solution)/shard_map/ppermute | solution.py:18
  49.0 9.5 %collective-permute-start.10 = (bf16[4,56,512]{2,1,0:T(8,128)(2,1)S(1)}, bf16[4,56,512]{2,1,0:T(8,128)(2,1)S(1)}, u32[]{:S(2)}, u32[]{:S(2)}) collective-permute-start(bf16[4,56,512]{2,1,0:T(8,128)(2,1)S(1)} %get-tuple-element.12), channel_id=1, source_target_pairs={{0,3},{1,0},{2,1},{3,2},{4,7},{5,4},{6,5},{7,6},{8,11},{9,8},{10,9... | collective-permute-start | bytes 688136 | tf_op jit(solution)/shard_map/ppermute | solution.py:18
  53.6 7.0 %collective-permute-start.13 = (bf16[4,56,512]{2,1,0:T(8,128)(2,1)S(1)}, bf16[4,56,512]{2,1,0:T(8,128)(2,1)S(1)}, u32[]{:S(2)}, u32[]{:S(2)}) collective-permute-start(bf16[4,56,512]{2,1,0:T(8,128)(2,1)S(1)} %get-tuple-element.13), channel_id=1, source_target_pairs={{0,32},{32,0},{1,33},{33,1},{2,34},{34,2},{3,35},{35,3},{4,36},{36... | collective-permute-start | bytes 688136 | tf_op jit(solution)/shard_map/ppermute | solution.py:18
  55.9 6.4 %collective-permute-start.14 = (bf16[4,56,512]{2,1,0:T(8,128)(2,1)S(1)}, bf16[4,56,512]{2,1,0:T(8,128)(2,1)S(1)}, u32[]{:S(2)}, u32[]{:S(2)}) collective-permute-start(bf16[4,56,512]{2,1,0:T(8,128)(2,1)S(1)} %get-tuple-element.12), channel_id=1, source_target_pairs={{0,32},{32,0},{1,33},{33,1},{2,34},{34,2},{3,35},{35,3},{4,36},{36... | collective-permute-start | bytes 688136 | tf_op jit(solution)/shard_map/ppermute | solution.py:18
  55.9 12.8 %collective-permute-start.6 = (bf16[64,3584]{1,0:T(8,128)(2,1)S(1)}, bf16[64,3584]{1,0:T(8,128)(2,1)S(1)}, u32[]{:S(2)}, u32[]{:S(2)}) collective-permute-start(bf16[64,3584]{1,0:T(8,128)(2,1)S(1)} %collective-permute-done.4), channel_id=1, source_target_pairs={{0,192},{64,0},{128,64},{192,128},{1,193},{65,1},{129,65},{193,129... | collective-permute-start | bytes 1376264 | tf_op jit(solution)/shard_map/ppermute | solution.py:18
  57.8 7.7 %collective-permute-start.11 = (bf16[4,56,512]{2,1,0:T(8,128)(2,1)S(1)}, bf16[4,56,512]{2,1,0:T(8,128)(2,1)S(1)}, u32[]{:S(2)}, u32[]{:S(2)}) collective-permute-start(bf16[4,56,512]{2,1,0:T(8,128)(2,1)S(1)} %collective-permute-done.7), channel_id=1, source_target_pairs={{0,1},{1,2},{2,3},{3,0},{4,5},{5,6},{6,7},{7,4},{8,9},{9,10},{10,1... | collective-permute-start | bytes 688136 | tf_op jit(solution)/shard_map/ppermute | solution.py:18
  58.5 8.7 %collective-permute-start.12 = (bf16[4,56,512]{2,1,0:T(8,128)(2,1)S(1)}, bf16[4,56,512]{2,1,0:T(8,128)(2,1)S(1)}, u32[]{:S(2)}, u32[]{:S(2)}) collective-permute-start(bf16[4,56,512]{2,1,0:T(8,128)(2,1)S(1)} %collective-permute-done.10), channel_id=1, source_target_pairs={{0,3},{1,0},{2,1},{3,2},{4,7},{5,4},{6,5},{7,6},{8,11},{9,8},{10,9... | collective-permute-start | bytes 688136 | tf_op jit(solution)/shard_map/ppermute | solution.py:18
  60.6 6.7 %collective-permute-start.15 = (bf16[4,56,512]{2,1,0:T(8,128)(2,1)S(1)}, bf16[4,56,512]{2,1,0:T(8,128)(2,1)S(1)}, u32[]{:S(2)}, u32[]{:S(2)}) collective-permute-start(bf16[4,56,512]{2,1,0:T(8,128)(2,1)S(1)} %collective-permute-done.7), channel_id=1, source_target_pairs={{0,32},{32,0},{1,33},{33,1},{2,34},{34,2},{3,35},{35,3},{4,36},{36... | collective-permute-start | bytes 688136 | tf_op jit(solution)/shard_map/ppermute | solution.py:18
  62.3 5.6 %collective-permute-start.16 = (bf16[4,56,512]{2,1,0:T(8,128)(2,1)S(1)}, bf16[4,56,512]{2,1,0:T(8,128)(2,1)S(1)}, u32[]{:S(2)}, u32[]{:S(2)}) collective-permute-start(bf16[4,56,512]{2,1,0:T(8,128)(2,1)S(1)} %collective-permute-done.8), channel_id=1, source_target_pairs={{0,32},{32,0},{1,33},{33,1},{2,34},{34,2},{3,35},{35,3},{4,36},{36... | collective-permute-start | bytes 688136 | tf_op jit(solution)/shard_map/ppermute | solution.py:18
  65.5 2.8 %collective-permute-start.17 = (bf16[4,56,512]{2,1,0:T(8,128)(2,1)S(1)}, bf16[4,56,512]{2,1,0:T(8,128)(2,1)S(1)}, u32[]{:S(2)}, u32[]{:S(2)}) collective-permute-start(bf16[4,56,512]{2,1,0:T(8,128)(2,1)S(1)} %collective-permute-done.9), channel_id=1, source_target_pairs={{0,32},{32,0},{1,33},{33,1},{2,34},{34,2},{3,35},{35,3},{4,36},{36... | collective-permute-start | bytes 688136 | tf_op jit(solution)/shard_map/ppermute | solution.py:18
  67.2 1.6 %collective-permute-start.18 = (bf16[4,56,512]{2,1,0:T(8,128)(2,1)S(1)}, bf16[4,56,512]{2,1,0:T(8,128)(2,1)S(1)}, u32[]{:S(2)}, u32[]{:S(2)}) collective-permute-start(bf16[4,56,512]{2,1,0:T(8,128)(2,1)S(1)} %collective-permute-done.10), channel_id=1, source_target_pairs={{0,32},{32,0},{1,33},{33,1},{2,34},{34,2},{3,35},{35,3},{4,36},{36... | collective-permute-start | bytes 688136 | tf_op jit(solution)/shard_map/ppermute | solution.py:18
  67.3 2.3 %collective-permute-start.19 = (bf16[4,56,512]{2,1,0:T(8,128)(2,1)S(1)}, bf16[4,56,512]{2,1,0:T(8,128)(2,1)S(1)}, u32[]{:S(2)}, u32[]{:S(2)}) collective-permute-start(bf16[4,56,512]{2,1,0:T(8,128)(2,1)S(1)} %collective-permute-done.11), channel_id=1, source_target_pairs={{0,32},{32,0},{1,33},{33,1},{2,34},{34,2},{3,35},{35,3},{4,36},{36... | collective-permute-start | bytes 688136 | tf_op jit(solution)/shard_map/ppermute | solution.py:18
  67.9 1.7 %collective-permute-start.20 = (bf16[4,56,512]{2,1,0:T(8,128)(2,1)S(1)}, bf16[4,56,512]{2,1,0:T(8,128)(2,1)S(1)}, u32[]{:S(2)}, u32[]{:S(2)}) collective-permute-start(bf16[4,56,512]{2,1,0:T(8,128)(2,1)S(1)} %collective-permute-done.12), channel_id=1, source_target_pairs={{0,32},{32,0},{1,33},{33,1},{2,34},{34,2},{3,35},{35,3},{4,36},{36... | collective-permute-start | bytes 688136 | tf_op jit(solution)/shard_map/ppermute | solution.py:18
  76.3 26.4 %copy-start = (f32[64,512]{1,0:T(8,128)}, f32[64,512]{1,0:T(8,128)S(1)}, u32[]{:S(2)}) copy-start(f32[64,512]{1,0:T(8,128)S(1)} %get-tuple-element.4.refs_0_) | copy-start | bytes 393220
  76.3 13.2 %collective-permute-start.24 = (f32[64,512]{1,0:T(8,128)S(1)}, f32[64,512]{1,0:T(8,128)S(1)}, u32[]{:S(2)}, u32[]{:S(2)}) collective-permute-start(f32[64,512]{1,0:T(8,128)S(1)} %get-tuple-element.4.refs_0_), channel_id=1, source_target_pairs={{0,64},{64,128},{128,192},{192,0},{1,65},{65,129},{129,193},{193,1... | collective-permute-start | bytes 393224 | tf_op jit(solution)/shard_map/ppermute | solution.py:18
  76.4 15.8 %collective-permute-start.22 = (f32[64,512]{1,0:T(8,128)S(1)}, f32[64,512]{1,0:T(8,128)S(1)}, u32[]{:S(2)}, u32[]{:S(2)}) collective-permute-start(f32[64,512]{1,0:T(8,128)S(1)} %get-tuple-element.4.refs_0_), channel_id=1, source_target_pairs={{0,192},{64,0},{128,64},{192,128},{1,193},{65,1},{129,65},{193,129... | collective-permute-start | bytes 393224 | tf_op jit(solution)/shard_map/ppermute | solution.py:18
  79.8 22.2 %all-to-all-start.1 = ((f32[64,1,512]{2,1,0:T(1,128)}), f32[64,1,512]{2,1,0:T(1,128)S(1)}, u32[]{:S(2)}, u32[]{:S(2)}) async-start(f32[64,1,512]{2,1,0:T(1,128)} %broadcast_in_dim.116), calls=%async_computation.1 | async-start | bytes 262144 | tf_op jit(solution)/shard_map/all_to_all | solution.py:175
  89.5 13.3 %copy-start.4 = (f32[64,512]{1,0:T(8,128)}, f32[64,512]{1,0:T(8,128)S(1)}, u32[]{:S(2)}) copy-start(f32[64,512]{1,0:T(8,128)S(1)} %collective-permute-done.24.refs_6_) | copy-start | bytes 393220
  89.5 5.1 %collective-permute-start.25 = (f32[32,512]{1,0:T(8,128)S(1)}, f32[32,512]{1,0:T(8,128)S(1)}, u32[]{:S(2)}, u32[]{:S(2)}) collective-permute-start(f32[32,512]{1,0:T(8,128)S(1)} %slice.50), channel_id=1, source_target_pairs={{0,64},{64,128},{128,192},{192,0},{1,65},{65,129},{129,193},{193,1... | collective-permute-start | bytes 196616 | tf_op jit(solution)/shard_map/ppermute | solution.py:18
  91.5 11.1 %collective-permute-start.21 = (f32[64,512]{1,0:T(8,128)S(1)}, f32[64,512]{1,0:T(8,128)S(1)}, u32[]{:S(2)}, u32[]{:S(2)}) collective-permute-start(f32[64,512]{1,0:T(8,128)S(1)} %get-tuple-element.4.refs_0_), channel_id=1, source_target_pairs={{0,32},{32,0},{1,33},{33,1},{2,34},{34,2},{3,35},{35,3},{4,36},{36... | collective-permute-start | bytes 393224 | tf_op jit(solution)/shard_map/ppermute | solution.py:18
  92.2 10.6 %copy-start.5 = (f32[64,512]{1,0:T(8,128)}, f32[64,512]{1,0:T(8,128)S(1)}, u32[]{:S(2)}) copy-start(f32[64,512]{1,0:T(8,128)S(1)} %collective-permute-done.22.refs_2_) | copy-start | bytes 393220
  92.2 3.9 %collective-permute-start.26 = (f32[32,512]{1,0:T(8,128)S(1)}, f32[32,512]{1,0:T(8,128)S(1)}, u32[]{:S(2)}, u32[]{:S(2)}) collective-permute-start(f32[32,512]{1,0:T(8,128)S(1)} %slice.51), channel_id=1, source_target_pairs={{0,192},{64,0},{128,64},{192,128},{1,193},{65,1},{129,65},{193,129... | collective-permute-start | bytes 196616 | tf_op jit(solution)/shard_map/ppermute | solution.py:18
  93.6 9.0 %collective-permute-start.23 = (f32[64,512]{1,0:T(8,128)S(1)}, f32[64,512]{1,0:T(8,128)S(1)}, u32[]{:S(2)}, u32[]{:S(2)}) collective-permute-start(f32[64,512]{1,0:T(8,128)S(1)} %collective-permute-done.22.refs_2_), channel_id=1, source_target_pairs={{0,32},{32,0},{1,33},{33,1},{2,34},{34,2},{3,35},{35,3},{4,36},{36... | collective-permute-start | bytes 393224 | tf_op jit(solution)/shard_map/ppermute | solution.py:18
  93.9 8.8 %collective-permute-start.28 = (f32[64,512]{1,0:T(8,128)S(1)}, f32[64,512]{1,0:T(8,128)S(1)}, u32[]{:S(2)}, u32[]{:S(2)}) collective-permute-start(f32[64,512]{1,0:T(8,128)S(1)} %collective-permute-done.24.refs_6_), channel_id=1, source_target_pairs={{0,32},{32,0},{1,33},{33,1},{2,34},{34,2},{3,35},{35,3},{4,36},{36... | collective-permute-start | bytes 393224 | tf_op jit(solution)/shard_map/ppermute | solution.py:18
  96.1 6.6 %copy-start.6 = (f32[64,512]{1,0:T(8,128)}, f32[64,512]{1,0:T(8,128)S(1)}, u32[]{:S(2)}) copy-start(f32[64,512]{1,0:T(8,128)S(1)} %constant_dynamic-update-slice_fusion.refs_4_) | copy-start | bytes 393220
  96.1 6.6 %collective-permute-start.27 = (f32[64,512]{1,0:T(8,128)S(1)}, f32[64,512]{1,0:T(8,128)S(1)}, u32[]{:S(2)}, u32[]{:S(2)}) collective-permute-start(f32[64,512]{1,0:T(8,128)S(1)} %constant_dynamic-update-slice_fusion.refs_4_), channel_id=1, source_target_pairs={{0,32},{32,0},{1,33},{33,1},{2,34},{34,2},{3,35},{35,3},{4,36},{36... | collective-permute-start | bytes 393224 | tf_op jit(solution)/shard_map/ppermute | solution.py:18
  102.7 0.7 copy-start.7
  102.7 0.7 copy-start.8
  102.7 0.7 copy-start.9
  103.4 0.6 copy-start.10

commit v2 on v1

v2 whole, which is shorter than its diff:
```python
import functools
import jax
import jax.numpy as jnp
from jax import lax
from jax.experimental import pallas as pl
from jax.experimental.pallas import tpu as pltpu
from jax.sharding import Mesh, PartitionSpec as P

SHARP = 2.0
STARTS = (0, 384, 896, 1280)
WIDE = 512
Y, CORE, Z, X = 4, 2, 2, 4
STEPS = Y * CORE
MIB = 1024 * 1024


def around(x, axis, by):
    n = lax.axis_size(axis)
    return lax.ppermute(x, axis, [(i, (i + by) % n) for i in range(n)])


def across(x, by):
    pairs = [(y * CORE + c, (y + by) % Y * CORE + 1 - c) for y in range(Y) for c in range(CORE)]
    return lax.ppermute(x, ("y", "core"), pairs)


def start_of(y):
    return pl.multiple_of(jnp.where(y < 2, 0, 896) + jnp.where(y % 2 == 1, 384, 0), 128)


def prepare_kernel(mask_ref, features_ref, weight_ref, keep_ref, give_ref, payload_ref):
    half = keep_ref.shape[0]
    core = lax.axis_index("core")
    for out_ref, which in ((keep_ref, core), (give_ref, 1 - core)):
        at = pl.ds(pl.multiple_of(which * half, half), half)
        kept = jnp.where(mask_ref[0, at, :] > 0, features_ref[at, :].astype(jnp.float32), 0.0)
        out_ref[...] = kept.astype(out_ref.dtype)
    for y, s in enumerate(STARTS):
        for z in range(Z):
            payload_ref[y * Z + z] = weight_ref[:, s : s + WIDE]


def student_kernel(*refs, tokens_all):
    pieces, (features_ref, weight_ref, threshold_ref, rates_ref, grad_ref, current_ref) = refs[:STEPS], refs[STEPS:]
    half = pieces[0].shape[0]
    core, y = lax.axis_index("core"), lax.axis_index("y")
    own = pl.ds(pl.multiple_of(core * half, half), half)
    left = jnp.concatenate([p[...] for p in pieces] + [features_ref[own, :]], axis=0)
    steps = [(y + dy) % Y * CORE + (core + dc) % CORE for dy, dc in ((0, 0), (0, 1), (3, 0), (3, 1), (1, 0), (1, 1), (2, 0), (2, 1))]
    for n in range(0, WIDE, 256):
        total = jnp.dot(left, weight_ref[:, n : n + 256], preferred_element_type=jnp.float32)
        for j, step in enumerate(steps + [STEPS]):
            current_ref[step, :, n : n + 256] = total[j * half : (j + 1) * half]
    threshold = threshold_ref[:, pl.ds(start_of(y), WIDE)]
    tall = 32

    def strip(i, grad_sum):
        at = pl.ds(pl.multiple_of(i * tall, tall), tall)
        potential = jnp.zeros((tall, WIDE), jnp.float32)
        total = jnp.zeros((tall, WIDE), jnp.float32)
        for t in range(STEPS):
            rising = potential + 2.0 * current_ref[t, at, :]
            fired = jax.nn.sigmoid(SHARP * (rising - threshold))
            potential = rising - threshold * fired
            current_ref[t, at, :] = fired
            total = total + fired
        rates = threshold * total / STEPS
        rates_ref[at, :] = rates
        v = current_ref[STEPS, at, :]
        error = (rates - v * jax.nn.sigmoid(v)) / tokens_all
        cotangent = jnp.zeros((tall, WIDE), jnp.float32)
        for t in reversed(range(STEPS)):
            fired = current_ref[t, at, :]
            dspike = error * threshold / STEPS - threshold * cotangent
            dwide = dspike * SHARP * fired * (1.0 - fired)
            grad_sum = grad_sum + (-dwide - fired * cotangent + error * fired / STEPS)
            cotangent = cotangent + dwide
        return grad_sum

    grad_sum = lax.fori_loop(0, half // tall, strip, jnp.zeros((tall, WIDE), jnp.float32))
    grad_ref[...] = jnp.broadcast_to(jnp.sum(grad_sum, axis=0, keepdims=True)[None], grad_ref.shape)


def place_kernel(*refs):
    out_ref = refs[-1]
    half = out_ref.shape[0] // 2
    core, y = lax.axis_index("core"), lax.axis_index("y")
    for j in range(Y):
        source = (y + j) % Y
        start = start_of(source)
        for k in range(CORE):
            row = pl.multiple_of(((core + k) % CORE) * half, half)
            piece = refs[CORE * j + k]

            @pl.when(source % 2 == 0)
            def _():
                out_ref[pl.ds(row, half), pl.ds(start, WIDE)] = piece[...]

            @pl.when(source % 2 == 1)
            def _():
                out_ref[pl.ds(row, half), pl.ds(pl.multiple_of(start + 128, 128), WIDE - 128)] = piece[:, 128:]


def add_kernel(grads_ref, out_ref):
    count = grads_ref.shape[0] // Y
    for y, s in enumerate(STARTS):
        total = jnp.sum(grads_ref[y * count : (y + 1) * count], axis=0)
        skip = 128 * (y % 2)
        out_ref[s + skip : s + WIDE] = total[0, skip:]


def on_device(features, spike_mask, gate_weight, threshold):
    core, x = lax.axis_index("core"), lax.axis_index("x")
    rows, deep = features.shape
    tokens_all = rows * Z * X
    half = rows // CORE
    part, width = gate_weight.shape
    vmem = pl.BlockSpec(memory_space=pltpu.VMEM)

    keep, give, payload = pl.pallas_call(
        prepare_kernel,
        out_shape=(
            jax.ShapeDtypeStruct((half, deep), features.dtype),
            jax.ShapeDtypeStruct((half, deep), features.dtype),
            jax.ShapeDtypeStruct((Y * Z, part, WIDE), gate_weight.dtype),
        ),
        in_specs=[vmem] * 3,
        out_specs=(vmem,) * 3,
        compiler_params=pltpu.CompilerParams(vmem_limit_bytes=8 * MIB),
        name="prepare",
    )(spike_mask, features, gate_weight)

    together = lax.optimization_barrier
    keep_p, keep_m = around(keep, "y", 1), around(keep, "y", -1)
    got = across(give, 0)
    landed = lax.all_to_all(payload, ("y", "z"), 0, 0, tiled=True).reshape(Y, Z, part, WIDE)
    keep_p, keep_m, got, give, landed = together((keep_p, keep_m, got, give, landed))

    got_p, got_m = across(give, 1), across(give, -1)
    w_p, w_m = around(landed, "x", 1), around(landed, "x", -1)
    landed_o = around(landed, "core", 1)
    keep_p, got_p, got_m, w_p, w_m, landed_o = together((keep_p, got_p, got_m, w_p, w_m, landed_o))

    keep_f = around(keep_p, "y", 1)
    got_f = around(got_m, "y", -1)
    w_f0, w_f1 = around(w_p[: Y // 2], "x", 1), around(w_m[Y // 2 :], "x", -1)
    weight = jnp.zeros((Y, CORE, Z, X, part, WIDE), gate_weight.dtype)
    for piece, other, at_y, dx in (
        (landed, landed_o, 0, 0),
        (w_p, around(w_p, "core", 1), 0, 3),
        (w_m, around(w_m, "core", 1), 0, 1),
        (w_f0, around(w_f0, "core", 1), 0, 2),
        (w_f1, around(w_f1, "core", 1), Y // 2, 2),
    ):
        at_x = lax.rem(x + dx, X)
        for v, at_core in ((piece, core), (other, 1 - core)):
            weight = lax.dynamic_update_slice(weight, v[:, None, :, None], (at_y, at_core, 0, at_x, 0, 0))
    weight = weight.reshape(deep, WIDE)

    peers = Y * CORE * Z * X
    rates, grad = pl.pallas_call(
        functools.partial(student_kernel, tokens_all=tokens_all),
        out_shape=(
            jax.ShapeDtypeStruct((half, WIDE), jnp.float32),
            jax.ShapeDtypeStruct((peers, 1, WIDE), jnp.float32),
        ),
        in_specs=[vmem] * (STEPS + 3),
        out_specs=(vmem, vmem),
        scratch_shapes=[pltpu.VMEM((STEPS + 1, half, WIDE), jnp.float32)],
        compiler_params=pltpu.CompilerParams(vmem_limit_bytes=16 * MIB),
        cost_estimate=pl.CostEstimate(
            flops=2 * 9 * half * deep * WIDE, bytes_accessed=8 * MIB, transcendentals=18 * half * WIDE
        ),
        name="student",
    )(keep, got, keep_p, got_p, keep_m, got_m, keep_f, got_f, features, weight, threshold[None])

    grads = lax.all_to_all(grad, ("y", "core", "z", "x"), 0, 0, tiled=True)

    pieces = []
    for piece in (rates, around(rates, "y", -1), around(rates, "y", 2), around(rates, "y", 1)):
        pieces += [piece, around(piece, "core", 1)]
    rates_out = pl.pallas_call(
        place_kernel,
        out_shape=jax.ShapeDtypeStruct((rows, width), jnp.float32),
        in_specs=[vmem] * 8,
        out_specs=vmem,
        compiler_params=pltpu.CompilerParams(vmem_limit_bytes=4 * MIB),
        name="place",
    )(*pieces)
    rates_out, grads = lax.optimization_barrier((rates_out, grads))

    grad_out = pl.pallas_call(
        add_kernel,
        out_shape=jax.ShapeDtypeStruct((width,), jnp.float32),
        in_specs=[vmem],
        out_specs=vmem,
        compiler_params=pltpu.CompilerParams(vmem_limit_bytes=4 * MIB),
        name="add",
    )(grads)
    return rates_out, grad_out


def solution(mesh):
    grid = mesh.devices.reshape(Y, CORE, mesh.shape["mp"], Z, X)
    fine = Mesh(grid, ("y", "core", "mp", "z", "x"))
    tm, tok = ("y", "core"), ("z", "x")
    return jax.shard_map(
        on_device,
        mesh=fine,
        in_specs=(P(tok, None), P(tm, tok, None), P(tm + tok, "mp"), P("mp")),
        out_specs=(P(tok, "mp"), P("mp")),
        check_vma=False,
    )
```

time: 108 us -> 109 us (level)
  waiting for transfers between devices: 20.4 us -> 41.4 us
  local copies, waits for them, and re-layouts: 19.9 us -> 10.3 us
  other arithmetic: 3.14 us -> 0 us
  Pallas kernels: 9.02 us -> 6.71 us
  between operations: 3.01 us -> 0.84 us
  starting transfers between devices: 51 us -> 49.1 us
    ppermute x29 -> x20, waiting for transfers between devices: 12.1 us -> 26.4 us  [around(): return lax.ppermute(x, axis, [(i, (i + by) % n) for i in range(n)])]
    ppermute x29 -> x20, starting transfers between devices: 33.4 us -> 21 us  [around(): return lax.ppermute(x, axis, [(i, (i + by) % n) for i in range(n)])]
    all_to_all x2, starting transfers between devices: 17.6 us -> 23.7 us  [the longest x1 12.1 us: on_device(): grads = lax.all_to_all(grad, ('y', 'core', 'z', 'x'), 0, 0, tiled=True)]
    ppermute x0 -> x3, waiting for transfers between devices: none -> 5.96 us  [across(): return lax.ppermute(x, ('y', 'core'), pairs)]
    ppermute x0 -> x3, starting transfers between devices: none -> 4.47 us  [across(): return lax.ppermute(x, ('y', 'core'), pairs)]
    dynamic_update_slice x23 -> x10, local copies, waits for them, and re-layouts: 8.03 us -> 4.4 us  [on_device(): lax.dynamic_update_slice(weight, v[:, None, :, None], (at_y, at_core, 0,...]
    unnamed x33 -> x10, local copies, waits for them, and re-layouts: 6.61 us -> 3.61 us
    pallas_call x1, Pallas kernels: 6.64 us -> 4.03 us  [on_device(): pl.pallas_call(functools.partial(student_kernel, tokens_all=tokens_all),...]
  transfers between devices with their start and end apart: 31 -> 25, of which waited for: 9 -> 11; matrix products, arithmetic and copies ran while one was open for 17% -> 6% of each run, Pallas kernels for 0% -> 1%
where the time goes in v2:
time: 109 us; the launch traced here: 108 us
  starting transfers between devices  49.1 us (45%)
  waiting for transfers between devices  41.4 us (38%)
  local copies, waits for them, and re-layouts  10.3 us (9%)
  Pallas kernels  6.71 us (6%)
    ppermute x20, waiting for transfers between devices, around(): return lax.ppermute(x, axis, [(i, (i + by) % n) for i in range(n)])  26.4 us
    ppermute x20, starting transfers between devices, around(): return lax.ppermute(x, axis, [(i, (i + by) % n) for i in range(n)])  21 us
    all_to_all x1, starting transfers between devices, on_device(): grads = lax.all_to_all(grad, ('y', 'core', 'z', 'x'), 0, 0, tiled=True)  12.1 us
    all_to_all x1, starting transfers between devices, on_device(): lax.all_to_all(payload, ('y', 'z'), 0, 0, tiled=True)  11.6 us
    all_to_all x1, waiting for transfers between devices, on_device(): grads = lax.all_to_all(grad, ('y', 'core', 'z', 'x'), 0, 0, tiled=True)  9.04 us
    ppermute x3, waiting for transfers between devices, across(): return lax.ppermute(x, ('y', 'core'), pairs)  5.96 us
    ppermute x3, starting transfers between devices, across(): return lax.ppermute(x, ('y', 'core'), pairs)  4.47 us
    dynamic_update_slice x10, local copies, waits for them, and re-layouts, on_device(): lax.dynamic_update_slice(weight, v[:, None, :, None], (at_y, at_core, 0,...  4.4 us
  transfers between devices with their start and end apart: 25, of which 11 were waited for; matrix products, arithmetic and copies ran while one was open for 6% of the time, Pallas kernels for 1%

profile of v2, /device:TPU:1, one launch (start us, length us, event | category | flops | bytes accessed | tf_op | source)
XLA Modules:
  0.0 108.4 jit_solution(13513776505046388049)
XLA Ops:
  0.6 1.2 %copy-done = bf16[128,3584]{1,0:T(8,128)(2,1)S(1)} copy-done((bf16[128,3584]{1,0:T(8,128)(2,1)S(1)}, bf16[128,3584]{1,0:T(8,128)(2,1)}, u32[]{:S(2)}) %copy-start) | copy-done | bytes 917528
  1.8 1.5 %copy-done.2 = s32[1,128,3584]{2,1,0:T(8,128)S(1)} copy-done((s32[1,128,3584]{2,1,0:T(8,128)S(1)}, s32[1,128,3584]{2,1,0:T(8,128)}, u32[]{:S(2)}) %copy-start.2) | copy-done | bytes 1835032
  3.3 0.9 copy-done.3
  4.2 0.9 prepare.1
  5.2 11.6 %all-to-all-start = ((bf16[8,56,512]{2,1,0:T(8,128)(2,1)}), bf16[8,56,512]{2,1,0:T(8,128)(2,1)}, u32[]{:S(2)}, u32[]{:S(2)}) async-start(bf16[8,56,512]{2,1,0:T(8,128)(2,1)} %get-tuple-element.22), calls=%async_computation | async-start | bytes 917504 | tf_op jit(solution)/shard_map/all_to_all | solution.py:136
  16.8 1.5 %collective-permute-start = (bf16[64,3584]{1,0:T(8,128)(2,1)S(1)}, bf16[64,3584]{1,0:T(8,128)(2,1)S(1)}, u32[]{:S(2)}, u32[]{:S(2)}) collective-permute-start(bf16[64,3584]{1,0:T(8,128)(2,1)S(1)} %get-tuple-element.20.refs_0_), channel_id=1, source_target_pairs={{0,64},{64,128},{128,192},{192,0},{1,65},{65,129},{129,193},{193,1... | collective-permute-start | bytes 1376264 | tf_op jit(solution)/shard_map/ppermute | solution.py:19
  18.3 1.2 %collective-permute-start.1 = (bf16[64,3584]{1,0:T(8,128)(2,1)S(1)}, bf16[64,3584]{1,0:T(8,128)(2,1)S(1)}, u32[]{:S(2)}, u32[]{:S(2)}) collective-permute-start(bf16[64,3584]{1,0:T(8,128)(2,1)S(1)} %get-tuple-element.20.refs_0_), channel_id=1, source_target_pairs={{0,192},{64,0},{128,64},{192,128},{1,193},{65,1},{129,65},{193,129... | collective-permute-start | bytes 1376264 | tf_op jit(solution)/shard_map/ppermute | solution.py:19
  19.5 1.5 %collective-permute-start.2 = (bf16[64,3584]{1,0:T(8,128)(2,1)S(1)}, bf16[64,3584]{1,0:T(8,128)(2,1)S(1)}, u32[]{:S(2)}, u32[]{:S(2)}) collective-permute-start(bf16[64,3584]{1,0:T(8,128)(2,1)S(1)} %get-tuple-element.25), channel_id=1, source_target_pairs={{0,32},{32,0},{64,96},{96,64},{128,160},{160,128},{192,224},{224,1... | collective-permute-start | bytes 1376264 | tf_op jit(solution)/shard_map/ppermute | solution.py:24
  21.0 13.6 %collective-permute-done.refs_2_ = bf16[64,3584]{1,0:T(8,128)(2,1)S(1)} collective-permute-done((bf16[64,3584]{1,0:T(8,128)(2,1)S(1)}, bf16[64,3584]{1,0:T(8,128)(2,1)S(1)}, u32[]{:S(2)}, u32[]{:S(2)}) %collective-permute-start) | collective-permute-done | bytes 458784 | tf_op jit(solution)/shard_map/ppermute | solution.py:19
  34.6 1.3 %collective-permute-start.5 = (bf16[4,2,56,512]{3,2,1,0:T(8,128)(2,1)}, bf16[4,2,56,512]{3,2,1,0:T(8,128)(2,1)}, u32[]{:S(2)}, u32[]{:S(2)}) collective-permute-start(bf16[4,2,56,512]{3,2,1,0:T(8,128)(2,1)} %bitcast), channel_id=1, source_target_pairs={{0,1},{1,2},{2,3},{3,0},{4,5},{5,6},{6,7},{7,4},{8,9},{9,10},{10,1... | collective-permute-start | bytes 1376264 | tf_op jit(solution)/shard_map/ppermute | solution.py:19
  35.9 1.5 %collective-permute-start.6 = (bf16[4,2,56,512]{3,2,1,0:T(8,128)(2,1)}, bf16[4,2,56,512]{3,2,1,0:T(8,128)(2,1)}, u32[]{:S(2)}, u32[]{:S(2)}) collective-permute-start(bf16[4,2,56,512]{3,2,1,0:T(8,128)(2,1)} %bitcast), channel_id=1, source_target_pairs={{0,3},{1,0},{2,1},{3,2},{4,7},{5,4},{6,5},{7,6},{8,11},{9,8},{10,9... | collective-permute-start | bytes 1376264 | tf_op jit(solution)/shard_map/ppermute | solution.py:19
  37.4 2.0 %collective-permute-start.7 = (bf16[4,2,56,512]{3,2,1,0:T(8,128)(2,1)}, bf16[4,2,56,512]{3,2,1,0:T(8,128)(2,1)}, u32[]{:S(2)}, u32[]{:S(2)}) collective-permute-start(bf16[4,2,56,512]{3,2,1,0:T(8,128)(2,1)} %bitcast), channel_id=1, source_target_pairs={{0,32},{32,0},{1,33},{33,1},{2,34},{34,2},{3,35},{35,3},{4,36},{36... | collective-permute-start | bytes 1376264 | tf_op jit(solution)/shard_map/ppermute | solution.py:19
  39.4 0.4 collective-permute-start.3
  39.8 2.6 %collective-permute-start.4 = (bf16[64,3584]{1,0:T(8,128)(2,1)S(1)}, bf16[64,3584]{1,0:T(8,128)(2,1)S(1)}, u32[]{:S(2)}, u32[]{:S(2)}) collective-permute-start(bf16[64,3584]{1,0:T(8,128)(2,1)S(1)} %get-tuple-element.25), channel_id=1, source_target_pairs={{0,224},{32,192},{64,32},{96,0},{128,96},{160,64},{192,160},{224,1... | collective-permute-start | bytes 1376264 | tf_op jit(solution)/shard_map/ppermute | solution.py:24
  42.4 0.4 broadcast_in_dim.36
  42.8 1.1 bitcast_dynamic-update-slice_fusion.5
  43.9 2.9 %collective-permute-done.5 = bf16[4,2,56,512]{3,2,1,0:T(8,128)(2,1)} collective-permute-done((bf16[4,2,56,512]{3,2,1,0:T(8,128)(2,1)}, bf16[4,2,56,512]{3,2,1,0:T(8,128)(2,1)}, u32[]{:S(2)}, u32[]{:S(2)}) %collective-permute-start.5) | collective-permute-done | bytes 458784 | tf_op jit(solution)/shard_map/ppermute | solution.py:19
  46.8 6.0 %collective-permute-done.3.refs_3_ = bf16[64,3584]{1,0:T(8,128)(2,1)S(1)} collective-permute-done((bf16[64,3584]{1,0:T(8,128)(2,1)S(1)}, bf16[64,3584]{1,0:T(8,128)(2,1)S(1)}, u32[]{:S(2)}, u32[]{:S(2)}) %collective-permute-start.3) | collective-permute-done | bytes 458784 | tf_op jit(solution)/shard_map/ppermute | solution.py:24
  52.8 0.3 collective-permute-start.10
  53.1 1.0 slice.6
  54.1 0.3 collective-permute-start.11
  54.3 1.0 slice.7
  55.4 2.7 %collective-permute-start.14 = (bf16[2,2,56,512]{3,2,1,0:T(8,128)(2,1)S(1)}, bf16[2,2,56,512]{3,2,1,0:T(8,128)(2,1)S(1)}, u32[]{:S(2)}, u32[]{:S(2)}) collective-permute-start(bf16[2,2,56,512]{3,2,1,0:T(8,128)(2,1)S(1)} %slice.7), channel_id=1, source_target_pairs={{0,3},{1,0},{2,1},{3,2},{4,7},{5,4},{6,5},{7,6},{8,11},{9,8},{10,9... | collective-permute-start | bytes 688136 | tf_op jit(solution)/shard_map/ppermute | solution.py:19
  58.0 0.1 collective-permute-start.8
  58.1 1.1 bitcast_dynamic-update-slice_fusion.4
  59.2 1.1 bitcast_dynamic-update-slice_fusion.3
  60.3 3.2 %collective-permute-done.12 = bf16[2,2,56,512]{3,2,1,0:T(8,128)(2,1)S(1)} collective-permute-done((bf16[2,2,56,512]{3,2,1,0:T(8,128)(2,1)S(1)}, bf16[2,2,56,512]{3,2,1,0:T(8,128)(2,1)S(1)}, u32[]{:S(2)}, u32[]{:S(2)}) %collective-permute-start.12) | collective-permute-done | bytes 229408 | tf_op jit(solution)/shard_map/ppermute | solution.py:19
  63.4 3.1 %collective-permute-start.9 = (bf16[64,3584]{1,0:T(8,128)(2,1)S(1)}, bf16[64,3584]{1,0:T(8,128)(2,1)S(1)}, u32[]{:S(2)}, u32[]{:S(2)}) collective-permute-start(bf16[64,3584]{1,0:T(8,128)(2,1)S(1)} %collective-permute-done.4.refs_5_), channel_id=1, source_target_pairs={{0,192},{64,0},{128,64},{192,128},{1,193},{65,1},{129,65},{193,129... | collective-permute-start | bytes 1376264 | tf_op jit(solution)/shard_map/ppermute | solution.py:19
  66.5 1.5 %collective-permute-start.13 = (bf16[2,2,56,512]{3,2,1,0:T(8,128)(2,1)S(1)}, bf16[2,2,56,512]{3,2,1,0:T(8,128)(2,1)S(1)}, u32[]{:S(2)}, u32[]{:S(2)}) collective-permute-start(bf16[2,2,56,512]{3,2,1,0:T(8,128)(2,1)S(1)} %collective-permute-done.12), channel_id=1, source_target_pairs={{0,32},{32,0},{1,33},{33,1},{2,34},{34,2},{3,35},{35,3},{4,36},{36... | collective-permute-start | bytes 688136 | tf_op jit(solution)/shard_map/ppermute | solution.py:19
  68.0 0.3 collective-permute-start.15
  68.4 1.1 bitcast_dynamic-update-slice_fusion.1
  69.6 1.5 %collective-permute-done.8.refs_6_ = bf16[64,3584]{1,0:T(8,128)(2,1)S(1)} collective-permute-done((bf16[64,3584]{1,0:T(8,128)(2,1)S(1)}, bf16[64,3584]{1,0:T(8,128)(2,1)S(1)}, u32[]{:S(2)}, u32[]{:S(2)}) %collective-permute-start.8) | collective-permute-done | bytes 458784 | tf_op jit(solution)/shard_map/ppermute | solution.py:19
  71.1 4.0 %collective-permute-done.9.refs_7_ = bf16[64,3584]{1,0:T(8,128)(2,1)S(1)} collective-permute-done((bf16[64,3584]{1,0:T(8,128)(2,1)S(1)}, bf16[64,3584]{1,0:T(8,128)(2,1)S(1)}, u32[]{:S(2)}, u32[]{:S(2)}) %collective-permute-start.9) | collective-permute-done | bytes 458784 | tf_op jit(solution)/shard_map/ppermute | solution.py:19
  75.1 4.0 %student.1 = (f32[64,512]{1,0:T(8,128)S(1)}, f32[64,1,512]{2,1,0:T(1,128)}) custom-call(bf16[64,3584]{1,0:T(8,128)(2,1)S(1)} %get-tuple-element.20.refs_0_, bf16[64,3584]{1,0:T(8,128)(2,1)S(1)} %collective-permute-done.2.refs_1_, bf16[64,3584]{1,0:T(8,128)(2,1)S(1)} %collective-permute-done.refs_2_, bf16[64,3584]{1,0:T(8,128)(2,1)S(1)} %collective-permute-done.3.refs_3_, ...), custom_call_target="tpu_custom_call" | custom-call | flops 2113929216 | bytes 8388608 | tf_op jit(solution)/shard_map/student/pallas_call | solution.py:161
  79.1 3.4 %collective-permute-start.17 = (f32[64,512]{1,0:T(8,128)S(1)}, f32[64,512]{1,0:T(8,128)S(1)}, u32[]{:S(2)}, u32[]{:S(2)}) collective-permute-start(f32[64,512]{1,0:T(8,128)S(1)} %get-tuple-element.34.refs_0_), channel_id=1, source_target_pairs={{0,192},{64,0},{128,64},{192,128},{1,193},{65,1},{129,65},{193,129... | collective-permute-start | bytes 393224 | tf_op jit(solution)/shard_map/ppermute | solution.py:19
  82.6 0.6 collective-permute-start.21
  83.1 12.1 %all-to-all-start.1 = ((f32[64,1,512]{2,1,0:T(1,128)}), f32[64,1,512]{2,1,0:T(1,128)S(1)}, u32[]{:S(2)}, u32[]{:S(2)}) async-start(f32[64,1,512]{2,1,0:T(1,128)} %get-tuple-element.35), calls=%async_computation.1 | async-start | bytes 262144 | tf_op jit(solution)/shard_map/all_to_all | solution.py:177
  95.2 0.5 collective-permute-start.16
  95.8 0.1 collective-permute-start.18
  95.9 0.4 collective-permute-start.20
  96.3 0.1 collective-permute-start.22
  96.4 0.4 collective-permute-done.16.refs_1_
  96.7 0.4 collective-permute-done.18.refs_3_
  97.1 0.2 collective-permute-done.20.refs_5_
  97.3 0.3 collective-permute-done.22.refs_7_
  97.6 1.1 place.1
  98.7 9.0 %all-to-all-done.1.grads_ref = f32[64,1,512]{2,1,0:T(1,128)S(1)} async-done(((f32[64,1,512]{2,1,0:T(1,128)}), f32[64,1,512]{2,1,0:T(1,128)S(1)}, u32[]{:S(2)}, u32[]{:S(2)}) %all-to-all-start.1) | async-done | bytes 131104 | tf_op jit(solution)/shard_map/all_to_all | solution.py:177
  107.7 0.7 add.53
  (30 shorter events, 0.3 us)
Async XLA Ops:
  0.6 1.2 %copy-start = (bf16[128,3584]{1,0:T(8,128)(2,1)S(1)}, bf16[128,3584]{1,0:T(8,128)(2,1)}, u32[]{:S(2)}) copy-start(bf16[128,3584]{1,0:T(8,128)(2,1)} %refs_8_.1) | copy-start | bytes 2752516
  1.8 1.5 %copy-start.2 = (s32[1,128,3584]{2,1,0:T(8,128)S(1)}, s32[1,128,3584]{2,1,0:T(8,128)}, u32[]{:S(2)}) copy-start(s32[1,128,3584]{2,1,0:T(8,128)} %mask_ref.1) | copy-start | bytes 5505028
  3.3 0.9 copy-start.3
  4.2 38.1 %copy-start.4 = (f32[1792]{0:T(1024)S(1)}, f32[1792]{0:T(1024)}, u32[]{:S(2)}) copy-start(f32[1792]{0:T(1024)} %param.7) | copy-start | bytes 21508
  5.2 29.5 %all-to-all-start = ((bf16[8,56,512]{2,1,0:T(8,128)(2,1)}), bf16[8,56,512]{2,1,0:T(8,128)(2,1)}, u32[]{:S(2)}, u32[]{:S(2)}) async-start(bf16[8,56,512]{2,1,0:T(8,128)(2,1)} %get-tuple-element.22), calls=%async_computation | async-start | bytes 917504 | tf_op jit(solution)/shard_map/all_to_all | solution.py:136
  16.8 17.8 %collective-permute-start = (bf16[64,3584]{1,0:T(8,128)(2,1)S(1)}, bf16[64,3584]{1,0:T(8,128)(2,1)S(1)}, u32[]{:S(2)}, u32[]{:S(2)}) collective-permute-start(bf16[64,3584]{1,0:T(8,128)(2,1)S(1)} %get-tuple-element.20.refs_0_), channel_id=1, source_target_pairs={{0,64},{64,128},{128,192},{192,0},{1,65},{65,129},{129,193},{193,1... | collective-permute-start | bytes 1376264 | tf_op jit(solution)/shard_map/ppermute | solution.py:19
  18.3 16.3 %collective-permute-start.1 = (bf16[64,3584]{1,0:T(8,128)(2,1)S(1)}, bf16[64,3584]{1,0:T(8,128)(2,1)S(1)}, u32[]{:S(2)}, u32[]{:S(2)}) collective-permute-start(bf16[64,3584]{1,0:T(8,128)(2,1)S(1)} %get-tuple-element.20.refs_0_), channel_id=1, source_target_pairs={{0,192},{64,0},{128,64},{192,128},{1,193},{65,1},{129,65},{193,129... | collective-permute-start | bytes 1376264 | tf_op jit(solution)/shard_map/ppermute | solution.py:19
  19.5 15.1 %collective-permute-start.2 = (bf16[64,3584]{1,0:T(8,128)(2,1)S(1)}, bf16[64,3584]{1,0:T(8,128)(2,1)S(1)}, u32[]{:S(2)}, u32[]{:S(2)}) collective-permute-start(bf16[64,3584]{1,0:T(8,128)(2,1)S(1)} %get-tuple-element.25), channel_id=1, source_target_pairs={{0,32},{32,0},{64,96},{96,64},{128,160},{160,128},{192,224},{224,1... | collective-permute-start | bytes 1376264 | tf_op jit(solution)/shard_map/ppermute | solution.py:24
  34.6 12.2 %collective-permute-start.5 = (bf16[4,2,56,512]{3,2,1,0:T(8,128)(2,1)}, bf16[4,2,56,512]{3,2,1,0:T(8,128)(2,1)}, u32[]{:S(2)}, u32[]{:S(2)}) collective-permute-start(bf16[4,2,56,512]{3,2,1,0:T(8,128)(2,1)} %bitcast), channel_id=1, source_target_pairs={{0,1},{1,2},{2,3},{3,0},{4,5},{5,6},{6,7},{7,4},{8,9},{9,10},{10,1... | collective-permute-start | bytes 1376264 | tf_op jit(solution)/shard_map/ppermute | solution.py:19
  35.9 10.9 %collective-permute-start.6 = (bf16[4,2,56,512]{3,2,1,0:T(8,128)(2,1)}, bf16[4,2,56,512]{3,2,1,0:T(8,128)(2,1)}, u32[]{:S(2)}, u32[]{:S(2)}) collective-permute-start(bf16[4,2,56,512]{3,2,1,0:T(8,128)(2,1)} %bitcast), channel_id=1, source_target_pairs={{0,3},{1,0},{2,1},{3,2},{4,7},{5,4},{6,5},{7,6},{8,11},{9,8},{10,9... | collective-permute-start | bytes 1376264 | tf_op jit(solution)/shard_map/ppermute | solution.py:19
  37.4 9.4 %collective-permute-start.7 = (bf16[4,2,56,512]{3,2,1,0:T(8,128)(2,1)}, bf16[4,2,56,512]{3,2,1,0:T(8,128)(2,1)}, u32[]{:S(2)}, u32[]{:S(2)}) collective-permute-start(bf16[4,2,56,512]{3,2,1,0:T(8,128)(2,1)} %bitcast), channel_id=1, source_target_pairs={{0,32},{32,0},{1,33},{33,1},{2,34},{34,2},{3,35},{35,3},{4,36},{36... | collective-permute-start | bytes 1376264 | tf_op jit(solution)/shard_map/ppermute | solution.py:19
  39.4 13.3 %collective-permute-start.3 = (bf16[64,3584]{1,0:T(8,128)(2,1)S(1)}, bf16[64,3584]{1,0:T(8,128)(2,1)S(1)}, u32[]{:S(2)}, u32[]{:S(2)}) collective-permute-start(bf16[64,3584]{1,0:T(8,128)(2,1)S(1)} %get-tuple-element.25), channel_id=1, source_target_pairs={{0,96},{32,64},{64,160},{96,128},{128,224},{160,192},{192,32},{224... | collective-permute-start | bytes 1376264 | tf_op jit(solution)/shard_map/ppermute | solution.py:24
  39.8 13.0 %collective-permute-start.4 = (bf16[64,3584]{1,0:T(8,128)(2,1)S(1)}, bf16[64,3584]{1,0:T(8,128)(2,1)S(1)}, u32[]{:S(2)}, u32[]{:S(2)}) collective-permute-start(bf16[64,3584]{1,0:T(8,128)(2,1)S(1)} %get-tuple-element.25), channel_id=1, source_target_pairs={{0,224},{32,192},{64,32},{96,0},{128,96},{160,64},{192,160},{224,1... | collective-permute-start | bytes 1376264 | tf_op jit(solution)/shard_map/ppermute | solution.py:24
  43.9 31.3 %copy-start.1 = (bf16[128,3584]{1,0:T(8,128)(2,1)S(1)}, bf16[128,3584]{1,0:T(8,128)(2,1)}, u32[]{:S(2)}) copy-start(bf16[128,3584]{1,0:T(8,128)(2,1)} %refs_8_.1) | copy-start | bytes 2752516
  52.8 15.3 %collective-permute-start.10 = (bf16[4,2,56,512]{3,2,1,0:T(8,128)(2,1)}, bf16[4,2,56,512]{3,2,1,0:T(8,128)(2,1)S(1)}, u32[]{:S(2)}, u32[]{:S(2)}) collective-permute-start(bf16[4,2,56,512]{3,2,1,0:T(8,128)(2,1)} %collective-permute-done.5), channel_id=1, source_target_pairs={{0,32},{32,0},{1,33},{33,1},{2,34},{34,2},{3,35},{35,3},{4,36},{36... | collective-permute-start | bytes 1376264 | tf_op jit(solution)/shard_map/ppermute | solution.py:19
  54.1 15.4 %collective-permute-start.11 = (bf16[4,2,56,512]{3,2,1,0:T(8,128)(2,1)}, bf16[4,2,56,512]{3,2,1,0:T(8,128)(2,1)S(1)}, u32[]{:S(2)}, u32[]{:S(2)}) collective-permute-start(bf16[4,2,56,512]{3,2,1,0:T(8,128)(2,1)} %collective-permute-done.6), channel_id=1, source_target_pairs={{0,32},{32,0},{1,33},{33,1},{2,34},{34,2},{3,35},{35,3},{4,36},{36... | collective-permute-start | bytes 1376264 | tf_op jit(solution)/shard_map/ppermute | solution.py:19
  55.3 8.1 %collective-permute-start.12 = (bf16[2,2,56,512]{3,2,1,0:T(8,128)(2,1)S(1)}, bf16[2,2,56,512]{3,2,1,0:T(8,128)(2,1)S(1)}, u32[]{:S(2)}, u32[]{:S(2)}) collective-permute-start(bf16[2,2,56,512]{3,2,1,0:T(8,128)(2,1)S(1)} %slice.6), channel_id=1, source_target_pairs={{0,1},{1,2},{2,3},{3,0},{4,5},{5,6},{6,7},{7,4},{8,9},{9,10},{10,1... | collective-permute-start | bytes 688136 | tf_op jit(solution)/shard_map/ppermute | solution.py:19
  55.4 11.2 %collective-permute-start.14 = (bf16[2,2,56,512]{3,2,1,0:T(8,128)(2,1)S(1)}, bf16[2,2,56,512]{3,2,1,0:T(8,128)(2,1)S(1)}, u32[]{:S(2)}, u32[]{:S(2)}) collective-permute-start(bf16[2,2,56,512]{3,2,1,0:T(8,128)(2,1)S(1)} %slice.7), channel_id=1, source_target_pairs={{0,3},{1,0},{2,1},{3,2},{4,7},{5,4},{6,5},{7,6},{8,11},{9,8},{10,9... | collective-permute-start | bytes 688136 | tf_op jit(solution)/shard_map/ppermute | solution.py:19
  58.0 13.1 %collective-permute-start.8 = (bf16[64,3584]{1,0:T(8,128)(2,1)S(1)}, bf16[64,3584]{1,0:T(8,128)(2,1)S(1)}, u32[]{:S(2)}, u32[]{:S(2)}) collective-permute-start(bf16[64,3584]{1,0:T(8,128)(2,1)S(1)} %collective-permute-done.refs_2_), channel_id=1, source_target_pairs={{0,64},{64,128},{128,192},{192,0},{1,65},{65,129},{129,193},{193,1... | collective-permute-start | bytes 1376264 | tf_op jit(solution)/shard_map/ppermute | solution.py:19
  63.4 11.7 %collective-permute-start.9 = (bf16[64,3584]{1,0:T(8,128)(2,1)S(1)}, bf16[64,3584]{1,0:T(8,128)(2,1)S(1)}, u32[]{:S(2)}, u32[]{:S(2)}) collective-permute-start(bf16[64,3584]{1,0:T(8,128)(2,1)S(1)} %collective-permute-done.4.refs_5_), channel_id=1, source_target_pairs={{0,192},{64,0},{128,64},{192,128},{1,193},{65,1},{129,65},{193,129... | collective-permute-start | bytes 1376264 | tf_op jit(solution)/shard_map/ppermute | solution.py:19
  66.5 3.0 %collective-permute-start.13 = (bf16[2,2,56,512]{3,2,1,0:T(8,128)(2,1)S(1)}, bf16[2,2,56,512]{3,2,1,0:T(8,128)(2,1)S(1)}, u32[]{:S(2)}, u32[]{:S(2)}) collective-permute-start(bf16[2,2,56,512]{3,2,1,0:T(8,128)(2,1)S(1)} %collective-permute-done.12), channel_id=1, source_target_pairs={{0,32},{32,0},{1,33},{33,1},{2,34},{34,2},{3,35},{35,3},{4,36},{36... | collective-permute-start | bytes 688136 | tf_op jit(solution)/shard_map/ppermute | solution.py:19
  68.0 1.6 %collective-permute-start.15 = (bf16[2,2,56,512]{3,2,1,0:T(8,128)(2,1)S(1)}, bf16[2,2,56,512]{3,2,1,0:T(8,128)(2,1)S(1)}, u32[]{:S(2)}, u32[]{:S(2)}) collective-permute-start(bf16[2,2,56,512]{3,2,1,0:T(8,128)(2,1)S(1)} %collective-permute-done.14), channel_id=1, source_target_pairs={{0,32},{32,0},{1,33},{33,1},{2,34},{34,2},{3,35},{35,3},{4,36},{36... | collective-permute-start | bytes 688136 | tf_op jit(solution)/shard_map/ppermute | solution.py:19
  79.1 16.6 %collective-permute-start.17 = (f32[64,512]{1,0:T(8,128)S(1)}, f32[64,512]{1,0:T(8,128)S(1)}, u32[]{:S(2)}, u32[]{:S(2)}) collective-permute-start(f32[64,512]{1,0:T(8,128)S(1)} %get-tuple-element.34.refs_0_), channel_id=1, source_target_pairs={{0,192},{64,0},{128,64},{192,128},{1,193},{65,1},{129,65},{193,129... | collective-permute-start | bytes 393224 | tf_op jit(solution)/shard_map/ppermute | solution.py:19
  82.6 13.3 %collective-permute-start.19 = (f32[64,512]{1,0:T(8,128)S(1)}, f32[64,512]{1,0:T(8,128)S(1)}, u32[]{:S(2)}, u32[]{:S(2)}) collective-permute-start(f32[64,512]{1,0:T(8,128)S(1)} %get-tuple-element.34.refs_0_), channel_id=1, source_target_pairs={{0,128},{64,192},{128,0},{192,64},{1,129},{65,193},{129,1},{193,65... | collective-permute-start | bytes 393224 | tf_op jit(solution)/shard_map/ppermute | solution.py:19
  82.6 13.7 %collective-permute-start.21 = (f32[64,512]{1,0:T(8,128)S(1)}, f32[64,512]{1,0:T(8,128)S(1)}, u32[]{:S(2)}, u32[]{:S(2)}) collective-permute-start(f32[64,512]{1,0:T(8,128)S(1)} %get-tuple-element.34.refs_0_), channel_id=1, source_target_pairs={{0,64},{64,128},{128,192},{192,0},{1,65},{65,129},{129,193},{193,1... | collective-permute-start | bytes 393224 | tf_op jit(solution)/shard_map/ppermute | solution.py:19
  83.1 24.6 %all-to-all-start.1 = ((f32[64,1,512]{2,1,0:T(1,128)}), f32[64,1,512]{2,1,0:T(1,128)S(1)}, u32[]{:S(2)}, u32[]{:S(2)}) async-start(f32[64,1,512]{2,1,0:T(1,128)} %get-tuple-element.35), calls=%async_computation.1 | async-start | bytes 262144 | tf_op jit(solution)/shard_map/all_to_all | solution.py:177
  95.2 1.5 %collective-permute-start.16 = (f32[64,512]{1,0:T(8,128)S(1)}, f32[64,512]{1,0:T(8,128)S(1)}, u32[]{:S(2)}, u32[]{:S(2)}) collective-permute-start(f32[64,512]{1,0:T(8,128)S(1)} %get-tuple-element.34.refs_0_), channel_id=1, source_target_pairs={{0,32},{32,0},{1,33},{33,1},{2,34},{34,2},{3,35},{35,3},{4,36},{36... | collective-permute-start | bytes 393224 | tf_op jit(solution)/shard_map/ppermute | solution.py:19
  95.8 1.3 %collective-permute-start.18 = (f32[64,512]{1,0:T(8,128)S(1)}, f32[64,512]{1,0:T(8,128)S(1)}, u32[]{:S(2)}, u32[]{:S(2)}) collective-permute-start(f32[64,512]{1,0:T(8,128)S(1)} %collective-permute-done.17.refs_2_), channel_id=1, source_target_pairs={{0,32},{32,0},{1,33},{33,1},{2,34},{34,2},{3,35},{35,3},{4,36},{36... | collective-permute-start | bytes 393224 | tf_op jit(solution)/shard_map/ppermute | solution.py:19
  95.9 1.4 %collective-permute-start.20 = (f32[64,512]{1,0:T(8,128)S(1)}, f32[64,512]{1,0:T(8,128)S(1)}, u32[]{:S(2)}, u32[]{:S(2)}) collective-permute-start(f32[64,512]{1,0:T(8,128)S(1)} %collective-permute-done.19.refs_4_), channel_id=1, source_target_pairs={{0,32},{32,0},{1,33},{33,1},{2,34},{34,2},{3,35},{35,3},{4,36},{36... | collective-permute-start | bytes 393224 | tf_op jit(solution)/shard_map/ppermute | solution.py:19
  96.3 1.3 %collective-permute-start.22 = (f32[64,512]{1,0:T(8,128)S(1)}, f32[64,512]{1,0:T(8,128)S(1)}, u32[]{:S(2)}, u32[]{:S(2)}) collective-permute-start(f32[64,512]{1,0:T(8,128)S(1)} %collective-permute-done.21.refs_6_), channel_id=1, source_target_pairs={{0,32},{32,0},{1,33},{33,1},{2,34},{34,2},{3,35},{35,3},{4,36},{36... | collective-permute-start | bytes 393224 | tf_op jit(solution)/shard_map/ppermute | solution.py:19

commit v3 on v2

v3 whole, which is shorter than its diff:
```python
import functools
import jax
import jax.numpy as jnp
from jax import lax
from jax.experimental import pallas as pl
from jax.experimental.pallas import tpu as pltpu
from jax.sharding import Mesh, PartitionSpec as P

SHARP = 2.0
STARTS = (0, 128, 384, 640, 896, 1024, 1280, 1536)
WIDE = 256
Y, CORE, Z, X = 4, 2, 2, 4
STEPS = Y * CORE
MIB = 1024 * 1024


def around(x, axis, by):
    n = lax.axis_size(axis)
    return lax.ppermute(x, axis, [(i, (i + by) % n) for i in range(n)])


def start_of(y, core):
    w = y * CORE + core
    start = 128 * ((7 * w) // 4)
    return pl.multiple_of(start, 128)


def prepare_kernel(mask_hbm, features_hbm, weight_hbm, driven_ref, payload_ref, mask_ref, features_ref, weight_ref, sems):
    copies = [
        pltpu.make_async_copy(a, b, sems.at[i])
        for i, (a, b) in enumerate(((mask_hbm, mask_ref), (features_hbm, features_ref), (weight_hbm, weight_ref)))
    ]
    for c in copies:
        c.start()
    for c in copies[:2]:
        c.wait()
    kept = jnp.where(mask_ref[0] > 0, features_ref[...].astype(jnp.float32), 0.0)
    driven_ref[...] = kept.astype(driven_ref.dtype)
    copies[2].wait()
    for w, s in enumerate(STARTS):
        for z in range(Z):
            payload_ref[w * Z + z] = weight_ref[:, s : s + WIDE]


def student_kernel(*refs, tokens_all, spans):
    count = len(spans)
    pieces, (features_ref, weight_ref, threshold_ref, rates_ref, grad_ref, current_ref) = refs[:count], refs[count:]
    rows = features_ref.shape[0]
    core, y = lax.axis_index("core"), lax.axis_index("y")
    left = jnp.concatenate([p[...] for p in pieces] + [features_ref[...]], axis=0)
    total = jnp.dot(left, weight_ref[...], preferred_element_type=jnp.float32)
    at = 0
    for dy, dc, first, tall in spans:
        step = (y + dy) % Y * CORE + (core + dc) % CORE
        current_ref[step, first : first + tall, :] = total[at : at + tall]
        at += tall
    current_ref[STEPS] = total[at:]
    threshold = threshold_ref[:, pl.ds(start_of(y, core), WIDE)]
    tall = 64

    def strip(i, grad_sum):
        at = pl.ds(pl.multiple_of(i * tall, tall), tall)
        potential = jnp.zeros((tall, WIDE), jnp.float32)
        total = jnp.zeros((tall, WIDE), jnp.float32)
        for t in range(STEPS):
            rising = potential + 2.0 * current_ref[t, at, :]
            fired = jax.nn.sigmoid(SHARP * (rising - threshold))
            potential = rising - threshold * fired
            current_ref[t, at, :] = fired
            total = total + fired
        rates = threshold * total / STEPS
        rates_ref[at, :] = rates
        v = current_ref[STEPS, at, :]
        error = (rates - v * jax.nn.sigmoid(v)) / tokens_all
        cotangent = jnp.zeros((tall, WIDE), jnp.float32)
        for t in reversed(range(STEPS)):
            fired = current_ref[t, at, :]
            dspike = error * threshold / STEPS - threshold * cotangent
            dwide = dspike * SHARP * fired * (1.0 - fired)
            grad_sum = grad_sum + (-dwide - fired * cotangent + error * fired / STEPS)
            cotangent = cotangent + dwide
        return grad_sum

    grad_sum = lax.fori_loop(0, rows // tall, strip, jnp.zeros((tall, WIDE), jnp.float32))
    grad_ref[...] = jnp.broadcast_to(jnp.sum(grad_sum, axis=0, keepdims=True)[None], grad_ref.shape)


def place_kernel(*refs):
    out_ref = refs[-1]
    core, y = lax.axis_index("core"), lax.axis_index("y")
    for j in range(Y):
        for k in range(CORE):
            from_y, from_core = (y + j) % Y, (core + k) % CORE
            start = start_of(from_y, from_core)
            piece = refs[CORE * j + k]

            @pl.when((from_core == 0) | (from_y % 2 == 1))
            def _():
                out_ref[:, pl.ds(start, WIDE)] = piece[...]

            @pl.when((from_core == 1) & (from_y % 2 == 0))
            def _():
                out_ref[:, pl.ds(pl.multiple_of(start + 128, 128), WIDE - 128)] = piece[:, 128:]


def add_kernel(grads_ref, out_ref):
    count = grads_ref.shape[0] // STEPS
    for w, s in enumerate(STARTS):
        total = jnp.sum(grads_ref[w * count : (w + 1) * count], axis=0)
        skip = 128 if w % 4 == 1 else 0
        out_ref[s + skip : s + WIDE] = total[0, skip:]


def on_device(features, spike_mask, gate_weight, threshold):
    x = lax.axis_index("x")
    rows, deep = features.shape
    tokens_all = rows * Z * X
    half = rows // 2
    part, width = gate_weight.shape
    vmem = pl.BlockSpec(memory_space=pltpu.VMEM)

    own, payload = pl.pallas_call(
        prepare_kernel,
        out_shape=(
            jax.ShapeDtypeStruct((rows, deep), features.dtype),
            jax.ShapeDtypeStruct((STEPS * Z, part, WIDE), gate_weight.dtype),
        ),
        in_specs=[pl.BlockSpec(memory_space=pltpu.HBM)] * 3,
        out_specs=(vmem,) * 2,
        scratch_shapes=[
            pltpu.VMEM(spike_mask.shape, spike_mask.dtype),
            pltpu.VMEM(features.shape, features.dtype),
            pltpu.VMEM(gate_weight.shape, gate_weight.dtype),
            pltpu.SemaphoreType.DMA((3,)),
        ],
        compiler_params=pltpu.CompilerParams(vmem_limit_bytes=8 * MIB),
        name="prepare",
    )(spike_mask, features, gate_weight)

    s_p, s_m = around(own, "y", 1), around(own, "y", -1)
    s_f0, s_f1 = around(s_p[:half], "y", 1), around(s_m[half:], "y", -1)

    landed = lax.all_to_all(payload, ("y", "core", "z"), 0, 0, tiled=True).reshape(STEPS, Z, part, WIDE)
    w_p, w_m = around(landed, "x", 1), around(landed, "x", -1)
    cut = STEPS // 2
    w_f0, w_f1 = around(w_p[:cut], "x", 1), around(w_m[cut:], "x", -1)
    s_q, s_n, w_f0, w_f1 = lax.optimization_barrier((s_p, s_m, w_f0, w_f1))
    o_own, o_p, o_m = (around(v, "core", 1) for v in (own, s_q, s_n))
    o_f0, o_f1 = around(s_f0, "core", 1), around(s_f1, "core", 1)
    steps, spans = [], []
    for mine, other, dy, first, tall in (
        (own, o_own, 0, 0, rows), (s_p, o_p, 3, 0, rows), (s_m, o_m, 1, 0, rows), (s_f0, o_f0, 2, 0, half), (s_f1, o_f1, 2, half, half),
    ):
        steps += [mine, other]
        spans += [(dy, 0, first, tall), (dy, 1, first, tall)]

    weight = jnp.zeros((STEPS, Z, X, part, WIDE), gate_weight.dtype)
    for piece, at, dx in ((landed, 0, 0), (w_p, 0, 3), (w_m, 0, 1), (w_f0, 0, 2), (w_f1, cut, 2)):
        weight = lax.dynamic_update_slice(weight, piece[:, :, None], (at, 0, lax.rem(x + dx, X), 0, 0))
    weight = weight.reshape(deep, WIDE)

    peers = Y * CORE * Z * X
    rates, grad = pl.pallas_call(
        functools.partial(student_kernel, tokens_all=tokens_all, spans=spans),
        out_shape=(
            jax.ShapeDtypeStruct((rows, WIDE), jnp.float32),
            jax.ShapeDtypeStruct((peers, 1, WIDE), jnp.float32),
        ),
        in_specs=[vmem] * (len(steps) + 3),
        out_specs=(vmem, vmem),
        scratch_shapes=[pltpu.VMEM((STEPS + 1, rows, WIDE), jnp.float32)],
        compiler_params=pltpu.CompilerParams(vmem_limit_bytes=12 * MIB),
        cost_estimate=pl.CostEstimate(
            flops=2 * 9 * rows * deep * WIDE, bytes_accessed=8 * MIB, transcendentals=18 * rows * WIDE
        ),
        name="student",
    )(*steps, features, weight, threshold[None])

    grads = lax.all_to_all(grad, ("y", "core", "z", "x"), 0, 0, tiled=True)

    pieces = []
    for piece in (rates, around(rates, "y", -1), around(rates, "y", 2), around(rates, "y", 1)):
        pieces += [piece, around(piece, "core", 1)]
    rates_out = pl.pallas_call(
        place_kernel,
        out_shape=jax.ShapeDtypeStruct((rows, width), jnp.float32),
        in_specs=[vmem] * 8,
        out_specs=vmem,
        compiler_params=pltpu.CompilerParams(vmem_limit_bytes=4 * MIB),
        cost_estimate=pl.CostEstimate(flops=0, bytes_accessed=0, transcendentals=0),
        name="place",
    )(*pieces)
    rates_out, grads = lax.optimization_barrier((rates_out, grads))

    grad_out = pl.pallas_call(
        add_kernel,
        out_shape=jax.ShapeDtypeStruct((width,), jnp.float32),
        in_specs=[vmem],
        out_specs=vmem,
        compiler_params=pltpu.CompilerParams(vmem_limit_bytes=4 * MIB),
        cost_estimate=pl.CostEstimate(flops=0, bytes_accessed=64 * MIB, transcendentals=0),
        name="add",
    )(grads)
    return rates_out, grad_out


def solution(mesh):
    grid = mesh.devices.reshape(Y, CORE, mesh.shape["mp"], Z, X)
    fine = Mesh(grid, ("y", "core", "mp", "z", "x"))
    tm, tok = ("y", "core"), ("z", "x")
    return jax.shard_map(
        on_device,
        mesh=fine,
        in_specs=(P(tok, None), P(tm, tok, None), P(tm + tok, "mp"), P("mp")),
        out_specs=(P(tok, "mp"), P("mp")),
        check_vma=False,
    )
```

time: 109 us -> 105 us (0.963)
  starting transfers between devices: 49.1 us -> 40.2 us
  waiting for transfers between devices: 41.4 us -> 46.5 us
  local copies, waits for them, and re-layouts: 10.3 us -> 7.42 us
  Pallas kernels: 6.71 us -> 8.59 us
    all_to_all x1, waiting for transfers between devices: 0.01 us -> 10.6 us  [on_device(): lax.all_to_all(payload, ('y', 'core', 'z'), 0, 0, tiled=True)]
    all_to_all x1, starting transfers between devices: 12.1 us -> 5.8 us  [on_device(): grads = lax.all_to_all(grad, ('y', 'core', 'z', 'x'), 0, 0, tiled=True)]
    ppermute x3 -> x0, waiting for transfers between devices: 5.96 us -> none  [across(): return lax.ppermute(x, ('y', 'core'), pairs)]
    ppermute x3 -> x0, starting transfers between devices: 4.47 us -> none  [across(): return lax.ppermute(x, ('y', 'core'), pairs)]
    dynamic_update_slice x10 -> x5, local copies, waits for them, and re-layouts: 4.4 us -> 2.05 us  [on_device(): lax.dynamic_update_slice(weight, piece[:, :, None], (at, 0, lax.rem(x + d...]
    pallas_call x2, Pallas kernels: 4.97 us -> 6.81 us  [the longest x1 5.17 us: on_device(): pl.pallas_call(functools.partial(student_kernel, tokens_all=tokens_all, s...]
    all_to_all x1, waiting for transfers between devices: 9.04 us -> 10.8 us  [on_device(): grads = lax.all_to_all(grad, ('y', 'core', 'z', 'x'), 0, 0, tiled=True)]
    ppermute x20, waiting for transfers between devices: 26.4 us -> 25.1 us  [around(): return lax.ppermute(x, axis, [(i, (i + by) % n) for i in range(n)])]
  transfers between devices with their start and end apart: 25 -> 22, of which waited for: 11 -> 7; matrix products, arithmetic and copies ran while one was open for 6% -> 4% of each run, Pallas kernels for 1% -> 1%
where the time goes in v3:
time: 105 us; the launch traced here: 104 us
  waiting for transfers between devices  46.5 us (44%)
  starting transfers between devices  40.2 us (38%)
  Pallas kernels  8.59 us (8%)
  local copies, waits for them, and re-layouts  7.42 us (7%)
    ppermute x20, waiting for transfers between devices, around(): return lax.ppermute(x, axis, [(i, (i + by) % n) for i in range(n)])  25.1 us
    ppermute x20, starting transfers between devices, around(): return lax.ppermute(x, axis, [(i, (i + by) % n) for i in range(n)])  21.8 us
    all_to_all x1, starting transfers between devices, on_device(): lax.all_to_all(payload, ('y', 'core', 'z'), 0, 0, tiled=True)  12.6 us
    all_to_all x1, waiting for transfers between devices, on_device(): grads = lax.all_to_all(grad, ('y', 'core', 'z', 'x'), 0, 0, tiled=True)  10.8 us
    all_to_all x1, waiting for transfers between devices, on_device(): lax.all_to_all(payload, ('y', 'core', 'z'), 0, 0, tiled=True)  10.6 us
    all_to_all x1, starting transfers between devices, on_device(): grads = lax.all_to_all(grad, ('y', 'core', 'z', 'x'), 0, 0, tiled=True)  5.8 us
    pallas_call x1, Pallas kernels, on_device(): pl.pallas_call(functools.partial(student_kernel, tokens_all=tokens_all, s...  5.17 us
    unnamed x18, local copies, waits for them, and re-layouts  3.63 us
  transfers between devices with their start and end apart: 22, of which 7 were waited for; matrix products, arithmetic and copies ran while one was open for 4% of the time, Pallas kernels for 1%

profile of v3, /device:TPU:1, one launch (start us, length us, event | category | flops | bytes accessed | tf_op | source)
XLA Modules:
  0.0 103.6 jit_solution(13703456775616337021)
XLA Ops:
  0.6 0.0 copy-start
  0.6 1.2 %copy-done = bf16[128,3584]{1,0:T(8,128)(2,1)S(1)} copy-done((bf16[128,3584]{1,0:T(8,128)(2,1)S(1)}, bf16[128,3584]{1,0:T(8,128)(2,1)}, u32[]{:S(2)}) %copy-start) | copy-done | bytes 917528
  1.8 1.5 %copy-done.2 = s32[1,128,3584]{2,1,0:T(8,128)S(1)} copy-done((s32[1,128,3584]{2,1,0:T(8,128)S(1)}, s32[1,128,3584]{2,1,0:T(8,128)}, u32[]{:S(2)}) %copy-start.2) | copy-done | bytes 1835032
  3.3 0.9 copy-done.3
  4.2 1.6 %prepare.1 = (bf16[128,3584]{1,0:T(8,128)(2,1)S(1)}, bf16[16,56,256]{2,1,0:T(8,128)(2,1)}) custom-call(s32[1,128,3584]{2,1,0:T(8,128)S(1)} %copy-done.2, bf16[128,3584]{1,0:T(8,128)(2,1)S(1)} %copy-done, bf16[56,1792]{1,0:T(8,128)(2,1)S(1)} %copy-done.3), custom_call_target="tpu_custom_call" | custom-call | tf_op jit(solution)/shard_map/prepare/pallas_call | solution.py:122
  5.9 12.6 %all-to-all-start = ((bf16[16,56,256]{2,1,0:T(8,128)(2,1)}), bf16[16,56,256]{2,1,0:T(8,128)(2,1)S(1)}, u32[]{:S(2)}, u32[]{:S(2)}) async-start(bf16[16,56,256]{2,1,0:T(8,128)(2,1)} %get-tuple-element.13), calls=%async_computation | async-start | bytes 917504 | tf_op jit(solution)/shard_map/all_to_all | solution.py:143
  18.5 1.4 %collective-permute-start.1 = (bf16[128,3584]{1,0:T(8,128)(2,1)S(1)}, bf16[128,3584]{1,0:T(8,128)(2,1)S(1)}, u32[]{:S(2)}, u32[]{:S(2)}) collective-permute-start(bf16[128,3584]{1,0:T(8,128)(2,1)S(1)} %get-tuple-element.12.refs_0_), channel_id=1, source_target_pairs={{0,64},{64,128},{128,192},{192,0},{1,65},{65,129},{129,193},{193,1... | collective-permute-start | bytes 2752520 | tf_op jit(solution)/shard_map/ppermute | solution.py:19
  19.9 1.3 %collective-permute-start.2 = (bf16[128,3584]{1,0:T(8,128)(2,1)S(1)}, bf16[128,3584]{1,0:T(8,128)(2,1)S(1)}, u32[]{:S(2)}, u32[]{:S(2)}) collective-permute-start(bf16[128,3584]{1,0:T(8,128)(2,1)S(1)} %get-tuple-element.12.refs_0_), channel_id=1, source_target_pairs={{0,192},{64,0},{128,64},{192,128},{1,193},{65,1},{129,65},{193,129... | collective-permute-start | bytes 2752520 | tf_op jit(solution)/shard_map/ppermute | solution.py:19
  21.2 10.6 %all-to-all-done = bf16[16,56,256]{2,1,0:T(8,128)(2,1)S(1)} async-done(((bf16[16,56,256]{2,1,0:T(8,128)(2,1)}), bf16[16,56,256]{2,1,0:T(8,128)(2,1)S(1)}, u32[]{:S(2)}, u32[]{:S(2)}) %all-to-all-start) | async-done | bytes 458784 | tf_op jit(solution)/shard_map/all_to_all | solution.py:143
  31.8 1.2 %collective-permute-start.3 = (bf16[8,2,56,256]{3,2,1,0:T(8,128)(2,1)S(1)}, bf16[8,2,56,256]{3,2,1,0:T(8,128)(2,1)S(1)}, u32[]{:S(2)}, u32[]{:S(2)}) collective-permute-start(bf16[8,2,56,256]{3,2,1,0:T(8,128)(2,1)S(1)} %bitcast.20), channel_id=1, source_target_pairs={{0,1},{1,2},{2,3},{3,0},{4,5},{5,6},{6,7},{7,4},{8,9},{9,10},{10,1... | collective-permute-start | bytes 1376264 | tf_op jit(solution)/shard_map/ppermute | solution.py:19
  33.0 1.5 %collective-permute-start.5 = (bf16[8,2,56,256]{3,2,1,0:T(8,128)(2,1)S(1)}, bf16[8,2,56,256]{3,2,1,0:T(8,128)(2,1)S(1)}, u32[]{:S(2)}, u32[]{:S(2)}) collective-permute-start(bf16[8,2,56,256]{3,2,1,0:T(8,128)(2,1)S(1)} %bitcast.21), channel_id=1, source_target_pairs={{0,3},{1,0},{2,1},{3,2},{4,7},{5,4},{6,5},{7,6},{8,11},{9,8},{10,9... | collective-permute-start | bytes 1376264 | tf_op jit(solution)/shard_map/ppermute | solution.py:19
  34.5 10.8 %collective-permute-done.3 = bf16[8,2,56,256]{3,2,1,0:T(8,128)(2,1)S(1)} collective-permute-done((bf16[8,2,56,256]{3,2,1,0:T(8,128)(2,1)S(1)}, bf16[8,2,56,256]{3,2,1,0:T(8,128)(2,1)S(1)}, u32[]{:S(2)}, u32[]{:S(2)}) %collective-permute-start.3) | collective-permute-done | bytes 458784 | tf_op jit(solution)/shard_map/ppermute | solution.py:19
  45.2 0.7 slice.16
  46.0 0.0 collective-permute-start.4
  46.0 0.0 collective-permute-done.5
  46.0 0.7 slice.17
  46.7 2.7 %collective-permute-start.6 = (bf16[4,2,56,256]{3,2,1,0:T(8,128)(2,1)}, bf16[4,2,56,256]{3,2,1,0:T(8,128)(2,1)}, u32[]{:S(2)}, u32[]{:S(2)}) collective-permute-start(bf16[4,2,56,256]{3,2,1,0:T(8,128)(2,1)} %slice.17), channel_id=1, source_target_pairs={{0,3},{1,0},{2,1},{3,2},{4,7},{5,4},{6,5},{7,6},{8,11},{9,8},{10,9... | collective-permute-start | bytes 688136 | tf_op jit(solution)/shard_map/ppermute | solution.py:19
  49.4 1.3 %collective-permute-start = (bf16[128,3584]{1,0:T(8,128)(2,1)S(1)}, bf16[128,3584]{1,0:T(8,128)(2,1)}, u32[]{:S(2)}, u32[]{:S(2)}) collective-permute-start(bf16[128,3584]{1,0:T(8,128)(2,1)S(1)} %get-tuple-element.12.refs_0_), channel_id=1, source_target_pairs={{0,32},{32,0},{1,33},{33,1},{2,34},{34,2},{3,35},{35,3},{4,36},{36... | collective-permute-start | bytes 2752520 | tf_op jit(solution)/shard_map/ppermute | solution.py:19
  50.7 0.2 broadcast_in_dim.18
  50.9 0.0 copy-start.5
  51.0 0.0 collective-permute-done.1.refs_2_
  51.0 0.0 copy-start.1
  51.0 1.3 %collective-permute-start.9 = (bf16[64,3584]{1,0:T(8,128)(2,1)S(1)}, bf16[64,3584]{1,0:T(8,128)(2,1)S(1)}, u32[]{:S(2)}, u32[]{:S(2)}) collective-permute-start(bf16[64,3584]{1,0:T(8,128)(2,1)S(1)} %slice.18), channel_id=1, source_target_pairs={{0,64},{64,128},{128,192},{192,0},{1,65},{65,129},{129,193},{193,1... | collective-permute-start | bytes 1376264 | tf_op jit(solution)/shard_map/ppermute | solution.py:19
  52.4 1.6 %collective-permute-start.11 = (bf16[64,3584]{1,0:T(8,128)(2,1)S(1)}, bf16[64,3584]{1,0:T(8,128)(2,1)S(1)}, u32[]{:S(2)}, u32[]{:S(2)}) collective-permute-start(bf16[64,3584]{1,0:T(8,128)(2,1)S(1)} %slice.19), channel_id=1, source_target_pairs={{0,192},{64,0},{128,64},{192,128},{1,193},{65,1},{129,65},{193,129... | collective-permute-start | bytes 1376264 | tf_op jit(solution)/shard_map/ppermute | solution.py:19
  53.9 0.0 collective-permute-done.4
  53.9 1.6 %collective-permute-start.7 = (bf16[128,3584]{1,0:T(8,128)(2,1)S(1)}, bf16[128,3584]{1,0:T(8,128)(2,1)S(1)}, u32[]{:S(2)}, u32[]{:S(2)}) collective-permute-start(bf16[128,3584]{1,0:T(8,128)(2,1)S(1)} %collective-permute-done.1.refs_2_), channel_id=1, source_target_pairs={{0,32},{32,0},{1,33},{33,1},{2,34},{34,2},{3,35},{35,3},{4,36},{36... | collective-permute-start | bytes 2752520 | tf_op jit(solution)/shard_map/ppermute | solution.py:19
  55.5 0.0 collective-permute-start.8
  55.7 8.8 %collective-permute-done.9.refs_6_ = bf16[64,3584]{1,0:T(8,128)(2,1)S(1)} collective-permute-done((bf16[64,3584]{1,0:T(8,128)(2,1)S(1)}, bf16[64,3584]{1,0:T(8,128)(2,1)S(1)}, u32[]{:S(2)}, u32[]{:S(2)}) %collective-permute-start.9) | collective-permute-done | bytes 458784 | tf_op jit(solution)/shard_map/ppermute | solution.py:19
  64.5 0.8 collective-permute-start.10
  65.3 0.0 collective-permute-done.11.refs_8_
  65.3 0.1 collective-permute-start.12
  65.4 1.0 bitcast_dynamic-update-slice_fusion.2
  66.3 1.0 bitcast_dynamic-update-slice_fusion.3
  67.3 0.0 collective-permute-done.10.refs_7_
  67.3 0.1 collective-permute-done.12.refs_9_
  67.4 5.2 %student.1 = (f32[128,256]{1,0:T(8,128)S(1)}, f32[64,1,256]{2,1,0:T(1,128)}) custom-call(bf16[128,3584]{1,0:T(8,128)(2,1)S(1)} %get-tuple-element.12.refs_0_, bf16[128,3584]{1,0:T(8,128)(2,1)} %collective-permute-done.refs_1_, bf16[128,3584]{1,0:T(8,128)(2,1)S(1)} %collective-permute-done.1.refs_2_, bf16[128,3584]{1,0:T(8,128)(2,1)S(1)} %collective-permute-done.7.refs_3_, ...), custom_call_target="tpu_custom_call" | custom-call | flops 2113929216 | bytes 8388608 | tf_op jit(solution)/shard_map/student/pallas_call | solution.py:163
  72.6 2.7 %collective-permute-start.14 = (f32[128,256]{1,0:T(8,128)S(1)}, f32[128,256]{1,0:T(8,128)S(1)}, u32[]{:S(2)}, u32[]{:S(2)}) collective-permute-start(f32[128,256]{1,0:T(8,128)S(1)} %get-tuple-element.18.refs_0_), channel_id=1, source_target_pairs={{0,192},{64,0},{128,64},{192,128},{1,193},{65,1},{129,65},{193,129... | collective-permute-start | bytes 393224 | tf_op jit(solution)/shard_map/ppermute | solution.py:19
  75.2 0.6 collective-permute-start.18
  75.8 0.6 collective-permute-start.13
  76.4 4.4 %collective-permute-done.14.refs_2_ = f32[128,256]{1,0:T(8,128)S(1)} collective-permute-done((f32[128,256]{1,0:T(8,128)S(1)}, f32[128,256]{1,0:T(8,128)S(1)}, u32[]{:S(2)}, u32[]{:S(2)}) %collective-permute-start.14) | collective-permute-done | bytes 131104 | tf_op jit(solution)/shard_map/ppermute | solution.py:19
  80.8 0.9 collective-permute-start.15
  81.7 1.6 %collective-permute-start.17 = (f32[128,256]{1,0:T(8,128)S(1)}, f32[128,256]{1,0:T(8,128)S(1)}, u32[]{:S(2)}, u32[]{:S(2)}) collective-permute-start(f32[128,256]{1,0:T(8,128)S(1)} %collective-permute-done.16.refs_4_), channel_id=1, source_target_pairs={{0,32},{32,0},{1,33},{33,1},{2,34},{34,2},{3,35},{35,3},{4,36},{36... | collective-permute-start | bytes 393224 | tf_op jit(solution)/shard_map/ppermute | solution.py:19
  83.4 1.0 collective-permute-done.18.refs_6_
  84.4 0.8 collective-permute-start.19
  85.2 5.8 %all-to-all-start.1 = ((f32[64,1,256]{2,1,0:T(1,128)}), f32[64,1,256]{2,1,0:T(1,128)S(1)}, u32[]{:S(2)}, u32[]{:S(2)}) async-start(f32[64,1,256]{2,1,0:T(1,128)} %get-tuple-element.19), calls=%async_computation.1 | async-start | bytes 131072 | tf_op jit(solution)/shard_map/all_to_all | solution.py:179
  91.0 1.1 %place.1 = f32[128,1792]{1,0:T(8,128)} custom-call(f32[128,256]{1,0:T(8,128)S(1)} %get-tuple-element.18.refs_0_, f32[128,256]{1,0:T(8,128)S(1)} %collective-permute-done.13.refs_1_, f32[128,256]{1,0:T(8,128)S(1)} %collective-permute-done.14.refs_2_, f32[128,256]{1,0:T(8,128)S(1)} %collective-permute-done.15.refs_3_, ...), custom_call_target="tpu_custom_call" | custom-call | tf_op jit(solution)/shard_map/place/pallas_call | solution.py:184
  92.2 10.8 %all-to-all-done.1.grads_ref = f32[64,1,256]{2,1,0:T(1,128)S(1)} async-done(((f32[64,1,256]{2,1,0:T(1,128)}), f32[64,1,256]{2,1,0:T(1,128)S(1)}, u32[]{:S(2)}, u32[]{:S(2)}) %all-to-all-start.1) | async-done | bytes 65568 | tf_op jit(solution)/shard_map/all_to_all | solution.py:179
  103.0 0.6 add.31
  (29 shorter events, 0.3 us)
Async XLA Ops:
  0.6 1.2 %copy-start = (bf16[128,3584]{1,0:T(8,128)(2,1)S(1)}, bf16[128,3584]{1,0:T(8,128)(2,1)}, u32[]{:S(2)}) copy-start(bf16[128,3584]{1,0:T(8,128)(2,1)} %refs_10_.1) | copy-start | bytes 2752516
  1.8 1.5 %copy-start.2 = (s32[1,128,3584]{2,1,0:T(8,128)S(1)}, s32[1,128,3584]{2,1,0:T(8,128)}, u32[]{:S(2)}) copy-start(s32[1,128,3584]{2,1,0:T(8,128)} %mask_hbm.1) | copy-start | bytes 5505028
  3.3 0.9 copy-start.3
  4.2 46.4 %copy-start.8 = (f32[1792]{0:T(1024)S(1)}, f32[1792]{0:T(1024)}, u32[]{:S(2)}) copy-start(f32[1792]{0:T(1024)} %param.7) | copy-start | bytes 21508
  5.9 25.9 %all-to-all-start = ((bf16[16,56,256]{2,1,0:T(8,128)(2,1)}), bf16[16,56,256]{2,1,0:T(8,128)(2,1)S(1)}, u32[]{:S(2)}, u32[]{:S(2)}) async-start(bf16[16,56,256]{2,1,0:T(8,128)(2,1)} %get-tuple-element.13), calls=%async_computation | async-start | bytes 917504 | tf_op jit(solution)/shard_map/all_to_all | solution.py:143
  18.5 32.5 %collective-permute-start.1 = (bf16[128,3584]{1,0:T(8,128)(2,1)S(1)}, bf16[128,3584]{1,0:T(8,128)(2,1)S(1)}, u32[]{:S(2)}, u32[]{:S(2)}) collective-permute-start(bf16[128,3584]{1,0:T(8,128)(2,1)S(1)} %get-tuple-element.12.refs_0_), channel_id=1, source_target_pairs={{0,64},{64,128},{128,192},{192,0},{1,65},{65,129},{129,193},{193,1... | collective-permute-start | bytes 2752520 | tf_op jit(solution)/shard_map/ppermute | solution.py:19
  19.9 32.4 %collective-permute-start.2 = (bf16[128,3584]{1,0:T(8,128)(2,1)S(1)}, bf16[128,3584]{1,0:T(8,128)(2,1)S(1)}, u32[]{:S(2)}, u32[]{:S(2)}) collective-permute-start(bf16[128,3584]{1,0:T(8,128)(2,1)S(1)} %get-tuple-element.12.refs_0_), channel_id=1, source_target_pairs={{0,192},{64,0},{128,64},{192,128},{1,193},{65,1},{129,65},{193,129... | collective-permute-start | bytes 2752520 | tf_op jit(solution)/shard_map/ppermute | solution.py:19
  31.8 13.4 %collective-permute-start.3 = (bf16[8,2,56,256]{3,2,1,0:T(8,128)(2,1)S(1)}, bf16[8,2,56,256]{3,2,1,0:T(8,128)(2,1)S(1)}, u32[]{:S(2)}, u32[]{:S(2)}) collective-permute-start(bf16[8,2,56,256]{3,2,1,0:T(8,128)(2,1)S(1)} %bitcast.20), channel_id=1, source_target_pairs={{0,1},{1,2},{2,3},{3,0},{4,5},{5,6},{6,7},{7,4},{8,9},{9,10},{10,1... | collective-permute-start | bytes 1376264 | tf_op jit(solution)/shard_map/ppermute | solution.py:19
  33.0 13.0 %collective-permute-start.5 = (bf16[8,2,56,256]{3,2,1,0:T(8,128)(2,1)S(1)}, bf16[8,2,56,256]{3,2,1,0:T(8,128)(2,1)S(1)}, u32[]{:S(2)}, u32[]{:S(2)}) collective-permute-start(bf16[8,2,56,256]{3,2,1,0:T(8,128)(2,1)S(1)} %bitcast.21), channel_id=1, source_target_pairs={{0,3},{1,0},{2,1},{3,2},{4,7},{5,4},{6,5},{7,6},{8,11},{9,8},{10,9... | collective-permute-start | bytes 1376264 | tf_op jit(solution)/shard_map/ppermute | solution.py:19
  45.2 1.5 %copy-start.4 = (bf16[8,2,56,256]{3,2,1,0:T(8,128)(2,1)}, bf16[8,2,56,256]{3,2,1,0:T(8,128)(2,1)S(1)}, u32[]{:S(2)}) copy-start(bf16[8,2,56,256]{3,2,1,0:T(8,128)(2,1)S(1)} %collective-permute-done.3) | copy-start | bytes 1376260
  46.0 8.0 %collective-permute-start.4 = (bf16[4,2,56,256]{3,2,1,0:T(8,128)(2,1)}, bf16[4,2,56,256]{3,2,1,0:T(8,128)(2,1)}, u32[]{:S(2)}, u32[]{:S(2)}) collective-permute-start(bf16[4,2,56,256]{3,2,1,0:T(8,128)(2,1)} %slice.16), channel_id=1, source_target_pairs={{0,1},{1,2},{2,3},{3,0},{4,5},{5,6},{6,7},{7,4},{8,9},{9,10},{10,1... | collective-permute-start | bytes 688136 | tf_op jit(solution)/shard_map/ppermute | solution.py:19
  46.0 3.4 %copy-start.6 = (bf16[8,2,56,256]{3,2,1,0:T(8,128)(2,1)}, bf16[8,2,56,256]{3,2,1,0:T(8,128)(2,1)S(1)}, u32[]{:S(2)}) copy-start(bf16[8,2,56,256]{3,2,1,0:T(8,128)(2,1)S(1)} %collective-permute-done.5) | copy-start | bytes 1376260
  46.7 7.2 %collective-permute-start.6 = (bf16[4,2,56,256]{3,2,1,0:T(8,128)(2,1)}, bf16[4,2,56,256]{3,2,1,0:T(8,128)(2,1)}, u32[]{:S(2)}, u32[]{:S(2)}) collective-permute-start(bf16[4,2,56,256]{3,2,1,0:T(8,128)(2,1)} %slice.17), channel_id=1, source_target_pairs={{0,3},{1,0},{2,1},{3,2},{4,7},{5,4},{6,5},{7,6},{8,11},{9,8},{10,9... | collective-permute-start | bytes 688136 | tf_op jit(solution)/shard_map/ppermute | solution.py:19
  49.4 17.9 %collective-permute-start = (bf16[128,3584]{1,0:T(8,128)(2,1)S(1)}, bf16[128,3584]{1,0:T(8,128)(2,1)}, u32[]{:S(2)}, u32[]{:S(2)}) collective-permute-start(bf16[128,3584]{1,0:T(8,128)(2,1)S(1)} %get-tuple-element.12.refs_0_), channel_id=1, source_target_pairs={{0,32},{32,0},{1,33},{33,1},{2,34},{34,2},{3,35},{35,3},{4,36},{36... | collective-permute-start | bytes 2752520 | tf_op jit(solution)/shard_map/ppermute | solution.py:19
  50.9 4.6 %copy-start.5 = (bf16[8,2,56,256]{3,2,1,0:T(8,128)(2,1)S(1)}, bf16[8,2,56,256]{3,2,1,0:T(8,128)(2,1)}, u32[]{:S(2)}) copy-start(bf16[8,2,56,256]{3,2,1,0:T(8,128)(2,1)} %copy-done.4) | copy-start | bytes 1376260
  50.9 4.7 %copy-start.7 = (bf16[8,2,56,256]{3,2,1,0:T(8,128)(2,1)S(1)}, bf16[8,2,56,256]{3,2,1,0:T(8,128)(2,1)}, u32[]{:S(2)}) copy-start(bf16[8,2,56,256]{3,2,1,0:T(8,128)(2,1)} %copy-done.6) | copy-start | bytes 1376260
  51.0 16.3 %copy-start.1 = (bf16[128,3584]{1,0:T(8,128)(2,1)S(1)}, bf16[128,3584]{1,0:T(8,128)(2,1)}, u32[]{:S(2)}) copy-start(bf16[128,3584]{1,0:T(8,128)(2,1)} %refs_10_.1) | copy-start | bytes 2752516
  51.0 13.4 %collective-permute-start.9 = (bf16[64,3584]{1,0:T(8,128)(2,1)S(1)}, bf16[64,3584]{1,0:T(8,128)(2,1)S(1)}, u32[]{:S(2)}, u32[]{:S(2)}) collective-permute-start(bf16[64,3584]{1,0:T(8,128)(2,1)S(1)} %slice.18), channel_id=1, source_target_pairs={{0,64},{64,128},{128,192},{192,0},{1,65},{65,129},{129,193},{193,1... | collective-permute-start | bytes 1376264 | tf_op jit(solution)/shard_map/ppermute | solution.py:19
  52.4 12.9 %collective-permute-start.11 = (bf16[64,3584]{1,0:T(8,128)(2,1)S(1)}, bf16[64,3584]{1,0:T(8,128)(2,1)S(1)}, u32[]{:S(2)}, u32[]{:S(2)}) collective-permute-start(bf16[64,3584]{1,0:T(8,128)(2,1)S(1)} %slice.19), channel_id=1, source_target_pairs={{0,192},{64,0},{128,64},{192,128},{1,193},{65,1},{129,65},{193,129... | collective-permute-start | bytes 1376264 | tf_op jit(solution)/shard_map/ppermute | solution.py:19
  53.9 13.4 %collective-permute-start.7 = (bf16[128,3584]{1,0:T(8,128)(2,1)S(1)}, bf16[128,3584]{1,0:T(8,128)(2,1)S(1)}, u32[]{:S(2)}, u32[]{:S(2)}) collective-permute-start(bf16[128,3584]{1,0:T(8,128)(2,1)S(1)} %collective-permute-done.1.refs_2_), channel_id=1, source_target_pairs={{0,32},{32,0},{1,33},{33,1},{2,34},{34,2},{3,35},{35,3},{4,36},{36... | collective-permute-start | bytes 2752520 | tf_op jit(solution)/shard_map/ppermute | solution.py:19
  55.5 11.8 %collective-permute-start.8 = (bf16[128,3584]{1,0:T(8,128)(2,1)S(1)}, bf16[128,3584]{1,0:T(8,128)(2,1)S(1)}, u32[]{:S(2)}, u32[]{:S(2)}) collective-permute-start(bf16[128,3584]{1,0:T(8,128)(2,1)S(1)} %collective-permute-done.2.refs_4_), channel_id=1, source_target_pairs={{0,32},{32,0},{1,33},{33,1},{2,34},{34,2},{3,35},{35,3},{4,36},{36... | collective-permute-start | bytes 2752520 | tf_op jit(solution)/shard_map/ppermute | solution.py:19
  64.5 2.8 %collective-permute-start.10 = (bf16[64,3584]{1,0:T(8,128)(2,1)S(1)}, bf16[64,3584]{1,0:T(8,128)(2,1)S(1)}, u32[]{:S(2)}, u32[]{:S(2)}) collective-permute-start(bf16[64,3584]{1,0:T(8,128)(2,1)S(1)} %collective-permute-done.9.refs_6_), channel_id=1, source_target_pairs={{0,32},{32,0},{1,33},{33,1},{2,34},{34,2},{3,35},{35,3},{4,36},{36... | collective-permute-start | bytes 1376264 | tf_op jit(solution)/shard_map/ppermute | solution.py:19
  65.3 2.1 %collective-permute-start.12 = (bf16[64,3584]{1,0:T(8,128)(2,1)S(1)}, bf16[64,3584]{1,0:T(8,128)(2,1)S(1)}, u32[]{:S(2)}, u32[]{:S(2)}) collective-permute-start(bf16[64,3584]{1,0:T(8,128)(2,1)S(1)} %collective-permute-done.11.refs_8_), channel_id=1, source_target_pairs={{0,32},{32,0},{1,33},{33,1},{2,34},{34,2},{3,35},{35,3},{4,36},{36... | collective-permute-start | bytes 1376264 | tf_op jit(solution)/shard_map/ppermute | solution.py:19
  72.6 8.3 %collective-permute-start.14 = (f32[128,256]{1,0:T(8,128)S(1)}, f32[128,256]{1,0:T(8,128)S(1)}, u32[]{:S(2)}, u32[]{:S(2)}) collective-permute-start(f32[128,256]{1,0:T(8,128)S(1)} %get-tuple-element.18.refs_0_), channel_id=1, source_target_pairs={{0,192},{64,0},{128,64},{192,128},{1,193},{65,1},{129,65},{193,129... | collective-permute-start | bytes 393224 | tf_op jit(solution)/shard_map/ppermute | solution.py:19
  75.2 6.5 %collective-permute-start.16 = (f32[128,256]{1,0:T(8,128)S(1)}, f32[128,256]{1,0:T(8,128)S(1)}, u32[]{:S(2)}, u32[]{:S(2)}) collective-permute-start(f32[128,256]{1,0:T(8,128)S(1)} %get-tuple-element.18.refs_0_), channel_id=1, source_target_pairs={{0,128},{64,192},{128,0},{192,64},{1,129},{65,193},{129,1},{193,65... | collective-permute-start | bytes 393224 | tf_op jit(solution)/shard_map/ppermute | solution.py:19
  75.2 9.1 %collective-permute-start.18 = (f32[128,256]{1,0:T(8,128)S(1)}, f32[128,256]{1,0:T(8,128)S(1)}, u32[]{:S(2)}, u32[]{:S(2)}) collective-permute-start(f32[128,256]{1,0:T(8,128)S(1)} %get-tuple-element.18.refs_0_), channel_id=1, source_target_pairs={{0,64},{64,128},{128,192},{192,0},{1,65},{65,129},{129,193},{193,1... | collective-permute-start | bytes 393224 | tf_op jit(solution)/shard_map/ppermute | solution.py:19
  75.8 15.2 %collective-permute-start.13 = (f32[128,256]{1,0:T(8,128)S(1)}, f32[128,256]{1,0:T(8,128)S(1)}, u32[]{:S(2)}, u32[]{:S(2)}) collective-permute-start(f32[128,256]{1,0:T(8,128)S(1)} %get-tuple-element.18.refs_0_), channel_id=1, source_target_pairs={{0,32},{32,0},{1,33},{33,1},{2,34},{34,2},{3,35},{35,3},{4,36},{36... | collective-permute-start | bytes 393224 | tf_op jit(solution)/shard_map/ppermute | solution.py:19
  80.8 10.2 %collective-permute-start.15 = (f32[128,256]{1,0:T(8,128)S(1)}, f32[128,256]{1,0:T(8,128)S(1)}, u32[]{:S(2)}, u32[]{:S(2)}) collective-permute-start(f32[128,256]{1,0:T(8,128)S(1)} %collective-permute-done.14.refs_2_), channel_id=1, source_target_pairs={{0,32},{32,0},{1,33},{33,1},{2,34},{34,2},{3,35},{35,3},{4,36},{36... | collective-permute-start | bytes 393224 | tf_op jit(solution)/shard_map/ppermute | solution.py:19
  81.7 9.2 %collective-permute-start.17 = (f32[128,256]{1,0:T(8,128)S(1)}, f32[128,256]{1,0:T(8,128)S(1)}, u32[]{:S(2)}, u32[]{:S(2)}) collective-permute-start(f32[128,256]{1,0:T(8,128)S(1)} %collective-permute-done.16.refs_4_), channel_id=1, source_target_pairs={{0,32},{32,0},{1,33},{33,1},{2,34},{34,2},{3,35},{35,3},{4,36},{36... | collective-permute-start | bytes 393224 | tf_op jit(solution)/shard_map/ppermute | solution.py:19
  84.4 6.6 %collective-permute-start.19 = (f32[128,256]{1,0:T(8,128)S(1)}, f32[128,256]{1,0:T(8,128)S(1)}, u32[]{:S(2)}, u32[]{:S(2)}) collective-permute-start(f32[128,256]{1,0:T(8,128)S(1)} %collective-permute-done.18.refs_6_), channel_id=1, source_target_pairs={{0,32},{32,0},{1,33},{33,1},{2,34},{34,2},{3,35},{35,3},{4,36},{36... | collective-permute-start | bytes 393224 | tf_op jit(solution)/shard_map/ppermute | solution.py:19
  85.2 17.8 %all-to-all-start.1 = ((f32[64,1,256]{2,1,0:T(1,128)}), f32[64,1,256]{2,1,0:T(1,128)S(1)}, u32[]{:S(2)}, u32[]{:S(2)}) async-start(f32[64,1,256]{2,1,0:T(1,128)} %get-tuple-element.19), calls=%async_computation.1 | async-start | bytes 131072 | tf_op jit(solution)/shard_map/all_to_all | solution.py:179

commit v4 on v3

--- a/solution.py
+++ b/solution.py
@@ -25,21 +25,41 @@
     return pl.multiple_of(start, 128)
 
 
-def prepare_kernel(mask_hbm, features_hbm, weight_hbm, driven_ref, payload_ref, mask_ref, features_ref, weight_ref, sems):
-    copies = [
-        pltpu.make_async_copy(a, b, sems.at[i])
-        for i, (a, b) in enumerate(((mask_hbm, mask_ref), (features_hbm, features_ref), (weight_hbm, weight_ref)))
+def window_kernel(weight_ref, payload_ref):
+    for w, s in enumerate(STARTS):
+        payload_ref[w] = weight_ref[:, s : s + WIDE]
+
+
+def assemble_kernel(*refs):
+    pieces, out_ref = refs[:-1], refs[-1]
+    z, x = lax.axis_index("z"), lax.axis_index("x")
+    for i, piece in enumerate(pieces):
+        out_ref[:, (z + i // X) % Z, (x + i % X) % X] = piece[...]
+
+
+def drive_kernel(mask_hbm, features_hbm, driven_hbm, mask_ref, features_ref, driven_ref, sems):
+    parts = sems.shape[0]
+    tall = features_ref.shape[0] // parts
+    spans = [pl.ds(i * tall, tall) for i in range(parts)]
+    arriving = [
+        (
+            pltpu.make_async_copy(mask_hbm.at[0, at], mask_ref.at[at], sems.at[i, 0]),
+            pltpu.make_async_copy(features_hbm.at[at], features_ref.at[at], sems.at[i, 1]),
+        )
+        for i, at in enumerate(spans)
     ]
-    for c in copies:
-        c.start()
-    for c in copies[:2]:
-        c.wait()
-    kept = jnp.where(mask_ref[0] > 0, features_ref[...].astype(jnp.float32), 0.0)
-    driven_ref[...] = kept.astype(driven_ref.dtype)
-    copies[2].wait()
-    for w, s in enumerate(STARTS):
-        for z in range(Z):
-            payload_ref[w * Z + z] = weight_ref[:, s : s + WIDE]
+    leaving = [pltpu.make_async_copy(driven_ref.at[at], driven_hbm.at[at], sems.at[i, 2]) for i, at in enumerate(spans)]
+    for pair in arriving:
+        for copy in pair:
+            copy.start()
+    for at, pair, out in zip(spans, arriving, leaving):
+        for copy in pair:
+            copy.wait()
+        kept = jnp.where(mask_ref[at, :] > 0, features_ref[at, :].astype(jnp.float32), 0.0)
+        driven_ref[at, :] = kept.astype(driven_ref.dtype)
+        out.start()
+    for out in leaving:
+        out.wait()
 
 
 def student_kernel(*refs, tokens_all, spans):
@@ -85,22 +105,22 @@
     grad_ref[...] = jnp.broadcast_to(jnp.sum(grad_sum, axis=0, keepdims=True)[None], grad_ref.shape)
 
 
-def place_kernel(*refs):
-    out_ref = refs[-1]
+def place_kernel(mine_ref, other_ref, out_ref):
+    rows = out_ref.shape[0]
     core, y = lax.axis_index("core"), lax.axis_index("y")
     for j in range(Y):
-        for k in range(CORE):
+        for k, piece in enumerate((mine_ref, other_ref)):
             from_y, from_core = (y + j) % Y, (core + k) % CORE
             start = start_of(from_y, from_core)
-            piece = refs[CORE * j + k]
+            at = slice(j * rows, (j + 1) * rows)
 
             @pl.when((from_core == 0) | (from_y % 2 == 1))
             def _():
-                out_ref[:, pl.ds(start, WIDE)] = piece[...]
+                out_ref[:, pl.ds(start, WIDE)] = piece[at, :]
 
             @pl.when((from_core == 1) & (from_y % 2 == 0))
             def _():
-                out_ref[:, pl.ds(pl.multiple_of(start + 128, 128), WIDE - 128)] = piece[:, 128:]
+                out_ref[:, pl.ds(pl.multiple_of(start + 128, 128), WIDE - 128)] = piece[at, 128:]
 
 
 def add_kernel(grads_ref, out_ref):
@@ -112,40 +132,49 @@
 
 
 def on_device(features, spike_mask, gate_weight, threshold):
-    x = lax.axis_index("x")
     rows, deep = features.shape
     tokens_all = rows * Z * X
     half = rows // 2
     part, width = gate_weight.shape
     vmem = pl.BlockSpec(memory_space=pltpu.VMEM)
 
-    own, payload = pl.pallas_call(
-        prepare_kernel,
-        out_shape=(
-            jax.ShapeDtypeStruct((rows, deep), features.dtype),
-            jax.ShapeDtypeStruct((STEPS * Z, part, WIDE), gate_weight.dtype),
-        ),
-        in_specs=[pl.BlockSpec(memory_space=pltpu.HBM)] * 3,
-        out_specs=(vmem,) * 2,
+    def along_x(held):
+        return around(held, "x", -1), around(held, "x", 2), around(held, "x", 1)
+
+    hbm = pl.BlockSpec(memory_space=pl.ANY)
+    own = pl.pallas_call(
+        drive_kernel,
+        out_shape=jax.ShapeDtypeStruct((rows, deep), features.dtype),
+        in_specs=[hbm] * 2,
+        out_specs=hbm,
         scratch_shapes=[
-            pltpu.VMEM(spike_mask.shape, spike_mask.dtype),
-            pltpu.VMEM(features.shape, features.dtype),
-            pltpu.VMEM(gate_weight.shape, gate_weight.dtype),
-            pltpu.SemaphoreType.DMA((3,)),
+            pltpu.VMEM((rows, deep), spike_mask.dtype),
+            pltpu.VMEM((rows, deep), features.dtype),
+            pltpu.VMEM((rows, deep), features.dtype),
+            pltpu.SemaphoreType.DMA((4, 3)),
         ],
-        compiler_params=pltpu.CompilerParams(vmem_limit_bytes=8 * MIB),
-        name="prepare",
-    )(spike_mask, features, gate_weight)
-
+        compiler_params=pltpu.CompilerParams(vmem_limit_bytes=60 * MIB),
+        name="drive",
+    )(spike_mask, features)
+
+    payload = pl.pallas_call(
+        window_kernel,
+        out_shape=jax.ShapeDtypeStruct((STEPS, part, WIDE), gate_weight.dtype),
+        in_specs=[vmem],
+        out_specs=vmem,
+        compiler_params=pltpu.CompilerParams(vmem_limit_bytes=4 * MIB),
+        name="windows",
+    )(gate_weight)
+    near_w = lax.all_to_all(payload, ("y", "core"), 0, 0, tiled=True)
+    own, near_w = lax.optimization_barrier((own, near_w))
     s_p, s_m = around(own, "y", 1), around(own, "y", -1)
+    near_x = along_x(near_w)
+    far_w = around(near_w, "z", 1)
+    s_p, s_m, far_w, *near_x = lax.optimization_barrier((s_p, s_m, far_w, *near_x))
     s_f0, s_f1 = around(s_p[:half], "y", 1), around(s_m[half:], "y", -1)
-
-    landed = lax.all_to_all(payload, ("y", "core", "z"), 0, 0, tiled=True).reshape(STEPS, Z, part, WIDE)
-    w_p, w_m = around(landed, "x", 1), around(landed, "x", -1)
-    cut = STEPS // 2
-    w_f0, w_f1 = around(w_p[:cut], "x", 1), around(w_m[cut:], "x", -1)
-    s_q, s_n, w_f0, w_f1 = lax.optimization_barrier((s_p, s_m, w_f0, w_f1))
-    o_own, o_p, o_m = (around(v, "core", 1) for v in (own, s_q, s_n))
+    far_x = along_x(far_w)
+    s_f0, s_f1, *far_x = lax.optimization_barrier((s_f0, s_f1, *far_x))
+    o_own, o_p, o_m = (around(v, "core", 1) for v in (own, s_p, s_m))
     o_f0, o_f1 = around(s_f0, "core", 1), around(s_f1, "core", 1)
     steps, spans = [], []
     for mine, other, dy, first, tall in (
@@ -153,13 +182,17 @@
     ):
         steps += [mine, other]
         spans += [(dy, 0, first, tall), (dy, 1, first, tall)]
-
-    weight = jnp.zeros((STEPS, Z, X, part, WIDE), gate_weight.dtype)
-    for piece, at, dx in ((landed, 0, 0), (w_p, 0, 3), (w_m, 0, 1), (w_f0, 0, 2), (w_f1, cut, 2)):
-        weight = lax.dynamic_update_slice(weight, piece[:, :, None], (at, 0, lax.rem(x + dx, X), 0, 0))
+    weight = pl.pallas_call(
+        assemble_kernel,
+        out_shape=jax.ShapeDtypeStruct((STEPS, Z, X, part, WIDE), gate_weight.dtype),
+        in_specs=[vmem] * (Z * X),
+        out_specs=vmem,
+        compiler_params=pltpu.CompilerParams(vmem_limit_bytes=8 * MIB),
+        name="assemble",
+    )(near_w, *near_x, far_w, *far_x)
     weight = weight.reshape(deep, WIDE)
 
-    peers = Y * CORE * Z * X
+    peers = STEPS * Z * X
     rates, grad = pl.pallas_call(
         functools.partial(student_kernel, tokens_all=tokens_all, spans=spans),
         out_shape=(
@@ -176,21 +209,21 @@
         name="student",
     )(*steps, features, weight, threshold[None])
 
+    rates_y = [around(rates, "y", -1), around(rates, "y", 2), around(rates, "y", 1)]
     grads = lax.all_to_all(grad, ("y", "core", "z", "x"), 0, 0, tiled=True)
-
-    pieces = []
-    for piece in (rates, around(rates, "y", -1), around(rates, "y", 2), around(rates, "y", 1)):
-        pieces += [piece, around(piece, "core", 1)]
+    *rates_y, grads = lax.optimization_barrier((*rates_y, grads))
+    mine = jnp.concatenate([rates] + rates_y)
+    other = around(mine, "core", 1)
     rates_out = pl.pallas_call(
         place_kernel,
         out_shape=jax.ShapeDtypeStruct((rows, width), jnp.float32),
-        in_specs=[vmem] * 8,
+        in_specs=[vmem] * 2,
         out_specs=vmem,
         compiler_params=pltpu.CompilerParams(vmem_limit_bytes=4 * MIB),
         cost_estimate=pl.CostEstimate(flops=0, bytes_accessed=0, transcendentals=0),
         name="place",
-    )(*pieces)
-    rates_out, grads = lax.optimization_barrier((rates_out, grads))
+    )(mine, other)
+
 
     grad_out = pl.pallas_call(
         add_kernel,
@@ -198,7 +231,6 @@
         in_specs=[vmem],
         out_specs=vmem,
         compiler_params=pltpu.CompilerParams(vmem_limit_bytes=4 * MIB),
-        cost_estimate=pl.CostEstimate(flops=0, bytes_accessed=64 * MIB, transcendentals=0),
         name="add",
     )(grads)
     return rates_out, grad_out

time: 105 us -> 93.6 us (0.89); the launches traced: 104 us -> 93.3 us
  waiting for transfers between devices: 46.5 us -> 29.5 us
  starting transfers between devices: 40.2 us -> 52.8 us
  local copies, waits for them, and re-layouts: 7.42 us -> 1.05 us
    ppermute x20, starting transfers between devices: 21.8 us -> 33.7 us  [around(): return lax.ppermute(x, axis, [(i, (i + by) % n) for i in range(n)])]
    ppermute x20, waiting for transfers between devices: 25.1 us -> 13.9 us  [around(): return lax.ppermute(x, axis, [(i, (i + by) % n) for i in range(n)])]
    all_to_all x1, waiting for transfers between devices: 10.6 us -> 3.6 us  [on_device(): near_w = lax.all_to_all(payload, ('y', 'core'), 0, 0, tiled=True)]
    all_to_all x1, starting transfers between devices: 5.8 us -> 12.5 us  [on_device(): grads = lax.all_to_all(grad, ('y', 'core', 'z', 'x'), 0, 0, tiled=True)]
    all_to_all x1, starting transfers between devices: 12.6 us -> 6.54 us  [on_device(): near_w = lax.all_to_all(payload, ('y', 'core'), 0, 0, tiled=True)]
    unnamed x18 -> x11, local copies, waits for them, and re-layouts: 3.63 us -> 0.97 us
    dynamic_update_slice x5 -> x0, local copies, waits for them, and re-layouts: 2.05 us -> none  [on_device(): lax.dynamic_update_slice(weight, piece[:, :, None], (at, 0, lax.rem(x + d...]
    pallas_call x1 -> x3, Pallas kernels: 1.63 us -> 3.43 us  [the longest x1 2.58 us: on_device(): pl.pallas_call(drive_kernel, out_shape=jax.ShapeDtypeStruct((rows, deep),...]
  transfers between devices with their start and end apart: 22 -> 22, of which waited for: 7 -> 10; matrix products, arithmetic and copies ran while one was open for 4% -> 0% of each run, Pallas kernels for 1% -> 4%
where the time goes in v4:
time: 93.6 us; the launch traced here: 93.3 us
  starting transfers between devices  52.8 us (56%)
  waiting for transfers between devices  29.5 us (32%)
  Pallas kernels  9.16 us (10%)
  local copies, waits for them, and re-layouts  1.05 us (1%)
    ppermute x20, starting transfers between devices, around(): return lax.ppermute(x, axis, [(i, (i + by) % n) for i in range(n)])  33.7 us
    ppermute x20, waiting for transfers between devices, around(): return lax.ppermute(x, axis, [(i, (i + by) % n) for i in range(n)])  13.9 us
    all_to_all x1, starting transfers between devices, on_device(): grads = lax.all_to_all(grad, ('y', 'core', 'z', 'x'), 0, 0, tiled=True)  12.5 us
    all_to_all x1, waiting for transfers between devices, on_device(): grads = lax.all_to_all(grad, ('y', 'core', 'z', 'x'), 0, 0, tiled=True)  12 us
    all_to_all x1, starting transfers between devices, on_device(): near_w = lax.all_to_all(payload, ('y', 'core'), 0, 0, tiled=True)  6.54 us
    pallas_call x1, Pallas kernels, on_device(): pl.pallas_call(functools.partial(student_kernel, tokens_all=tokens_all, s...  3.98 us
    all_to_all x1, waiting for transfers between devices, on_device(): near_w = lax.all_to_all(payload, ('y', 'core'), 0, 0, tiled=True)  3.6 us
    pallas_call x1, Pallas kernels, on_device(): pl.pallas_call(drive_kernel, out_shape=jax.ShapeDtypeStruct((rows, deep),...  2.58 us
  transfers between devices with their start and end apart: 22, of which 10 were waited for; matrix products, arithmetic and copies ran while one was open for 0% of the time, Pallas kernels for 4%

profile of v4, /device:TPU:1, one launch (start us, length us, event | category | flops | bytes accessed | tf_op | source)
XLA Modules:
  0.0 93.3 jit_solution(7094680480956962042)
XLA Ops:
  0.6 0.9 copy-done.2
  1.6 0.7 windows.1
  2.3 6.5 %all-to-all-start = ((bf16[8,56,256]{2,1,0:T(8,128)(2,1)}), bf16[8,56,256]{2,1,0:T(8,128)(2,1)S(1)}, u32[]{:S(2)}, u32[]{:S(2)}) async-start(bf16[8,56,256]{2,1,0:T(8,128)(2,1)} %windows.1), calls=%async_computation | async-start | bytes 458752 | tf_op jit(solution)/shard_map/all_to_all | solution.py:168
  8.8 2.6 %drive.1.refs_0_ = bf16[128,3584]{1,0:T(8,128)(2,1)} custom-call(s32[1,128,3584]{2,1,0:T(8,128)} %mask_hbm.1, bf16[128,3584]{1,0:T(8,128)(2,1)} %refs_10_.1), custom_call_target="tpu_custom_call" | custom-call | tf_op jit(solution)/shard_map/drive/pallas_call | solution.py:145
  11.4 0.0 copy-start.1
  11.4 0.0 copy-start.3
  11.4 3.6 %all-to-all-done.refs_0_ = bf16[8,56,256]{2,1,0:T(8,128)(2,1)S(1)} async-done(((bf16[8,56,256]{2,1,0:T(8,128)(2,1)}), bf16[8,56,256]{2,1,0:T(8,128)(2,1)S(1)}, u32[]{:S(2)}, u32[]{:S(2)}) %all-to-all-start) | async-done | bytes 229408 | tf_op jit(solution)/shard_map/all_to_all | solution.py:168
  15.0 0.9 collective-permute-start.2
  15.9 0.6 collective-permute-start.1
  16.5 0.6 collective-permute-start.6
  17.1 2.5 %collective-permute-start.5 = (bf16[8,56,256]{2,1,0:T(8,128)(2,1)S(1)}, bf16[8,56,256]{2,1,0:T(8,128)(2,1)S(1)}, u32[]{:S(2)}, u32[]{:S(2)}) collective-permute-start(bf16[8,56,256]{2,1,0:T(8,128)(2,1)S(1)} %all-to-all-done.refs_0_), channel_id=1, source_target_pairs={{0,2},{1,3},{2,0},{3,1},{4,6},{5,7},{6,4},{7,5},{8,10},{9,11},{10,... | collective-permute-start | bytes 688136 | tf_op jit(solution)/shard_map/ppermute | solution.py:19
  19.6 1.2 %collective-permute-start.4 = (bf16[8,56,256]{2,1,0:T(8,128)(2,1)S(1)}, bf16[8,56,256]{2,1,0:T(8,128)(2,1)S(1)}, u32[]{:S(2)}, u32[]{:S(2)}) collective-permute-start(bf16[8,56,256]{2,1,0:T(8,128)(2,1)S(1)} %all-to-all-done.refs_0_), channel_id=1, source_target_pairs={{0,3},{1,0},{2,1},{3,2},{4,7},{5,4},{6,5},{7,6},{8,11},{9,8},{10,9... | collective-permute-start | bytes 688136 | tf_op jit(solution)/shard_map/ppermute | solution.py:19
  20.7 2.5 %collective-permute-done.6.refs_3_ = bf16[8,56,256]{2,1,0:T(8,128)(2,1)S(1)} collective-permute-done((bf16[8,56,256]{2,1,0:T(8,128)(2,1)S(1)}, bf16[8,56,256]{2,1,0:T(8,128)(2,1)S(1)}, u32[]{:S(2)}, u32[]{:S(2)}) %collective-permute-start.6) | collective-permute-done | bytes 229408 | tf_op jit(solution)/shard_map/ppermute | solution.py:19
  23.2 6.3 %collective-permute-start.3 = (bf16[8,56,256]{2,1,0:T(8,128)(2,1)S(1)}, bf16[8,56,256]{2,1,0:T(8,128)(2,1)S(1)}, u32[]{:S(2)}, u32[]{:S(2)}) collective-permute-start(bf16[8,56,256]{2,1,0:T(8,128)(2,1)S(1)} %all-to-all-done.refs_0_), channel_id=1, source_target_pairs={{0,4},{4,0},{1,5},{5,1},{2,6},{6,2},{3,7},{7,3},{8,12},{12,8},{9,1... | collective-permute-start | bytes 688136 | tf_op jit(solution)/shard_map/ppermute | solution.py:19
  29.6 0.0 collective-permute-done.5.refs_2_
  29.6 0.0 collective-permute-done.4.refs_1_
  29.6 3.5 %collective-permute-done.3.refs_4_ = bf16[8,56,256]{2,1,0:T(8,128)(2,1)S(1)} collective-permute-done((bf16[8,56,256]{2,1,0:T(8,128)(2,1)S(1)}, bf16[8,56,256]{2,1,0:T(8,128)(2,1)S(1)}, u32[]{:S(2)}, u32[]{:S(2)}) %collective-permute-start.3) | collective-permute-done | bytes 229408 | tf_op jit(solution)/shard_map/ppermute | solution.py:19
  33.1 3.0 %collective-permute-done.2.refs_4_ = bf16[128,3584]{1,0:T(8,128)(2,1)S(1)} collective-permute-done((bf16[128,3584]{1,0:T(8,128)(2,1)}, bf16[128,3584]{1,0:T(8,128)(2,1)S(1)}, u32[]{:S(2)}, u32[]{:S(2)}) %collective-permute-start.2) | collective-permute-done | bytes 917536 | tf_op jit(solution)/shard_map/ppermute | solution.py:19
  36.1 1.8 %collective-permute-done.1.refs_2_ = bf16[128,3584]{1,0:T(8,128)(2,1)S(1)} collective-permute-done((bf16[128,3584]{1,0:T(8,128)(2,1)}, bf16[128,3584]{1,0:T(8,128)(2,1)S(1)}, u32[]{:S(2)}, u32[]{:S(2)}) %collective-permute-start.1) | collective-permute-done | bytes 917536 | tf_op jit(solution)/shard_map/ppermute | solution.py:19
  37.9 0.6 collective-permute-start.13
  38.5 2.5 %collective-permute-start.12 = (bf16[8,56,256]{2,1,0:T(8,128)(2,1)S(1)}, bf16[8,56,256]{2,1,0:T(8,128)(2,1)S(1)}, u32[]{:S(2)}, u32[]{:S(2)}) collective-permute-start(bf16[8,56,256]{2,1,0:T(8,128)(2,1)S(1)} %collective-permute-done.3.refs_4_), channel_id=1, source_target_pairs={{0,2},{1,3},{2,0},{3,1},{4,6},{5,7},{6,4},{7,5},{8,10},{9,11},{10,... | collective-permute-start | bytes 688136 | tf_op jit(solution)/shard_map/ppermute | solution.py:19
  41.0 1.2 %collective-permute-start.11 = (bf16[8,56,256]{2,1,0:T(8,128)(2,1)S(1)}, bf16[8,56,256]{2,1,0:T(8,128)(2,1)S(1)}, u32[]{:S(2)}, u32[]{:S(2)}) collective-permute-start(bf16[8,56,256]{2,1,0:T(8,128)(2,1)S(1)} %collective-permute-done.3.refs_4_), channel_id=1, source_target_pairs={{0,3},{1,0},{2,1},{3,2},{4,7},{5,4},{6,5},{7,6},{8,11},{9,8},{10,9... | collective-permute-start | bytes 688136 | tf_op jit(solution)/shard_map/ppermute | solution.py:19
  42.2 0.4 collective-permute-start.10
  42.6 1.2 %collective-permute-start.9 = (bf16[64,3584]{1,0:T(8,128)(2,1)S(1)}, bf16[64,3584]{1,0:T(8,128)(2,1)S(1)}, u32[]{:S(2)}, u32[]{:S(2)}) collective-permute-start(bf16[64,3584]{1,0:T(8,128)(2,1)S(1)} %slice.6), channel_id=1, source_target_pairs={{0,64},{64,128},{128,192},{192,0},{1,65},{65,129},{129,193},{193,1... | collective-permute-start | bytes 1376264 | tf_op jit(solution)/shard_map/ppermute | solution.py:19
  43.7 0.2 collective-permute-done.13.refs_7_
  44.0 5.8 %collective-permute-start = (bf16[128,3584]{1,0:T(8,128)(2,1)S(1)}, bf16[128,3584]{1,0:T(8,128)(2,1)S(1)}, u32[]{:S(2)}, u32[]{:S(2)}) collective-permute-start(bf16[128,3584]{1,0:T(8,128)(2,1)S(1)} %copy-done.1), channel_id=1, source_target_pairs={{0,32},{32,0},{1,33},{33,1},{2,34},{34,2},{3,35},{35,3},{4,36},{36... | collective-permute-start | bytes 2752520 | tf_op jit(solution)/shard_map/ppermute | solution.py:19
  49.8 2.7 %collective-permute-start.7 = (bf16[128,3584]{1,0:T(8,128)(2,1)S(1)}, bf16[128,3584]{1,0:T(8,128)(2,1)S(1)}, u32[]{:S(2)}, u32[]{:S(2)}) collective-permute-start(bf16[128,3584]{1,0:T(8,128)(2,1)S(1)} %collective-permute-done.1.refs_2_), channel_id=1, source_target_pairs={{0,32},{32,0},{1,33},{33,1},{2,34},{34,2},{3,35},{35,3},{4,36},{36... | collective-permute-start | bytes 2752520 | tf_op jit(solution)/shard_map/ppermute | solution.py:19
  52.4 0.2 collective-permute-start.8
  52.6 0.0 collective-permute-done.10.refs_8_
  52.6 4.1 %collective-permute-start.14 = (bf16[64,3584]{1,0:T(8,128)(2,1)S(1)}, bf16[64,3584]{1,0:T(8,128)(2,1)S(1)}, u32[]{:S(2)}, u32[]{:S(2)}) collective-permute-start(bf16[64,3584]{1,0:T(8,128)(2,1)S(1)} %collective-permute-done.9.refs_6_), channel_id=1, source_target_pairs={{0,32},{32,0},{1,33},{33,1},{2,34},{34,2},{3,35},{35,3},{4,36},{36... | collective-permute-start | bytes 1376264 | tf_op jit(solution)/shard_map/ppermute | solution.py:19
  56.7 0.0 collective-permute-start.15
  56.7 0.0 copy-start
  56.7 0.1 assemble.1
  56.9 1.3 %collective-permute-done.14.refs_7_ = bf16[64,3584]{1,0:T(8,128)(2,1)S(1)} collective-permute-done((bf16[64,3584]{1,0:T(8,128)(2,1)S(1)}, bf16[64,3584]{1,0:T(8,128)(2,1)S(1)}, u32[]{:S(2)}, u32[]{:S(2)}) %collective-permute-start.14) | collective-permute-done | bytes 458784 | tf_op jit(solution)/shard_map/ppermute | solution.py:19
  58.2 0.7 collective-permute-done.15.refs_9_
  58.8 4.0 %student.1 = (f32[128,256]{1,0:T(8,128)S(1)}, f32[64,1,256]{2,1,0:T(1,128)}) custom-call(bf16[128,3584]{1,0:T(8,128)(2,1)S(1)} %copy-done.1, bf16[128,3584]{1,0:T(8,128)(2,1)S(1)} %collective-permute-done.refs_1_, bf16[128,3584]{1,0:T(8,128)(2,1)S(1)} %collective-permute-done.1.refs_2_, bf16[128,3584]{1,0:T(8,128)(2,1)S(1)} %collective-permute-done.7.refs_3_, ...), custom_call_target="tpu_custom_call" | custom-call | flops 2113929216 | bytes 8388608 | tf_op jit(solution)/shard_map/student/pallas_call | solution.py:196
  62.8 0.0 collective-permute-start.18
  62.8 1.7 %collective-permute-start.17 = (f32[128,256]{1,0:T(8,128)S(1)}, f32[128,256]{1,0:T(8,128)S(1)}, u32[]{:S(2)}, u32[]{:S(2)}) collective-permute-start(f32[128,256]{1,0:T(8,128)S(1)} %get-tuple-element.34), channel_id=1, source_target_pairs={{0,128},{64,192},{128,0},{192,64},{1,129},{65,193},{129,1},{193,65... | collective-permute-start | bytes 393224 | tf_op jit(solution)/shard_map/ppermute | solution.py:19
  64.5 1.0 %collective-permute-start.16 = (f32[128,256]{1,0:T(8,128)S(1)}, f32[128,256]{1,0:T(8,128)S(1)}, u32[]{:S(2)}, u32[]{:S(2)}) collective-permute-start(f32[128,256]{1,0:T(8,128)S(1)} %get-tuple-element.34), channel_id=1, source_target_pairs={{0,192},{64,0},{128,64},{192,128},{1,193},{65,1},{129,65},{193,129... | collective-permute-start | bytes 393224 | tf_op jit(solution)/shard_map/ppermute | solution.py:19
  65.5 12.5 %all-to-all-start.1 = ((f32[64,1,256]{2,1,0:T(1,128)}), f32[64,1,256]{2,1,0:T(1,128)S(1)}, u32[]{:S(2)}, u32[]{:S(2)}) async-start(f32[64,1,256]{2,1,0:T(1,128)} %get-tuple-element.35), calls=%async_computation.1 | async-start | bytes 131072 | tf_op jit(solution)/shard_map/all_to_all | solution.py:213
  78.0 12.0 %all-to-all-done.1.grads_ref = f32[64,1,256]{2,1,0:T(1,128)S(1)} async-done(((f32[64,1,256]{2,1,0:T(1,128)}), f32[64,1,256]{2,1,0:T(1,128)S(1)}, u32[]{:S(2)}, u32[]{:S(2)}) %all-to-all-start.1) | async-done | bytes 65568 | tf_op jit(solution)/shard_map/all_to_all | solution.py:213
  90.0 0.0 collective-permute-done.18
  90.0 0.0 collective-permute-done.17
  90.0 0.0 collective-permute-done.16
  90.1 0.5 collective-permute-start.19
  90.6 0.6 add.1
  91.3 0.9 collective-permute-done.19.other_ref
  92.2 1.1 %place.1 = f32[128,1792]{1,0:T(8,128)} custom-call(f32[512,256]{1,0:T(8,128)S(1)} %constant_dynamic-update-slice_fusion.mine_ref, f32[512,256]{1,0:T(8,128)S(1)} %collective-permute-done.19.other_ref), custom_call_target="tpu_custom_call" | custom-call | tf_op jit(solution)/shard_map/place/pallas_call | solution.py:217
  (17 shorter events, 0.1 us)
Async XLA Ops:
  0.6 0.9 copy-start.2
  2.3 12.8 %all-to-all-start = ((bf16[8,56,256]{2,1,0:T(8,128)(2,1)}), bf16[8,56,256]{2,1,0:T(8,128)(2,1)S(1)}, u32[]{:S(2)}, u32[]{:S(2)}) async-start(bf16[8,56,256]{2,1,0:T(8,128)(2,1)} %windows.1), calls=%async_computation | async-start | bytes 458752 | tf_op jit(solution)/shard_map/all_to_all | solution.py:168
  11.4 32.6 %copy-start.1 = (bf16[128,3584]{1,0:T(8,128)(2,1)S(1)}, bf16[128,3584]{1,0:T(8,128)(2,1)}, u32[]{:S(2)}) copy-start(bf16[128,3584]{1,0:T(8,128)(2,1)} %drive.1.refs_0_) | copy-start | bytes 2752516
  11.4 45.3 %copy-start.3 = (f32[1792]{0:T(1024)S(1)}, f32[1792]{0:T(1024)}, u32[]{:S(2)}) copy-start(f32[1792]{0:T(1024)} %param.7) | copy-start | bytes 21508
  15.0 21.1 %collective-permute-start.2 = (bf16[128,3584]{1,0:T(8,128)(2,1)}, bf16[128,3584]{1,0:T(8,128)(2,1)S(1)}, u32[]{:S(2)}, u32[]{:S(2)}) collective-permute-start(bf16[128,3584]{1,0:T(8,128)(2,1)} %drive.1.refs_0_), channel_id=1, source_target_pairs={{0,192},{64,0},{128,64},{192,128},{1,193},{65,1},{129,65},{193,129... | collective-permute-start | bytes 2752520 | tf_op jit(solution)/shard_map/ppermute | solution.py:19
  15.9 22.0 %collective-permute-start.1 = (bf16[128,3584]{1,0:T(8,128)(2,1)}, bf16[128,3584]{1,0:T(8,128)(2,1)S(1)}, u32[]{:S(2)}, u32[]{:S(2)}) collective-permute-start(bf16[128,3584]{1,0:T(8,128)(2,1)} %drive.1.refs_0_), channel_id=1, source_target_pairs={{0,64},{64,128},{128,192},{192,0},{1,65},{65,129},{129,193},{193,1... | collective-permute-start | bytes 2752520 | tf_op jit(solution)/shard_map/ppermute | solution.py:19
  16.5 6.8 %collective-permute-start.6 = (bf16[8,56,256]{2,1,0:T(8,128)(2,1)S(1)}, bf16[8,56,256]{2,1,0:T(8,128)(2,1)S(1)}, u32[]{:S(2)}, u32[]{:S(2)}) collective-permute-start(bf16[8,56,256]{2,1,0:T(8,128)(2,1)S(1)} %all-to-all-done.refs_0_), channel_id=1, source_target_pairs={{0,1},{1,2},{2,3},{3,0},{4,5},{5,6},{6,7},{7,4},{8,9},{9,10},{10,1... | collective-permute-start | bytes 688136 | tf_op jit(solution)/shard_map/ppermute | solution.py:19
  17.1 12.5 %collective-permute-start.5 = (bf16[8,56,256]{2,1,0:T(8,128)(2,1)S(1)}, bf16[8,56,256]{2,1,0:T(8,128)(2,1)S(1)}, u32[]{:S(2)}, u32[]{:S(2)}) collective-permute-start(bf16[8,56,256]{2,1,0:T(8,128)(2,1)S(1)} %all-to-all-done.refs_0_), channel_id=1, source_target_pairs={{0,2},{1,3},{2,0},{3,1},{4,6},{5,7},{6,4},{7,5},{8,10},{9,11},{10,... | collective-permute-start | bytes 688136 | tf_op jit(solution)/shard_map/ppermute | solution.py:19
  19.6 10.0 %collective-permute-start.4 = (bf16[8,56,256]{2,1,0:T(8,128)(2,1)S(1)}, bf16[8,56,256]{2,1,0:T(8,128)(2,1)S(1)}, u32[]{:S(2)}, u32[]{:S(2)}) collective-permute-start(bf16[8,56,256]{2,1,0:T(8,128)(2,1)S(1)} %all-to-all-done.refs_0_), channel_id=1, source_target_pairs={{0,3},{1,0},{2,1},{3,2},{4,7},{5,4},{6,5},{7,6},{8,11},{9,8},{10,9... | collective-permute-start | bytes 688136 | tf_op jit(solution)/shard_map/ppermute | solution.py:19
  23.2 9.8 %collective-permute-start.3 = (bf16[8,56,256]{2,1,0:T(8,128)(2,1)S(1)}, bf16[8,56,256]{2,1,0:T(8,128)(2,1)S(1)}, u32[]{:S(2)}, u32[]{:S(2)}) collective-permute-start(bf16[8,56,256]{2,1,0:T(8,128)(2,1)S(1)} %all-to-all-done.refs_0_), channel_id=1, source_target_pairs={{0,4},{4,0},{1,5},{5,1},{2,6},{6,2},{3,7},{7,3},{8,12},{12,8},{9,1... | collective-permute-start | bytes 688136 | tf_op jit(solution)/shard_map/ppermute | solution.py:19
  37.9 6.1 %collective-permute-start.13 = (bf16[8,56,256]{2,1,0:T(8,128)(2,1)S(1)}, bf16[8,56,256]{2,1,0:T(8,128)(2,1)S(1)}, u32[]{:S(2)}, u32[]{:S(2)}) collective-permute-start(bf16[8,56,256]{2,1,0:T(8,128)(2,1)S(1)} %collective-permute-done.3.refs_4_), channel_id=1, source_target_pairs={{0,1},{1,2},{2,3},{3,0},{4,5},{5,6},{6,7},{7,4},{8,9},{9,10},{10,1... | collective-permute-start | bytes 688136 | tf_op jit(solution)/shard_map/ppermute | solution.py:19
  38.5 11.3 %collective-permute-start.12 = (bf16[8,56,256]{2,1,0:T(8,128)(2,1)S(1)}, bf16[8,56,256]{2,1,0:T(8,128)(2,1)S(1)}, u32[]{:S(2)}, u32[]{:S(2)}) collective-permute-start(bf16[8,56,256]{2,1,0:T(8,128)(2,1)S(1)} %collective-permute-done.3.refs_4_), channel_id=1, source_target_pairs={{0,2},{1,3},{2,0},{3,1},{4,6},{5,7},{6,4},{7,5},{8,10},{9,11},{10,... | collective-permute-start | bytes 688136 | tf_op jit(solution)/shard_map/ppermute | solution.py:19
  41.0 11.5 %collective-permute-start.11 = (bf16[8,56,256]{2,1,0:T(8,128)(2,1)S(1)}, bf16[8,56,256]{2,1,0:T(8,128)(2,1)S(1)}, u32[]{:S(2)}, u32[]{:S(2)}) collective-permute-start(bf16[8,56,256]{2,1,0:T(8,128)(2,1)S(1)} %collective-permute-done.3.refs_4_), channel_id=1, source_target_pairs={{0,3},{1,0},{2,1},{3,2},{4,7},{5,4},{6,5},{7,6},{8,11},{9,8},{10,9... | collective-permute-start | bytes 688136 | tf_op jit(solution)/shard_map/ppermute | solution.py:19
  42.2 10.4 %collective-permute-start.10 = (bf16[64,3584]{1,0:T(8,128)(2,1)S(1)}, bf16[64,3584]{1,0:T(8,128)(2,1)S(1)}, u32[]{:S(2)}, u32[]{:S(2)}) collective-permute-start(bf16[64,3584]{1,0:T(8,128)(2,1)S(1)} %slice.7), channel_id=1, source_target_pairs={{0,192},{64,0},{128,64},{192,128},{1,193},{65,1},{129,65},{193,129... | collective-permute-start | bytes 1376264 | tf_op jit(solution)/shard_map/ppermute | solution.py:19
  42.6 10.1 %collective-permute-start.9 = (bf16[64,3584]{1,0:T(8,128)(2,1)S(1)}, bf16[64,3584]{1,0:T(8,128)(2,1)S(1)}, u32[]{:S(2)}, u32[]{:S(2)}) collective-permute-start(bf16[64,3584]{1,0:T(8,128)(2,1)S(1)} %slice.6), channel_id=1, source_target_pairs={{0,64},{64,128},{128,192},{192,0},{1,65},{65,129},{129,193},{193,1... | collective-permute-start | bytes 1376264 | tf_op jit(solution)/shard_map/ppermute | solution.py:19
  44.0 12.9 %collective-permute-start = (bf16[128,3584]{1,0:T(8,128)(2,1)S(1)}, bf16[128,3584]{1,0:T(8,128)(2,1)S(1)}, u32[]{:S(2)}, u32[]{:S(2)}) collective-permute-start(bf16[128,3584]{1,0:T(8,128)(2,1)S(1)} %copy-done.1), channel_id=1, source_target_pairs={{0,32},{32,0},{1,33},{33,1},{2,34},{34,2},{3,35},{35,3},{4,36},{36... | collective-permute-start | bytes 2752520 | tf_op jit(solution)/shard_map/ppermute | solution.py:19
  49.8 9.0 %collective-permute-start.7 = (bf16[128,3584]{1,0:T(8,128)(2,1)S(1)}, bf16[128,3584]{1,0:T(8,128)(2,1)S(1)}, u32[]{:S(2)}, u32[]{:S(2)}) collective-permute-start(bf16[128,3584]{1,0:T(8,128)(2,1)S(1)} %collective-permute-done.1.refs_2_), channel_id=1, source_target_pairs={{0,32},{32,0},{1,33},{33,1},{2,34},{34,2},{3,35},{35,3},{4,36},{36... | collective-permute-start | bytes 2752520 | tf_op jit(solution)/shard_map/ppermute | solution.py:19
  52.4 6.4 %collective-permute-start.8 = (bf16[128,3584]{1,0:T(8,128)(2,1)S(1)}, bf16[128,3584]{1,0:T(8,128)(2,1)S(1)}, u32[]{:S(2)}, u32[]{:S(2)}) collective-permute-start(bf16[128,3584]{1,0:T(8,128)(2,1)S(1)} %collective-permute-done.2.refs_4_), channel_id=1, source_target_pairs={{0,32},{32,0},{1,33},{33,1},{2,34},{34,2},{3,35},{35,3},{4,36},{36... | collective-permute-start | bytes 2752520 | tf_op jit(solution)/shard_map/ppermute | solution.py:19
  52.6 5.5 %collective-permute-start.14 = (bf16[64,3584]{1,0:T(8,128)(2,1)S(1)}, bf16[64,3584]{1,0:T(8,128)(2,1)S(1)}, u32[]{:S(2)}, u32[]{:S(2)}) collective-permute-start(bf16[64,3584]{1,0:T(8,128)(2,1)S(1)} %collective-permute-done.9.refs_6_), channel_id=1, source_target_pairs={{0,32},{32,0},{1,33},{33,1},{2,34},{34,2},{3,35},{35,3},{4,36},{36... | collective-permute-start | bytes 1376264 | tf_op jit(solution)/shard_map/ppermute | solution.py:19
  56.7 2.1 %collective-permute-start.15 = (bf16[64,3584]{1,0:T(8,128)(2,1)S(1)}, bf16[64,3584]{1,0:T(8,128)(2,1)S(1)}, u32[]{:S(2)}, u32[]{:S(2)}) collective-permute-start(bf16[64,3584]{1,0:T(8,128)(2,1)S(1)} %collective-permute-done.10.refs_8_), channel_id=1, source_target_pairs={{0,32},{32,0},{1,33},{33,1},{2,34},{34,2},{3,35},{35,3},{4,36},{36... | collective-permute-start | bytes 1376264 | tf_op jit(solution)/shard_map/ppermute | solution.py:19
  56.7 2.1 %copy-start = (bf16[128,3584]{1,0:T(8,128)(2,1)S(1)}, bf16[128,3584]{1,0:T(8,128)(2,1)}, u32[]{:S(2)}) copy-start(bf16[128,3584]{1,0:T(8,128)(2,1)} %refs_10_.1) | copy-start | bytes 2752516
  62.8 27.2 %collective-permute-start.18 = (f32[128,256]{1,0:T(8,128)S(1)}, f32[128,256]{1,0:T(8,128)S(1)}, u32[]{:S(2)}, u32[]{:S(2)}) collective-permute-start(f32[128,256]{1,0:T(8,128)S(1)} %get-tuple-element.34), channel_id=1, source_target_pairs={{0,64},{64,128},{128,192},{192,0},{1,65},{65,129},{129,193},{193,1... | collective-permute-start | bytes 393224 | tf_op jit(solution)/shard_map/ppermute | solution.py:19
  62.8 27.2 %collective-permute-start.17 = (f32[128,256]{1,0:T(8,128)S(1)}, f32[128,256]{1,0:T(8,128)S(1)}, u32[]{:S(2)}, u32[]{:S(2)}) collective-permute-start(f32[128,256]{1,0:T(8,128)S(1)} %get-tuple-element.34), channel_id=1, source_target_pairs={{0,128},{64,192},{128,0},{192,64},{1,129},{65,193},{129,1},{193,65... | collective-permute-start | bytes 393224 | tf_op jit(solution)/shard_map/ppermute | solution.py:19
  64.5 25.5 %collective-permute-start.16 = (f32[128,256]{1,0:T(8,128)S(1)}, f32[128,256]{1,0:T(8,128)S(1)}, u32[]{:S(2)}, u32[]{:S(2)}) collective-permute-start(f32[128,256]{1,0:T(8,128)S(1)} %get-tuple-element.34), channel_id=1, source_target_pairs={{0,192},{64,0},{128,64},{192,128},{1,193},{65,1},{129,65},{193,129... | collective-permute-start | bytes 393224 | tf_op jit(solution)/shard_map/ppermute | solution.py:19
  65.5 24.5 %all-to-all-start.1 = ((f32[64,1,256]{2,1,0:T(1,128)}), f32[64,1,256]{2,1,0:T(1,128)S(1)}, u32[]{:S(2)}, u32[]{:S(2)}) async-start(f32[64,1,256]{2,1,0:T(1,128)} %get-tuple-element.35), calls=%async_computation.1 | async-start | bytes 131072 | tf_op jit(solution)/shard_map/all_to_all | solution.py:213
  90.1 2.1 %collective-permute-start.19 = (f32[512,256]{1,0:T(8,128)S(1)}, f32[512,256]{1,0:T(8,128)S(1)}, u32[]{:S(2)}, u32[]{:S(2)}) collective-permute-start(f32[512,256]{1,0:T(8,128)S(1)} %constant_dynamic-update-slice_fusion.mine_ref), channel_id=1, source_target_pairs={{0,32},{32,0},{1,33},{33,1},{2,34},{34,2},{3,35},{35,3},{4,36},{36... | collective-permute-start | bytes 1572872 | tf_op jit(solution)/shard_map/ppermute | solution.py:19

commit v5 on v4

--- a/solution.py
+++ b/solution.py
@@ -12,6 +12,7 @@
 Y, CORE, Z, X = 4, 2, 2, 4
 STEPS = Y * CORE
 MIB = 1024 * 1024
+GROUPS = ((0, 24), (24, 48), (48, 64))
 
 
 def around(x, axis, by):
@@ -76,7 +77,7 @@
         at += tall
     current_ref[STEPS] = total[at:]
     threshold = threshold_ref[:, pl.ds(start_of(y, core), WIDE)]
-    tall = 64
+    tall = GROUPS[-1][1]
 
     def strip(i, grad_sum):
         at = pl.ds(pl.multiple_of(i * tall, tall), tall)
@@ -102,33 +103,34 @@
         return grad_sum
 
     grad_sum = lax.fori_loop(0, rows // tall, strip, jnp.zeros((tall, WIDE), jnp.float32))
-    grad_ref[...] = jnp.broadcast_to(jnp.sum(grad_sum, axis=0, keepdims=True)[None], grad_ref.shape)
-
-
-def place_kernel(mine_ref, other_ref, out_ref):
-    rows = out_ref.shape[0]
+    for i, (first, last) in enumerate(GROUPS):
+        part = jnp.sum(grad_sum[first:last], axis=0, keepdims=True)
+        grad_ref[:, :, i * WIDE : (i + 1) * WIDE] = jnp.broadcast_to(part[None], (grad_ref.shape[0], 1, WIDE))
+
+
+def finish_kernel(*refs):
+    grads_ref, rates_ref, grad_ref = refs[-3:]
     core, y = lax.axis_index("core"), lax.axis_index("y")
     for j in range(Y):
-        for k, piece in enumerate((mine_ref, other_ref)):
+        for k in range(CORE):
+            piece = refs[Y * k + j]
             from_y, from_core = (y + j) % Y, (core + k) % CORE
             start = start_of(from_y, from_core)
-            at = slice(j * rows, (j + 1) * rows)
 
             @pl.when((from_core == 0) | (from_y % 2 == 1))
             def _():
-                out_ref[:, pl.ds(start, WIDE)] = piece[at, :]
+                rates_ref[:, pl.ds(start, WIDE)] = piece[...]
 
             @pl.when((from_core == 1) & (from_y % 2 == 0))
             def _():
-                out_ref[:, pl.ds(pl.multiple_of(start + 128, 128), WIDE - 128)] = piece[at, 128:]
-
-
-def add_kernel(grads_ref, out_ref):
+                rates_ref[:, pl.ds(pl.multiple_of(start + 128, 128), WIDE - 128)] = piece[:, 128:]
+
     count = grads_ref.shape[0] // STEPS
     for w, s in enumerate(STARTS):
         total = jnp.sum(grads_ref[w * count : (w + 1) * count], axis=0)
+        total = sum(total[:, i : i + WIDE] for i in range(0, total.shape[1], WIDE))
         skip = 128 if w % 4 == 1 else 0
-        out_ref[s + skip : s + WIDE] = total[0, skip:]
+        grad_ref[s + skip : s + WIDE] = total[0, skip:]
 
 
 def on_device(features, spike_mask, gate_weight, threshold):
@@ -170,10 +172,12 @@
     s_p, s_m = around(own, "y", 1), around(own, "y", -1)
     near_x = along_x(near_w)
     far_w = around(near_w, "z", 1)
-    s_p, s_m, far_w, *near_x = lax.optimization_barrier((s_p, s_m, far_w, *near_x))
+    n_1, n_2, n_3 = near_x
+    far_w, n_1, n_3 = lax.optimization_barrier((far_w, n_1, n_3))
     s_f0, s_f1 = around(s_p[:half], "y", 1), around(s_m[half:], "y", -1)
     far_x = along_x(far_w)
-    s_f0, s_f1, *far_x = lax.optimization_barrier((s_f0, s_f1, *far_x))
+    s_f0, s_f1, n_2, *far_x = lax.optimization_barrier((s_f0, s_f1, n_2, *far_x))
+    near_x = (n_1, n_2, n_3)
     o_own, o_p, o_m = (around(v, "core", 1) for v in (own, s_p, s_m))
     o_f0, o_f1 = around(s_f0, "core", 1), around(s_f1, "core", 1)
     steps, spans = [], []
@@ -197,7 +201,7 @@
         functools.partial(student_kernel, tokens_all=tokens_all, spans=spans),
         out_shape=(
             jax.ShapeDtypeStruct((rows, WIDE), jnp.float32),
-            jax.ShapeDtypeStruct((peers, 1, WIDE), jnp.float32),
+            jax.ShapeDtypeStruct((peers, 1, len(GROUPS) * WIDE), jnp.float32),
         ),
         in_specs=[vmem] * (len(steps) + 3),
         out_specs=(vmem, vmem),
@@ -211,29 +215,19 @@
 
     rates_y = [around(rates, "y", -1), around(rates, "y", 2), around(rates, "y", 1)]
     grads = lax.all_to_all(grad, ("y", "core", "z", "x"), 0, 0, tiled=True)
-    *rates_y, grads = lax.optimization_barrier((*rates_y, grads))
-    mine = jnp.concatenate([rates] + rates_y)
-    other = around(mine, "core", 1)
-    rates_out = pl.pallas_call(
-        place_kernel,
-        out_shape=jax.ShapeDtypeStruct((rows, width), jnp.float32),
-        in_specs=[vmem] * 2,
-        out_specs=vmem,
-        compiler_params=pltpu.CompilerParams(vmem_limit_bytes=4 * MIB),
-        cost_estimate=pl.CostEstimate(flops=0, bytes_accessed=0, transcendentals=0),
-        name="place",
-    )(mine, other)
-
-
-    grad_out = pl.pallas_call(
-        add_kernel,
-        out_shape=jax.ShapeDtypeStruct((width,), jnp.float32),
-        in_specs=[vmem],
-        out_specs=vmem,
-        compiler_params=pltpu.CompilerParams(vmem_limit_bytes=4 * MIB),
-        name="add",
-    )(grads)
-    return rates_out, grad_out
+    pieces = [rates] + rates_y
+    other = [around(v, "core", 1) for v in pieces]
+    return pl.pallas_call(
+        finish_kernel,
+        out_shape=(
+            jax.ShapeDtypeStruct((rows, width), jnp.float32),
+            jax.ShapeDtypeStruct((width,), jnp.float32),
+        ),
+        in_specs=[vmem] * (2 * Y + 1),
+        out_specs=(vmem, vmem),
+        compiler_params=pltpu.CompilerParams(vmem_limit_bytes=6 * MIB),
+        name="finish",
+    )(*pieces, *other, grads)
 
 
 def solution(mesh):

time: 93.6 us -> 86.1 us (0.920)
  waiting for transfers between devices: 29.5 us -> 22.2 us
    all_to_all x1, waiting for transfers between devices: 12 us -> 0.01 us  [on_device(): grads = lax.all_to_all(grad, ('y', 'core', 'z', 'x'), 0, 0, tiled=True)]
    ppermute x20 -> x23, waiting for transfers between devices: 13.9 us -> 18.6 us  [around(): return lax.ppermute(x, axis, [(i, (i + by) % n) for i in range(n)])]
    ppermute x20 -> x23, starting transfers between devices: 33.7 us -> 36.9 us  [around(): return lax.ppermute(x, axis, [(i, (i + by) % n) for i in range(n)])]
    all_to_all x1, starting transfers between devices: 12.5 us -> 9.66 us  [on_device(): grads = lax.all_to_all(grad, ('y', 'core', 'z', 'x'), 0, 0, tiled=True)]
  transfers between devices with their start and end apart: 22 -> 25, of which waited for: 10 -> 11; matrix products, arithmetic and copies ran while one was open for 0% -> 0% of each run, Pallas kernels for 4% -> 3%
where the time goes in v5:
time: 86.1 us; the launch traced here: 85.8 us
  starting transfers between devices  53.1 us (62%)
  waiting for transfers between devices  22.2 us (26%)
  Pallas kernels  8.68 us (10%)
  local copies, waits for them, and re-layouts  1.01 us (1%)
    ppermute x23, starting transfers between devices, around(): return lax.ppermute(x, axis, [(i, (i + by) % n) for i in range(n)])  36.9 us
    ppermute x23, waiting for transfers between devices, around(): return lax.ppermute(x, axis, [(i, (i + by) % n) for i in range(n)])  18.6 us
    all_to_all x1, starting transfers between devices, on_device(): grads = lax.all_to_all(grad, ('y', 'core', 'z', 'x'), 0, 0, tiled=True)  9.66 us
    all_to_all x1, starting transfers between devices, on_device(): near_w = lax.all_to_all(payload, ('y', 'core'), 0, 0, tiled=True)  6.54 us
    pallas_call x1, Pallas kernels, on_device(): pl.pallas_call(functools.partial(student_kernel, tokens_all=tokens_all, s...  4.06 us
    all_to_all x1, waiting for transfers between devices, on_device(): near_w = lax.all_to_all(payload, ('y', 'core'), 0, 0, tiled=True)  3.6 us
    pallas_call x1, Pallas kernels, on_device(): pl.pallas_call(drive_kernel, out_shape=jax.ShapeDtypeStruct((rows, deep),...  2.58 us
  transfers between devices with their start and end apart: 25, of which 11 were waited for; matrix products, arithmetic and copies ran while one was open for 0% of the time, Pallas kernels for 3%

profile of v5, /device:TPU:1, one launch (start us, length us, event | category | flops | bytes accessed | tf_op | source)
XLA Modules:
  0.0 85.8 jit_solution(4914328020088289454)
XLA Ops:
  0.6 0.9 %copy-done.2 = bf16[56,1792]{1,0:T(8,128)(2,1)S(1)} copy-done((bf16[56,1792]{1,0:T(8,128)(2,1)S(1)}, bf16[56,1792]{1,0:T(8,128)(2,1)}, u32[]{:S(2)}) %copy-start.2) | copy-done | bytes 200728
  1.6 0.7 windows.1
  2.3 6.5 %all-to-all-start = ((bf16[8,56,256]{2,1,0:T(8,128)(2,1)}), bf16[8,56,256]{2,1,0:T(8,128)(2,1)S(1)}, u32[]{:S(2)}, u32[]{:S(2)}) async-start(bf16[8,56,256]{2,1,0:T(8,128)(2,1)} %windows.1), calls=%async_computation | async-start | bytes 458752 | tf_op jit(solution)/shard_map/all_to_all | solution.py:170
  8.8 2.6 %drive.1.refs_0_ = bf16[128,3584]{1,0:T(8,128)(2,1)} custom-call(s32[1,128,3584]{2,1,0:T(8,128)} %mask_hbm.1, bf16[128,3584]{1,0:T(8,128)(2,1)} %refs_10_.1), custom_call_target="tpu_custom_call" | custom-call | tf_op jit(solution)/shard_map/drive/pallas_call | solution.py:147
  11.4 0.0 copy-start.1
  11.4 0.0 copy-start.3
  11.4 3.6 %all-to-all-done.refs_0_ = bf16[8,56,256]{2,1,0:T(8,128)(2,1)S(1)} async-done(((bf16[8,56,256]{2,1,0:T(8,128)(2,1)}), bf16[8,56,256]{2,1,0:T(8,128)(2,1)S(1)}, u32[]{:S(2)}, u32[]{:S(2)}) %all-to-all-start) | async-done | bytes 229408 | tf_op jit(solution)/shard_map/all_to_all | solution.py:170
  15.0 0.9 %collective-permute-start.3 = (bf16[128,3584]{1,0:T(8,128)(2,1)}, bf16[128,3584]{1,0:T(8,128)(2,1)S(1)}, u32[]{:S(2)}, u32[]{:S(2)}) collective-permute-start(bf16[128,3584]{1,0:T(8,128)(2,1)} %drive.1.refs_0_), channel_id=1, source_target_pairs={{0,192},{64,0},{128,64},{192,128},{1,193},{65,1},{129,65},{193,129... | collective-permute-start | bytes 2752520 | tf_op jit(solution)/shard_map/ppermute | solution.py:20
  15.9 0.6 collective-permute-start.1
  16.5 0.6 collective-permute-start.10
  17.1 2.1 %collective-permute-start.9 = (bf16[8,56,256]{2,1,0:T(8,128)(2,1)S(1)}, bf16[8,56,256]{2,1,0:T(8,128)(2,1)S(1)}, u32[]{:S(2)}, u32[]{:S(2)}) collective-permute-start(bf16[8,56,256]{2,1,0:T(8,128)(2,1)S(1)} %all-to-all-done.refs_0_), channel_id=1, source_target_pairs={{0,3},{1,0},{2,1},{3,2},{4,7},{5,4},{6,5},{7,6},{8,11},{9,8},{10,9... | collective-permute-start | bytes 688136 | tf_op jit(solution)/shard_map/ppermute | solution.py:20
  19.2 6.3 %collective-permute-start.8 = (bf16[8,56,256]{2,1,0:T(8,128)(2,1)S(1)}, bf16[8,56,256]{2,1,0:T(8,128)(2,1)S(1)}, u32[]{:S(2)}, u32[]{:S(2)}) collective-permute-start(bf16[8,56,256]{2,1,0:T(8,128)(2,1)S(1)} %all-to-all-done.refs_0_), channel_id=1, source_target_pairs={{0,4},{4,0},{1,5},{5,1},{2,6},{6,2},{3,7},{7,3},{8,12},{12,8},{9,1... | collective-permute-start | bytes 688136 | tf_op jit(solution)/shard_map/ppermute | solution.py:20
  25.5 1.5 %collective-permute-start.7 = (bf16[8,56,256]{2,1,0:T(8,128)(2,1)S(1)}, bf16[8,56,256]{2,1,0:T(8,128)(2,1)S(1)}, u32[]{:S(2)}, u32[]{:S(2)}) collective-permute-start(bf16[8,56,256]{2,1,0:T(8,128)(2,1)S(1)} %all-to-all-done.refs_0_), channel_id=1, source_target_pairs={{0,2},{1,3},{2,0},{3,1},{4,6},{5,7},{6,4},{7,5},{8,10},{9,11},{10,... | collective-permute-start | bytes 688136 | tf_op jit(solution)/shard_map/ppermute | solution.py:20
  27.0 0.0 collective-permute-done.9.refs_1_
  27.0 2.3 %collective-permute-done.8.refs_4_ = bf16[8,56,256]{2,1,0:T(8,128)(2,1)S(1)} collective-permute-done((bf16[8,56,256]{2,1,0:T(8,128)(2,1)S(1)}, bf16[8,56,256]{2,1,0:T(8,128)(2,1)S(1)}, u32[]{:S(2)}, u32[]{:S(2)}) %collective-permute-start.8) | collective-permute-done | bytes 229408 | tf_op jit(solution)/shard_map/ppermute | solution.py:20
  29.3 0.0 collective-permute-start.13
  29.3 2.4 %collective-permute-start.12 = (bf16[8,56,256]{2,1,0:T(8,128)(2,1)S(1)}, bf16[8,56,256]{2,1,0:T(8,128)(2,1)S(1)}, u32[]{:S(2)}, u32[]{:S(2)}) collective-permute-start(bf16[8,56,256]{2,1,0:T(8,128)(2,1)S(1)} %collective-permute-done.8.refs_4_), channel_id=1, source_target_pairs={{0,2},{1,3},{2,0},{3,1},{4,6},{5,7},{6,4},{7,5},{8,10},{9,11},{10,... | collective-permute-start | bytes 688136 | tf_op jit(solution)/shard_map/ppermute | solution.py:20
  31.7 4.4 %collective-permute-done.3.refs_4_ = bf16[128,3584]{1,0:T(8,128)(2,1)S(1)} collective-permute-done((bf16[128,3584]{1,0:T(8,128)(2,1)}, bf16[128,3584]{1,0:T(8,128)(2,1)S(1)}, u32[]{:S(2)}, u32[]{:S(2)}) %collective-permute-start.3) | collective-permute-done | bytes 917536 | tf_op jit(solution)/shard_map/ppermute | solution.py:20
  36.1 1.9 %collective-permute-start.11 = (bf16[8,56,256]{2,1,0:T(8,128)(2,1)S(1)}, bf16[8,56,256]{2,1,0:T(8,128)(2,1)S(1)}, u32[]{:S(2)}, u32[]{:S(2)}) collective-permute-start(bf16[8,56,256]{2,1,0:T(8,128)(2,1)S(1)} %collective-permute-done.8.refs_4_), channel_id=1, source_target_pairs={{0,3},{1,0},{2,1},{3,2},{4,7},{5,4},{6,5},{7,6},{8,11},{9,8},{10,9... | collective-permute-start | bytes 688136 | tf_op jit(solution)/shard_map/ppermute | solution.py:20
  38.0 0.0 collective-permute-done.1.refs_2_
  38.0 2.2 %collective-permute-start.6 = (bf16[64,3584]{1,0:T(8,128)(2,1)S(1)}, bf16[64,3584]{1,0:T(8,128)(2,1)S(1)}, u32[]{:S(2)}, u32[]{:S(2)}) collective-permute-start(bf16[64,3584]{1,0:T(8,128)(2,1)S(1)} %slice.9), channel_id=1, source_target_pairs={{0,192},{64,0},{128,64},{192,128},{1,193},{65,1},{129,65},{193,129... | collective-permute-start | bytes 1376264 | tf_op jit(solution)/shard_map/ppermute | solution.py:20
  40.2 0.0 collective-permute-done.7.refs_2_
  40.2 0.1 collective-permute-start.5
  40.3 5.1 %collective-permute-start = (bf16[128,3584]{1,0:T(8,128)(2,1)S(1)}, bf16[128,3584]{1,0:T(8,128)(2,1)S(1)}, u32[]{:S(2)}, u32[]{:S(2)}) collective-permute-start(bf16[128,3584]{1,0:T(8,128)(2,1)S(1)} %copy-done.1), channel_id=1, source_target_pairs={{0,32},{32,0},{1,33},{33,1},{2,34},{34,2},{3,35},{35,3},{4,36},{36... | collective-permute-start | bytes 2752520 | tf_op jit(solution)/shard_map/ppermute | solution.py:20
  45.4 0.1 collective-permute-start.4
  45.5 1.1 %collective-permute-start.2 = (bf16[128,3584]{1,0:T(8,128)(2,1)S(1)}, bf16[128,3584]{1,0:T(8,128)(2,1)S(1)}, u32[]{:S(2)}, u32[]{:S(2)}) collective-permute-start(bf16[128,3584]{1,0:T(8,128)(2,1)S(1)} %collective-permute-done.1.refs_2_), channel_id=1, source_target_pairs={{0,32},{32,0},{1,33},{33,1},{2,34},{34,2},{3,35},{35,3},{4,36},{36... | collective-permute-start | bytes 2752520 | tf_op jit(solution)/shard_map/ppermute | solution.py:20
  46.6 1.3 %collective-permute-done.6.refs_8_ = bf16[64,3584]{1,0:T(8,128)(2,1)S(1)} collective-permute-done((bf16[64,3584]{1,0:T(8,128)(2,1)S(1)}, bf16[64,3584]{1,0:T(8,128)(2,1)S(1)}, u32[]{:S(2)}, u32[]{:S(2)}) %collective-permute-start.6) | collective-permute-done | bytes 458784 | tf_op jit(solution)/shard_map/ppermute | solution.py:20
  47.9 3.2 %collective-permute-done.5.refs_6_ = bf16[64,3584]{1,0:T(8,128)(2,1)S(1)} collective-permute-done((bf16[64,3584]{1,0:T(8,128)(2,1)S(1)}, bf16[64,3584]{1,0:T(8,128)(2,1)S(1)}, u32[]{:S(2)}, u32[]{:S(2)}) %collective-permute-start.5) | collective-permute-done | bytes 458784 | tf_op jit(solution)/shard_map/ppermute | solution.py:20
  51.1 3.4 %collective-permute-start.14 = (bf16[64,3584]{1,0:T(8,128)(2,1)S(1)}, bf16[64,3584]{1,0:T(8,128)(2,1)S(1)}, u32[]{:S(2)}, u32[]{:S(2)}) collective-permute-start(bf16[64,3584]{1,0:T(8,128)(2,1)S(1)} %collective-permute-done.5.refs_6_), channel_id=1, source_target_pairs={{0,32},{32,0},{1,33},{33,1},{2,34},{34,2},{3,35},{35,3},{4,36},{36... | collective-permute-start | bytes 1376264 | tf_op jit(solution)/shard_map/ppermute | solution.py:20
  54.5 0.0 collective-permute-start.15
  54.5 0.0 copy-start
  54.5 0.1 assemble.1
  54.7 1.2 %collective-permute-done.14.refs_7_ = bf16[64,3584]{1,0:T(8,128)(2,1)S(1)} collective-permute-done((bf16[64,3584]{1,0:T(8,128)(2,1)S(1)}, bf16[64,3584]{1,0:T(8,128)(2,1)S(1)}, u32[]{:S(2)}, u32[]{:S(2)}) %collective-permute-start.14) | collective-permute-done | bytes 458784 | tf_op jit(solution)/shard_map/ppermute | solution.py:20
  55.9 0.7 collective-permute-done.15.refs_9_
  56.6 4.1 %student.1 = (f32[128,256]{1,0:T(8,128)S(1)}, f32[64,1,768]{2,1,0:T(1,128)}) custom-call(bf16[128,3584]{1,0:T(8,128)(2,1)S(1)} %copy-done.1, bf16[128,3584]{1,0:T(8,128)(2,1)S(1)} %collective-permute-done.refs_1_, bf16[128,3584]{1,0:T(8,128)(2,1)S(1)} %collective-permute-done.1.refs_2_, bf16[128,3584]{1,0:T(8,128)(2,1)S(1)} %collective-permute-done.2.refs_3_, ...), custom_call_target="tpu_custom_call" | custom-call | flops 2113929216 | bytes 8388608 | tf_op jit(solution)/shard_map/student/pallas_call | solution.py:200
  60.6 9.7 %all-to-all-start.1 = ((f32[64,1,768]{2,1,0:T(1,128)}), f32[64,1,768]{2,1,0:T(1,128)S(1)}, u32[]{:S(2)}, u32[]{:S(2)}) async-start(f32[64,1,768]{2,1,0:T(1,128)} %get-tuple-element.27), calls=%async_computation.1 | async-start | bytes 393216 | tf_op jit(solution)/shard_map/all_to_all | solution.py:217
  70.3 1.5 %collective-permute-start.18 = (f32[128,256]{1,0:T(8,128)S(1)}, f32[128,256]{1,0:T(8,128)S(1)}, u32[]{:S(2)}, u32[]{:S(2)}) collective-permute-start(f32[128,256]{1,0:T(8,128)S(1)} %get-tuple-element.26.refs_0_), channel_id=1, source_target_pairs={{0,64},{64,128},{128,192},{192,0},{1,65},{65,129},{129,193},{193,1... | collective-permute-start | bytes 393224 | tf_op jit(solution)/shard_map/ppermute | solution.py:20
  71.8 2.6 %collective-permute-start.17 = (f32[128,256]{1,0:T(8,128)S(1)}, f32[128,256]{1,0:T(8,128)S(1)}, u32[]{:S(2)}, u32[]{:S(2)}) collective-permute-start(f32[128,256]{1,0:T(8,128)S(1)} %get-tuple-element.26.refs_0_), channel_id=1, source_target_pairs={{0,128},{64,192},{128,0},{192,64},{1,129},{65,193},{129,1},{193,65... | collective-permute-start | bytes 393224 | tf_op jit(solution)/shard_map/ppermute | solution.py:20
  74.4 1.1 %collective-permute-start.16 = (f32[128,256]{1,0:T(8,128)S(1)}, f32[128,256]{1,0:T(8,128)S(1)}, u32[]{:S(2)}, u32[]{:S(2)}) collective-permute-start(f32[128,256]{1,0:T(8,128)S(1)} %get-tuple-element.26.refs_0_), channel_id=1, source_target_pairs={{0,192},{64,0},{128,64},{192,128},{1,193},{65,1},{129,65},{193,129... | collective-permute-start | bytes 393224 | tf_op jit(solution)/shard_map/ppermute | solution.py:20
  75.4 1.2 %collective-permute-start.19 = (f32[128,256]{1,0:T(8,128)S(1)}, f32[128,256]{1,0:T(8,128)S(1)}, u32[]{:S(2)}, u32[]{:S(2)}) collective-permute-start(f32[128,256]{1,0:T(8,128)S(1)} %get-tuple-element.26.refs_0_), channel_id=1, source_target_pairs={{0,32},{32,0},{1,33},{33,1},{2,34},{34,2},{3,35},{35,3},{4,36},{36... | collective-permute-start | bytes 393224 | tf_op jit(solution)/shard_map/ppermute | solution.py:20
  76.6 1.1 %collective-permute-done.18.refs_3_ = f32[128,256]{1,0:T(8,128)S(1)} collective-permute-done((f32[128,256]{1,0:T(8,128)S(1)}, f32[128,256]{1,0:T(8,128)S(1)}, u32[]{:S(2)}, u32[]{:S(2)}) %collective-permute-start.18) | collective-permute-done | bytes 131104 | tf_op jit(solution)/shard_map/ppermute | solution.py:20
  77.7 0.9 %collective-permute-start.22 = (f32[128,256]{1,0:T(8,128)S(1)}, f32[128,256]{1,0:T(8,128)S(1)}, u32[]{:S(2)}, u32[]{:S(2)}) collective-permute-start(f32[128,256]{1,0:T(8,128)S(1)} %collective-permute-done.18.refs_3_), channel_id=1, source_target_pairs={{0,32},{32,0},{1,33},{33,1},{2,34},{34,2},{3,35},{35,3},{4,36},{36... | collective-permute-start | bytes 393224 | tf_op jit(solution)/shard_map/ppermute | solution.py:20
  78.6 3.2 %collective-permute-done.17.refs_2_ = f32[128,256]{1,0:T(8,128)S(1)} collective-permute-done((f32[128,256]{1,0:T(8,128)S(1)}, f32[128,256]{1,0:T(8,128)S(1)}, u32[]{:S(2)}, u32[]{:S(2)}) %collective-permute-start.17) | collective-permute-done | bytes 131104 | tf_op jit(solution)/shard_map/ppermute | solution.py:20
  81.8 1.4 %collective-permute-start.21 = (f32[128,256]{1,0:T(8,128)S(1)}, f32[128,256]{1,0:T(8,128)S(1)}, u32[]{:S(2)}, u32[]{:S(2)}) collective-permute-start(f32[128,256]{1,0:T(8,128)S(1)} %collective-permute-done.17.refs_2_), channel_id=1, source_target_pairs={{0,32},{32,0},{1,33},{33,1},{2,34},{34,2},{3,35},{35,3},{4,36},{36... | collective-permute-start | bytes 393224 | tf_op jit(solution)/shard_map/ppermute | solution.py:20
  83.2 0.0 collective-permute-start.20
  83.2 1.0 %collective-permute-done.21.refs_6_ = f32[128,256]{1,0:T(8,128)S(1)} collective-permute-done((f32[128,256]{1,0:T(8,128)S(1)}, f32[128,256]{1,0:T(8,128)S(1)}, u32[]{:S(2)}, u32[]{:S(2)}) %collective-permute-start.21) | collective-permute-done | bytes 131104 | tf_op jit(solution)/shard_map/ppermute | solution.py:20
  84.2 0.4 collective-permute-done.20.refs_5_
  84.6 1.2 %finish.1 = (f32[128,1792]{1,0:T(8,128)}, f32[1792]{0:T(1024)}) custom-call(f32[128,256]{1,0:T(8,128)S(1)} %get-tuple-element.26.refs_0_, f32[128,256]{1,0:T(8,128)S(1)} %collective-permute-done.16.refs_1_, f32[128,256]{1,0:T(8,128)S(1)} %collective-permute-done.17.refs_2_, f32[128,256]{1,0:T(8,128)S(1)} %collective-permute-done.18.refs_3_, ...), custom_call_target="tpu_custom_call" | custom-call | tf_op jit(solution)/shard_map/finish/pallas_call | solution.py:220
  (18 shorter events, 0.1 us)
Async XLA Ops:
  0.6 0.9 %copy-start.2 = (bf16[56,1792]{1,0:T(8,128)(2,1)S(1)}, bf16[56,1792]{1,0:T(8,128)(2,1)}, u32[]{:S(2)}) copy-start(bf16[56,1792]{1,0:T(8,128)(2,1)} %weight_ref.1) | copy-start | bytes 602116
  2.3 12.8 %all-to-all-start = ((bf16[8,56,256]{2,1,0:T(8,128)(2,1)}), bf16[8,56,256]{2,1,0:T(8,128)(2,1)S(1)}, u32[]{:S(2)}, u32[]{:S(2)}) async-start(bf16[8,56,256]{2,1,0:T(8,128)(2,1)} %windows.1), calls=%async_computation | async-start | bytes 458752 | tf_op jit(solution)/shard_map/all_to_all | solution.py:170
  11.4 28.9 %copy-start.1 = (bf16[128,3584]{1,0:T(8,128)(2,1)S(1)}, bf16[128,3584]{1,0:T(8,128)(2,1)}, u32[]{:S(2)}) copy-start(bf16[128,3584]{1,0:T(8,128)(2,1)} %drive.1.refs_0_) | copy-start | bytes 2752516
  11.4 43.1 %copy-start.3 = (f32[1792]{0:T(1024)S(1)}, f32[1792]{0:T(1024)}, u32[]{:S(2)}) copy-start(f32[1792]{0:T(1024)} %param.7) | copy-start | bytes 21508
  15.0 21.1 %collective-permute-start.3 = (bf16[128,3584]{1,0:T(8,128)(2,1)}, bf16[128,3584]{1,0:T(8,128)(2,1)S(1)}, u32[]{:S(2)}, u32[]{:S(2)}) collective-permute-start(bf16[128,3584]{1,0:T(8,128)(2,1)} %drive.1.refs_0_), channel_id=1, source_target_pairs={{0,192},{64,0},{128,64},{192,128},{1,193},{65,1},{129,65},{193,129... | collective-permute-start | bytes 2752520 | tf_op jit(solution)/shard_map/ppermute | solution.py:20
  15.9 22.1 %collective-permute-start.1 = (bf16[128,3584]{1,0:T(8,128)(2,1)}, bf16[128,3584]{1,0:T(8,128)(2,1)S(1)}, u32[]{:S(2)}, u32[]{:S(2)}) collective-permute-start(bf16[128,3584]{1,0:T(8,128)(2,1)} %drive.1.refs_0_), channel_id=1, source_target_pairs={{0,64},{64,128},{128,192},{192,0},{1,65},{65,129},{129,193},{193,1... | collective-permute-start | bytes 2752520 | tf_op jit(solution)/shard_map/ppermute | solution.py:20
  16.5 9.0 %collective-permute-start.10 = (bf16[8,56,256]{2,1,0:T(8,128)(2,1)S(1)}, bf16[8,56,256]{2,1,0:T(8,128)(2,1)S(1)}, u32[]{:S(2)}, u32[]{:S(2)}) collective-permute-start(bf16[8,56,256]{2,1,0:T(8,128)(2,1)S(1)} %all-to-all-done.refs_0_), channel_id=1, source_target_pairs={{0,1},{1,2},{2,3},{3,0},{4,5},{5,6},{6,7},{7,4},{8,9},{9,10},{10,1... | collective-permute-start | bytes 688136 | tf_op jit(solution)/shard_map/ppermute | solution.py:20
  17.1 9.9 %collective-permute-start.9 = (bf16[8,56,256]{2,1,0:T(8,128)(2,1)S(1)}, bf16[8,56,256]{2,1,0:T(8,128)(2,1)S(1)}, u32[]{:S(2)}, u32[]{:S(2)}) collective-permute-start(bf16[8,56,256]{2,1,0:T(8,128)(2,1)S(1)} %all-to-all-done.refs_0_), channel_id=1, source_target_pairs={{0,3},{1,0},{2,1},{3,2},{4,7},{5,4},{6,5},{7,6},{8,11},{9,8},{10,9... | collective-permute-start | bytes 688136 | tf_op jit(solution)/shard_map/ppermute | solution.py:20
  19.2 10.1 %collective-permute-start.8 = (bf16[8,56,256]{2,1,0:T(8,128)(2,1)S(1)}, bf16[8,56,256]{2,1,0:T(8,128)(2,1)S(1)}, u32[]{:S(2)}, u32[]{:S(2)}) collective-permute-start(bf16[8,56,256]{2,1,0:T(8,128)(2,1)S(1)} %all-to-all-done.refs_0_), channel_id=1, source_target_pairs={{0,4},{4,0},{1,5},{5,1},{2,6},{6,2},{3,7},{7,3},{8,12},{12,8},{9,1... | collective-permute-start | bytes 688136 | tf_op jit(solution)/shard_map/ppermute | solution.py:20
  25.5 14.7 %collective-permute-start.7 = (bf16[8,56,256]{2,1,0:T(8,128)(2,1)S(1)}, bf16[8,56,256]{2,1,0:T(8,128)(2,1)S(1)}, u32[]{:S(2)}, u32[]{:S(2)}) collective-permute-start(bf16[8,56,256]{2,1,0:T(8,128)(2,1)S(1)} %all-to-all-done.refs_0_), channel_id=1, source_target_pairs={{0,2},{1,3},{2,0},{3,1},{4,6},{5,7},{6,4},{7,5},{8,10},{9,11},{10,... | collective-permute-start | bytes 688136 | tf_op jit(solution)/shard_map/ppermute | solution.py:20
  29.3 11.0 %collective-permute-start.13 = (bf16[8,56,256]{2,1,0:T(8,128)(2,1)S(1)}, bf16[8,56,256]{2,1,0:T(8,128)(2,1)S(1)}, u32[]{:S(2)}, u32[]{:S(2)}) collective-permute-start(bf16[8,56,256]{2,1,0:T(8,128)(2,1)S(1)} %collective-permute-done.8.refs_4_), channel_id=1, source_target_pairs={{0,1},{1,2},{2,3},{3,0},{4,5},{5,6},{6,7},{7,4},{8,9},{9,10},{10,1... | collective-permute-start | bytes 688136 | tf_op jit(solution)/shard_map/ppermute | solution.py:20
  29.3 16.1 %collective-permute-start.12 = (bf16[8,56,256]{2,1,0:T(8,128)(2,1)S(1)}, bf16[8,56,256]{2,1,0:T(8,128)(2,1)S(1)}, u32[]{:S(2)}, u32[]{:S(2)}) collective-permute-start(bf16[8,56,256]{2,1,0:T(8,128)(2,1)S(1)} %collective-permute-done.8.refs_4_), channel_id=1, source_target_pairs={{0,2},{1,3},{2,0},{3,1},{4,6},{5,7},{6,4},{7,5},{8,10},{9,11},{10,... | collective-permute-start | bytes 688136 | tf_op jit(solution)/shard_map/ppermute | solution.py:20
  36.1 9.4 %collective-permute-start.11 = (bf16[8,56,256]{2,1,0:T(8,128)(2,1)S(1)}, bf16[8,56,256]{2,1,0:T(8,128)(2,1)S(1)}, u32[]{:S(2)}, u32[]{:S(2)}) collective-permute-start(bf16[8,56,256]{2,1,0:T(8,128)(2,1)S(1)} %collective-permute-done.8.refs_4_), channel_id=1, source_target_pairs={{0,3},{1,0},{2,1},{3,2},{4,7},{5,4},{6,5},{7,6},{8,11},{9,8},{10,9... | collective-permute-start | bytes 688136 | tf_op jit(solution)/shard_map/ppermute | solution.py:20
  38.0 9.9 %collective-permute-start.6 = (bf16[64,3584]{1,0:T(8,128)(2,1)S(1)}, bf16[64,3584]{1,0:T(8,128)(2,1)S(1)}, u32[]{:S(2)}, u32[]{:S(2)}) collective-permute-start(bf16[64,3584]{1,0:T(8,128)(2,1)S(1)} %slice.9), channel_id=1, source_target_pairs={{0,192},{64,0},{128,64},{192,128},{1,193},{65,1},{129,65},{193,129... | collective-permute-start | bytes 1376264 | tf_op jit(solution)/shard_map/ppermute | solution.py:20
  40.2 10.8 %collective-permute-start.5 = (bf16[64,3584]{1,0:T(8,128)(2,1)S(1)}, bf16[64,3584]{1,0:T(8,128)(2,1)S(1)}, u32[]{:S(2)}, u32[]{:S(2)}) collective-permute-start(bf16[64,3584]{1,0:T(8,128)(2,1)S(1)} %slice.8), channel_id=1, source_target_pairs={{0,64},{64,128},{128,192},{192,0},{1,65},{65,129},{129,193},{193,1... | collective-permute-start | bytes 1376264 | tf_op jit(solution)/shard_map/ppermute | solution.py:20
  40.3 14.3 %collective-permute-start = (bf16[128,3584]{1,0:T(8,128)(2,1)S(1)}, bf16[128,3584]{1,0:T(8,128)(2,1)S(1)}, u32[]{:S(2)}, u32[]{:S(2)}) collective-permute-start(bf16[128,3584]{1,0:T(8,128)(2,1)S(1)} %copy-done.1), channel_id=1, source_target_pairs={{0,32},{32,0},{1,33},{33,1},{2,34},{34,2},{3,35},{35,3},{4,36},{36... | collective-permute-start | bytes 2752520 | tf_op jit(solution)/shard_map/ppermute | solution.py:20
  45.4 9.2 %collective-permute-start.4 = (bf16[128,3584]{1,0:T(8,128)(2,1)S(1)}, bf16[128,3584]{1,0:T(8,128)(2,1)S(1)}, u32[]{:S(2)}, u32[]{:S(2)}) collective-permute-start(bf16[128,3584]{1,0:T(8,128)(2,1)S(1)} %collective-permute-done.3.refs_4_), channel_id=1, source_target_pairs={{0,32},{32,0},{1,33},{33,1},{2,34},{34,2},{3,35},{35,3},{4,36},{36... | collective-permute-start | bytes 2752520 | tf_op jit(solution)/shard_map/ppermute | solution.py:20
  45.5 11.1 %collective-permute-start.2 = (bf16[128,3584]{1,0:T(8,128)(2,1)S(1)}, bf16[128,3584]{1,0:T(8,128)(2,1)S(1)}, u32[]{:S(2)}, u32[]{:S(2)}) collective-permute-start(bf16[128,3584]{1,0:T(8,128)(2,1)S(1)} %collective-permute-done.1.refs_2_), channel_id=1, source_target_pairs={{0,32},{32,0},{1,33},{33,1},{2,34},{34,2},{3,35},{35,3},{4,36},{36... | collective-permute-start | bytes 2752520 | tf_op jit(solution)/shard_map/ppermute | solution.py:20
  51.1 4.8 %collective-permute-start.14 = (bf16[64,3584]{1,0:T(8,128)(2,1)S(1)}, bf16[64,3584]{1,0:T(8,128)(2,1)S(1)}, u32[]{:S(2)}, u32[]{:S(2)}) collective-permute-start(bf16[64,3584]{1,0:T(8,128)(2,1)S(1)} %collective-permute-done.5.refs_6_), channel_id=1, source_target_pairs={{0,32},{32,0},{1,33},{33,1},{2,34},{34,2},{3,35},{35,3},{4,36},{36... | collective-permute-start | bytes 1376264 | tf_op jit(solution)/shard_map/ppermute | solution.py:20
  54.5 2.1 %collective-permute-start.15 = (bf16[64,3584]{1,0:T(8,128)(2,1)S(1)}, bf16[64,3584]{1,0:T(8,128)(2,1)S(1)}, u32[]{:S(2)}, u32[]{:S(2)}) collective-permute-start(bf16[64,3584]{1,0:T(8,128)(2,1)S(1)} %collective-permute-done.6.refs_8_), channel_id=1, source_target_pairs={{0,32},{32,0},{1,33},{33,1},{2,34},{34,2},{3,35},{35,3},{4,36},{36... | collective-permute-start | bytes 1376264 | tf_op jit(solution)/shard_map/ppermute | solution.py:20
  54.5 2.1 %copy-start = (bf16[128,3584]{1,0:T(8,128)(2,1)S(1)}, bf16[128,3584]{1,0:T(8,128)(2,1)}, u32[]{:S(2)}) copy-start(bf16[128,3584]{1,0:T(8,128)(2,1)} %refs_10_.1) | copy-start | bytes 2752516
  60.6 23.9 %all-to-all-start.1 = ((f32[64,1,768]{2,1,0:T(1,128)}), f32[64,1,768]{2,1,0:T(1,128)S(1)}, u32[]{:S(2)}, u32[]{:S(2)}) async-start(f32[64,1,768]{2,1,0:T(1,128)} %get-tuple-element.27), calls=%async_computation.1 | async-start | bytes 393216 | tf_op jit(solution)/shard_map/all_to_all | solution.py:217
  70.3 7.4 %collective-permute-start.18 = (f32[128,256]{1,0:T(8,128)S(1)}, f32[128,256]{1,0:T(8,128)S(1)}, u32[]{:S(2)}, u32[]{:S(2)}) collective-permute-start(f32[128,256]{1,0:T(8,128)S(1)} %get-tuple-element.26.refs_0_), channel_id=1, source_target_pairs={{0,64},{64,128},{128,192},{192,0},{1,65},{65,129},{129,193},{193,1... | collective-permute-start | bytes 393224 | tf_op jit(solution)/shard_map/ppermute | solution.py:20
  71.8 10.1 %collective-permute-start.17 = (f32[128,256]{1,0:T(8,128)S(1)}, f32[128,256]{1,0:T(8,128)S(1)}, u32[]{:S(2)}, u32[]{:S(2)}) collective-permute-start(f32[128,256]{1,0:T(8,128)S(1)} %get-tuple-element.26.refs_0_), channel_id=1, source_target_pairs={{0,128},{64,192},{128,0},{192,64},{1,129},{65,193},{129,1},{193,65... | collective-permute-start | bytes 393224 | tf_op jit(solution)/shard_map/ppermute | solution.py:20
  74.4 8.8 %collective-permute-start.16 = (f32[128,256]{1,0:T(8,128)S(1)}, f32[128,256]{1,0:T(8,128)S(1)}, u32[]{:S(2)}, u32[]{:S(2)}) collective-permute-start(f32[128,256]{1,0:T(8,128)S(1)} %get-tuple-element.26.refs_0_), channel_id=1, source_target_pairs={{0,192},{64,0},{128,64},{192,128},{1,193},{65,1},{129,65},{193,129... | collective-permute-start | bytes 393224 | tf_op jit(solution)/shard_map/ppermute | solution.py:20
  75.4 7.8 %collective-permute-start.19 = (f32[128,256]{1,0:T(8,128)S(1)}, f32[128,256]{1,0:T(8,128)S(1)}, u32[]{:S(2)}, u32[]{:S(2)}) collective-permute-start(f32[128,256]{1,0:T(8,128)S(1)} %get-tuple-element.26.refs_0_), channel_id=1, source_target_pairs={{0,32},{32,0},{1,33},{33,1},{2,34},{34,2},{3,35},{35,3},{4,36},{36... | collective-permute-start | bytes 393224 | tf_op jit(solution)/shard_map/ppermute | solution.py:20
  77.7 5.5 %collective-permute-start.22 = (f32[128,256]{1,0:T(8,128)S(1)}, f32[128,256]{1,0:T(8,128)S(1)}, u32[]{:S(2)}, u32[]{:S(2)}) collective-permute-start(f32[128,256]{1,0:T(8,128)S(1)} %collective-permute-done.18.refs_3_), channel_id=1, source_target_pairs={{0,32},{32,0},{1,33},{33,1},{2,34},{34,2},{3,35},{35,3},{4,36},{36... | collective-permute-start | bytes 393224 | tf_op jit(solution)/shard_map/ppermute | solution.py:20
  81.8 2.3 %collective-permute-start.21 = (f32[128,256]{1,0:T(8,128)S(1)}, f32[128,256]{1,0:T(8,128)S(1)}, u32[]{:S(2)}, u32[]{:S(2)}) collective-permute-start(f32[128,256]{1,0:T(8,128)S(1)} %collective-permute-done.17.refs_2_), channel_id=1, source_target_pairs={{0,32},{32,0},{1,33},{33,1},{2,34},{34,2},{3,35},{35,3},{4,36},{36... | collective-permute-start | bytes 393224 | tf_op jit(solution)/shard_map/ppermute | solution.py:20
  83.2 1.3 %collective-permute-start.20 = (f32[128,256]{1,0:T(8,128)S(1)}, f32[128,256]{1,0:T(8,128)S(1)}, u32[]{:S(2)}, u32[]{:S(2)}) collective-permute-start(f32[128,256]{1,0:T(8,128)S(1)} %collective-permute-done.16.refs_1_), channel_id=1, source_target_pairs={{0,32},{32,0},{1,33},{33,1},{2,34},{34,2},{3,35},{35,3},{4,36},{36... | collective-permute-start | bytes 393224 | tf_op jit(solution)/shard_map/ppermute | solution.py:20

commit v6 on v5

--- a/solution.py
+++ b/solution.py
@@ -12,7 +12,8 @@
 Y, CORE, Z, X = 4, 2, 2, 4
 STEPS = Y * CORE
 MIB = 1024 * 1024
-GROUPS = ((0, 24), (24, 48), (48, 64))
+LANES = 128
+GROUPS = 4
 
 
 def around(x, axis, by):
@@ -68,44 +69,44 @@
     pieces, (features_ref, weight_ref, threshold_ref, rates_ref, grad_ref, current_ref) = refs[:count], refs[count:]
     rows = features_ref.shape[0]
     core, y = lax.axis_index("core"), lax.axis_index("y")
-    left = jnp.concatenate([p[...] for p in pieces] + [features_ref[...]], axis=0)
-    total = jnp.dot(left, weight_ref[...], preferred_element_type=jnp.float32)
-    at = 0
-    for dy, dc, first, tall in spans:
-        step = (y + dy) % Y * CORE + (core + dc) % CORE
-        current_ref[step, first : first + tall, :] = total[at : at + tall]
-        at += tall
-    current_ref[STEPS] = total[at:]
+    cut = 4
+    for part in (range(cut), range(cut, count)):
+        last = part.stop == count
+        held = [pieces[i][...] for i in part] + ([features_ref[...]] if last else [])
+        total = jnp.dot(jnp.concatenate(held, axis=0), weight_ref[...], preferred_element_type=jnp.float32)
+        at = 0
+        for i in part:
+            dy, dc, first, tall = spans[i]
+            step = (y + dy) % Y * CORE + (core + dc) % CORE
+            current_ref[step, first : first + tall, :] = total[at : at + tall]
+            at += tall
+        if last:
+            current_ref[STEPS] = total[at:]
     threshold = threshold_ref[:, pl.ds(start_of(y, core), WIDE)]
-    tall = GROUPS[-1][1]
-
-    def strip(i, grad_sum):
-        at = pl.ds(pl.multiple_of(i * tall, tall), tall)
-        potential = jnp.zeros((tall, WIDE), jnp.float32)
-        total = jnp.zeros((tall, WIDE), jnp.float32)
-        for t in range(STEPS):
-            rising = potential + 2.0 * current_ref[t, at, :]
-            fired = jax.nn.sigmoid(SHARP * (rising - threshold))
-            potential = rising - threshold * fired
-            current_ref[t, at, :] = fired
-            total = total + fired
-        rates = threshold * total / STEPS
-        rates_ref[at, :] = rates
-        v = current_ref[STEPS, at, :]
-        error = (rates - v * jax.nn.sigmoid(v)) / tokens_all
-        cotangent = jnp.zeros((tall, WIDE), jnp.float32)
-        for t in reversed(range(STEPS)):
-            fired = current_ref[t, at, :]
-            dspike = error * threshold / STEPS - threshold * cotangent
-            dwide = dspike * SHARP * fired * (1.0 - fired)
-            grad_sum = grad_sum + (-dwide - fired * cotangent + error * fired / STEPS)
-            cotangent = cotangent + dwide
-        return grad_sum
-
-    grad_sum = lax.fori_loop(0, rows // tall, strip, jnp.zeros((tall, WIDE), jnp.float32))
-    for i, (first, last) in enumerate(GROUPS):
-        part = jnp.sum(grad_sum[first:last], axis=0, keepdims=True)
-        grad_ref[:, :, i * WIDE : (i + 1) * WIDE] = jnp.broadcast_to(part[None], (grad_ref.shape[0], 1, WIDE))
+    potential = jnp.zeros((rows, WIDE), jnp.float32)
+    total = jnp.zeros((rows, WIDE), jnp.float32)
+    for t in range(STEPS):
+        rising = potential + 2.0 * current_ref[t]
+        fired = jax.nn.sigmoid(SHARP * (rising - threshold))
+        potential = rising - threshold * fired
+        current_ref[t] = fired
+        total = total + fired
+    rates = threshold * total / STEPS
+    rates_ref[...] = rates
+    v = current_ref[STEPS]
+    share = (rates - v * jax.nn.sigmoid(v)) / tokens_all / STEPS
+    cotangent = jnp.zeros((rows, WIDE), jnp.float32)
+    grad_sum = jnp.zeros((rows, WIDE), jnp.float32)
+    for t in reversed(range(STEPS)):
+        fired = current_ref[t]
+        pull = share - cotangent
+        dwide = pull * (SHARP * threshold) * (fired * (1.0 - fired))
+        grad_sum = grad_sum + (fired * pull - dwide)
+        cotangent = cotangent + dwide
+    tall = rows // GROUPS
+    parts = [jnp.sum(grad_sum[g * tall : (g + 1) * tall], axis=0, keepdims=True) for g in range(GROUPS)]
+    tile = jnp.concatenate([p[:, h : h + LANES] for p in parts for h in range(0, WIDE, LANES)], axis=0)
+    grad_ref[...] = jnp.broadcast_to(tile[None], grad_ref.shape)
 
 
 def finish_kernel(*refs):
@@ -127,10 +128,12 @@
 
     count = grads_ref.shape[0] // STEPS
     for w, s in enumerate(STARTS):
-        total = jnp.sum(grads_ref[w * count : (w + 1) * count], axis=0)
-        total = sum(total[:, i : i + WIDE] for i in range(0, total.shape[1], WIDE))
-        skip = 128 if w % 4 == 1 else 0
-        grad_ref[s + skip : s + WIDE] = total[0, skip:]
+        tile = jnp.sum(grads_ref[w * count : (w + 1) * count], axis=0)
+        for h in range(WIDE // LANES):
+            if w % 4 == 1 and h == 0:
+                continue
+            lanes = sum(tile[i : i + 1] for i in range(h, tile.shape[0], WIDE // LANES))
+            grad_ref[s + h * LANES : s + (h + 1) * LANES] = lanes[0]
 
 
 def on_device(features, spike_mask, gate_weight, threshold):
@@ -201,7 +204,7 @@
         functools.partial(student_kernel, tokens_all=tokens_all, spans=spans),
         out_shape=(
             jax.ShapeDtypeStruct((rows, WIDE), jnp.float32),
-            jax.ShapeDtypeStruct((peers, 1, len(GROUPS) * WIDE), jnp.float32),
+            jax.ShapeDtypeStruct((peers, GROUPS * WIDE // LANES, LANES), jnp.float32),
         ),
         in_specs=[vmem] * (len(steps) + 3),
         out_specs=(vmem, vmem),

time: 86.1 us -> 86.5 us (level)
  no operation moved by 1% of the time
where the time goes in v6:
time: 86.5 us; the launch traced here: 86.2 us
  starting transfers between devices  53.1 us (61%)
  waiting for transfers between devices  22.8 us (26%)
  Pallas kernels  8.5 us (10%)
  local copies, waits for them, and re-layouts  1.01 us (1%)
    ppermute x23, starting transfers between devices, around(): return lax.ppermute(x, axis, [(i, (i + by) % n) for i in range(n)])  36.9 us
    ppermute x23, waiting for transfers between devices, around(): return lax.ppermute(x, axis, [(i, (i + by) % n) for i in range(n)])  19.2 us
    all_to_all x1, starting transfers between devices, on_device(): grads = lax.all_to_all(grad, ('y', 'core', 'z', 'x'), 0, 0, tiled=True)  9.66 us
    all_to_all x1, starting transfers between devices, on_device(): near_w = lax.all_to_all(payload, ('y', 'core'), 0, 0, tiled=True)  6.54 us
    pallas_call x1, Pallas kernels, on_device(): pl.pallas_call(functools.partial(student_kernel, tokens_all=tokens_all, s...  3.95 us
    all_to_all x1, waiting for transfers between devices, on_device(): near_w = lax.all_to_all(payload, ('y', 'core'), 0, 0, tiled=True)  3.6 us
    pallas_call x1, Pallas kernels, on_device(): pl.pallas_call(drive_kernel, out_shape=jax.ShapeDtypeStruct((rows, deep),...  2.58 us
  transfers between devices with their start and end apart: 25, of which 11 were waited for; matrix products, arithmetic and copies ran while one was open for 0% of the time, Pallas kernels for 3%

profile of v6, /device:TPU:1, one launch (start us, length us, event | category | flops | bytes accessed | tf_op | source)
XLA Modules:
  0.0 86.2 jit_solution(6211546357127748944)
XLA Ops:
  0.6 0.9 %copy-done.2 = bf16[56,1792]{1,0:T(8,128)(2,1)S(1)} copy-done((bf16[56,1792]{1,0:T(8,128)(2,1)S(1)}, bf16[56,1792]{1,0:T(8,128)(2,1)}, u32[]{:S(2)}) %copy-start.2) | copy-done | bytes 200728
  1.6 0.7 windows.1
  2.3 6.5 %all-to-all-start = ((bf16[8,56,256]{2,1,0:T(8,128)(2,1)}), bf16[8,56,256]{2,1,0:T(8,128)(2,1)S(1)}, u32[]{:S(2)}, u32[]{:S(2)}) async-start(bf16[8,56,256]{2,1,0:T(8,128)(2,1)} %windows.1), calls=%async_computation | async-start | bytes 458752 | tf_op jit(solution)/shard_map/all_to_all | solution.py:173
  8.8 2.6 %drive.1.refs_0_ = bf16[128,3584]{1,0:T(8,128)(2,1)} custom-call(s32[1,128,3584]{2,1,0:T(8,128)} %mask_hbm.1, bf16[128,3584]{1,0:T(8,128)(2,1)} %refs_10_.1), custom_call_target="tpu_custom_call" | custom-call | tf_op jit(solution)/shard_map/drive/pallas_call | solution.py:150
  11.4 0.0 copy-start.1
  11.4 0.0 copy-start.3
  11.4 3.6 %all-to-all-done.refs_0_ = bf16[8,56,256]{2,1,0:T(8,128)(2,1)S(1)} async-done(((bf16[8,56,256]{2,1,0:T(8,128)(2,1)}), bf16[8,56,256]{2,1,0:T(8,128)(2,1)S(1)}, u32[]{:S(2)}, u32[]{:S(2)}) %all-to-all-start) | async-done | bytes 229408 | tf_op jit(solution)/shard_map/all_to_all | solution.py:173
  15.0 0.9 %collective-permute-start.3 = (bf16[128,3584]{1,0:T(8,128)(2,1)}, bf16[128,3584]{1,0:T(8,128)(2,1)S(1)}, u32[]{:S(2)}, u32[]{:S(2)}) collective-permute-start(bf16[128,3584]{1,0:T(8,128)(2,1)} %drive.1.refs_0_), channel_id=1, source_target_pairs={{0,192},{64,0},{128,64},{192,128},{1,193},{65,1},{129,65},{193,129... | collective-permute-start | bytes 2752520 | tf_op jit(solution)/shard_map/ppermute | solution.py:21
  15.9 0.6 collective-permute-start.1
  16.5 0.6 collective-permute-start.10
  17.1 2.1 %collective-permute-start.9 = (bf16[8,56,256]{2,1,0:T(8,128)(2,1)S(1)}, bf16[8,56,256]{2,1,0:T(8,128)(2,1)S(1)}, u32[]{:S(2)}, u32[]{:S(2)}) collective-permute-start(bf16[8,56,256]{2,1,0:T(8,128)(2,1)S(1)} %all-to-all-done.refs_0_), channel_id=1, source_target_pairs={{0,3},{1,0},{2,1},{3,2},{4,7},{5,4},{6,5},{7,6},{8,11},{9,8},{10,9... | collective-permute-start | bytes 688136 | tf_op jit(solution)/shard_map/ppermute | solution.py:21
  19.2 6.3 %collective-permute-start.8 = (bf16[8,56,256]{2,1,0:T(8,128)(2,1)S(1)}, bf16[8,56,256]{2,1,0:T(8,128)(2,1)S(1)}, u32[]{:S(2)}, u32[]{:S(2)}) collective-permute-start(bf16[8,56,256]{2,1,0:T(8,128)(2,1)S(1)} %all-to-all-done.refs_0_), channel_id=1, source_target_pairs={{0,4},{4,0},{1,5},{5,1},{2,6},{6,2},{3,7},{7,3},{8,12},{12,8},{9,1... | collective-permute-start | bytes 688136 | tf_op jit(solution)/shard_map/ppermute | solution.py:21
  25.5 0.0 collective-permute-done.10.refs_3_
  25.5 1.5 %collective-permute-start.7 = (bf16[8,56,256]{2,1,0:T(8,128)(2,1)S(1)}, bf16[8,56,256]{2,1,0:T(8,128)(2,1)S(1)}, u32[]{:S(2)}, u32[]{:S(2)}) collective-permute-start(bf16[8,56,256]{2,1,0:T(8,128)(2,1)S(1)} %all-to-all-done.refs_0_), channel_id=1, source_target_pairs={{0,2},{1,3},{2,0},{3,1},{4,6},{5,7},{6,4},{7,5},{8,10},{9,11},{10,... | collective-permute-start | bytes 688136 | tf_op jit(solution)/shard_map/ppermute | solution.py:21
  27.0 0.0 collective-permute-done.9.refs_1_
  27.0 2.3 %collective-permute-done.8.refs_4_ = bf16[8,56,256]{2,1,0:T(8,128)(2,1)S(1)} collective-permute-done((bf16[8,56,256]{2,1,0:T(8,128)(2,1)S(1)}, bf16[8,56,256]{2,1,0:T(8,128)(2,1)S(1)}, u32[]{:S(2)}, u32[]{:S(2)}) %collective-permute-start.8) | collective-permute-done | bytes 229408 | tf_op jit(solution)/shard_map/ppermute | solution.py:21
  29.3 2.4 %collective-permute-start.12 = (bf16[8,56,256]{2,1,0:T(8,128)(2,1)S(1)}, bf16[8,56,256]{2,1,0:T(8,128)(2,1)S(1)}, u32[]{:S(2)}, u32[]{:S(2)}) collective-permute-start(bf16[8,56,256]{2,1,0:T(8,128)(2,1)S(1)} %collective-permute-done.8.refs_4_), channel_id=1, source_target_pairs={{0,2},{1,3},{2,0},{3,1},{4,6},{5,7},{6,4},{7,5},{8,10},{9,11},{10,... | collective-permute-start | bytes 688136 | tf_op jit(solution)/shard_map/ppermute | solution.py:21
  31.7 4.4 %collective-permute-done.3.refs_4_ = bf16[128,3584]{1,0:T(8,128)(2,1)S(1)} collective-permute-done((bf16[128,3584]{1,0:T(8,128)(2,1)}, bf16[128,3584]{1,0:T(8,128)(2,1)S(1)}, u32[]{:S(2)}, u32[]{:S(2)}) %collective-permute-start.3) | collective-permute-done | bytes 917536 | tf_op jit(solution)/shard_map/ppermute | solution.py:21
  36.1 1.9 %collective-permute-start.11 = (bf16[8,56,256]{2,1,0:T(8,128)(2,1)S(1)}, bf16[8,56,256]{2,1,0:T(8,128)(2,1)S(1)}, u32[]{:S(2)}, u32[]{:S(2)}) collective-permute-start(bf16[8,56,256]{2,1,0:T(8,128)(2,1)S(1)} %collective-permute-done.8.refs_4_), channel_id=1, source_target_pairs={{0,3},{1,0},{2,1},{3,2},{4,7},{5,4},{6,5},{7,6},{8,11},{9,8},{10,9... | collective-permute-start | bytes 688136 | tf_op jit(solution)/shard_map/ppermute | solution.py:21
  38.0 2.2 %collective-permute-start.6 = (bf16[64,3584]{1,0:T(8,128)(2,1)S(1)}, bf16[64,3584]{1,0:T(8,128)(2,1)S(1)}, u32[]{:S(2)}, u32[]{:S(2)}) collective-permute-start(bf16[64,3584]{1,0:T(8,128)(2,1)S(1)} %slice.9), channel_id=1, source_target_pairs={{0,192},{64,0},{128,64},{192,128},{1,193},{65,1},{129,65},{193,129... | collective-permute-start | bytes 1376264 | tf_op jit(solution)/shard_map/ppermute | solution.py:21
  40.2 0.1 collective-permute-start.5
  40.3 5.1 %collective-permute-start = (bf16[128,3584]{1,0:T(8,128)(2,1)S(1)}, bf16[128,3584]{1,0:T(8,128)(2,1)S(1)}, u32[]{:S(2)}, u32[]{:S(2)}) collective-permute-start(bf16[128,3584]{1,0:T(8,128)(2,1)S(1)} %copy-done.1), channel_id=1, source_target_pairs={{0,32},{32,0},{1,33},{33,1},{2,34},{34,2},{3,35},{35,3},{4,36},{36... | collective-permute-start | bytes 2752520 | tf_op jit(solution)/shard_map/ppermute | solution.py:21
  45.4 0.1 collective-permute-start.4
  45.5 0.0 collective-permute-done.11.refs_5_
  45.5 1.1 %collective-permute-start.2 = (bf16[128,3584]{1,0:T(8,128)(2,1)S(1)}, bf16[128,3584]{1,0:T(8,128)(2,1)S(1)}, u32[]{:S(2)}, u32[]{:S(2)}) collective-permute-start(bf16[128,3584]{1,0:T(8,128)(2,1)S(1)} %collective-permute-done.1.refs_2_), channel_id=1, source_target_pairs={{0,32},{32,0},{1,33},{33,1},{2,34},{34,2},{3,35},{35,3},{4,36},{36... | collective-permute-start | bytes 2752520 | tf_op jit(solution)/shard_map/ppermute | solution.py:21
  46.6 1.3 %collective-permute-done.6.refs_8_ = bf16[64,3584]{1,0:T(8,128)(2,1)S(1)} collective-permute-done((bf16[64,3584]{1,0:T(8,128)(2,1)S(1)}, bf16[64,3584]{1,0:T(8,128)(2,1)S(1)}, u32[]{:S(2)}, u32[]{:S(2)}) %collective-permute-start.6) | collective-permute-done | bytes 458784 | tf_op jit(solution)/shard_map/ppermute | solution.py:21
  47.9 3.2 %collective-permute-done.5.refs_6_ = bf16[64,3584]{1,0:T(8,128)(2,1)S(1)} collective-permute-done((bf16[64,3584]{1,0:T(8,128)(2,1)S(1)}, bf16[64,3584]{1,0:T(8,128)(2,1)S(1)}, u32[]{:S(2)}, u32[]{:S(2)}) %collective-permute-start.5) | collective-permute-done | bytes 458784 | tf_op jit(solution)/shard_map/ppermute | solution.py:21
  51.1 3.4 %collective-permute-start.14 = (bf16[64,3584]{1,0:T(8,128)(2,1)S(1)}, bf16[64,3584]{1,0:T(8,128)(2,1)S(1)}, u32[]{:S(2)}, u32[]{:S(2)}) collective-permute-start(bf16[64,3584]{1,0:T(8,128)(2,1)S(1)} %collective-permute-done.5.refs_6_), channel_id=1, source_target_pairs={{0,32},{32,0},{1,33},{33,1},{2,34},{34,2},{3,35},{35,3},{4,36},{36... | collective-permute-start | bytes 1376264 | tf_op jit(solution)/shard_map/ppermute | solution.py:21
  54.5 0.0 collective-permute-start.15
  54.5 0.0 copy-start
  54.5 0.1 assemble.1
  54.6 0.0 collective-permute-done.refs_1_
  54.7 1.2 %collective-permute-done.14.refs_7_ = bf16[64,3584]{1,0:T(8,128)(2,1)S(1)} collective-permute-done((bf16[64,3584]{1,0:T(8,128)(2,1)S(1)}, bf16[64,3584]{1,0:T(8,128)(2,1)S(1)}, u32[]{:S(2)}, u32[]{:S(2)}) %collective-permute-start.14) | collective-permute-done | bytes 458784 | tf_op jit(solution)/shard_map/ppermute | solution.py:21
  55.9 0.7 collective-permute-done.15.refs_9_
  56.6 4.0 %student.1 = (f32[128,256]{1,0:T(8,128)S(1)}, f32[64,8,128]{2,1,0:T(8,128)}) custom-call(bf16[128,3584]{1,0:T(8,128)(2,1)S(1)} %copy-done.1, bf16[128,3584]{1,0:T(8,128)(2,1)S(1)} %collective-permute-done.refs_1_, bf16[128,3584]{1,0:T(8,128)(2,1)S(1)} %collective-permute-done.1.refs_2_, bf16[128,3584]{1,0:T(8,128)(2,1)S(1)} %collective-permute-done.2.refs_3_, ...), custom_call_target="tpu_custom_call" | custom-call | flops 2113929216 | bytes 8388608 | tf_op jit(solution)/shard_map/student/pallas_call | solution.py:203
  60.5 9.7 %all-to-all-start.1 = ((f32[64,8,128]{2,1,0:T(8,128)}), f32[64,8,128]{2,1,0:T(8,128)S(1)}, u32[]{:S(2)}, u32[]{:S(2)}) async-start(f32[64,8,128]{2,1,0:T(8,128)} %get-tuple-element.27), calls=%async_computation.1 | async-start | bytes 524288 | tf_op jit(solution)/shard_map/all_to_all | solution.py:220
  70.2 1.5 %collective-permute-start.18 = (f32[128,256]{1,0:T(8,128)S(1)}, f32[128,256]{1,0:T(8,128)S(1)}, u32[]{:S(2)}, u32[]{:S(2)}) collective-permute-start(f32[128,256]{1,0:T(8,128)S(1)} %get-tuple-element.26.refs_0_), channel_id=1, source_target_pairs={{0,64},{64,128},{128,192},{192,0},{1,65},{65,129},{129,193},{193,1... | collective-permute-start | bytes 393224 | tf_op jit(solution)/shard_map/ppermute | solution.py:21
  71.7 2.6 %collective-permute-start.17 = (f32[128,256]{1,0:T(8,128)S(1)}, f32[128,256]{1,0:T(8,128)S(1)}, u32[]{:S(2)}, u32[]{:S(2)}) collective-permute-start(f32[128,256]{1,0:T(8,128)S(1)} %get-tuple-element.26.refs_0_), channel_id=1, source_target_pairs={{0,128},{64,192},{128,0},{192,64},{1,129},{65,193},{129,1},{193,65... | collective-permute-start | bytes 393224 | tf_op jit(solution)/shard_map/ppermute | solution.py:21
  74.3 1.1 %collective-permute-start.16 = (f32[128,256]{1,0:T(8,128)S(1)}, f32[128,256]{1,0:T(8,128)S(1)}, u32[]{:S(2)}, u32[]{:S(2)}) collective-permute-start(f32[128,256]{1,0:T(8,128)S(1)} %get-tuple-element.26.refs_0_), channel_id=1, source_target_pairs={{0,192},{64,0},{128,64},{192,128},{1,193},{65,1},{129,65},{193,129... | collective-permute-start | bytes 393224 | tf_op jit(solution)/shard_map/ppermute | solution.py:21
  75.3 1.2 %collective-permute-start.19 = (f32[128,256]{1,0:T(8,128)S(1)}, f32[128,256]{1,0:T(8,128)S(1)}, u32[]{:S(2)}, u32[]{:S(2)}) collective-permute-start(f32[128,256]{1,0:T(8,128)S(1)} %get-tuple-element.26.refs_0_), channel_id=1, source_target_pairs={{0,32},{32,0},{1,33},{33,1},{2,34},{34,2},{3,35},{35,3},{4,36},{36... | collective-permute-start | bytes 393224 | tf_op jit(solution)/shard_map/ppermute | solution.py:21
  76.5 1.5 %collective-permute-done.18.refs_3_ = f32[128,256]{1,0:T(8,128)S(1)} collective-permute-done((f32[128,256]{1,0:T(8,128)S(1)}, f32[128,256]{1,0:T(8,128)S(1)}, u32[]{:S(2)}, u32[]{:S(2)}) %collective-permute-start.18) | collective-permute-done | bytes 131104 | tf_op jit(solution)/shard_map/ppermute | solution.py:21
  78.1 0.8 collective-permute-start.22
  78.9 3.3 %collective-permute-done.17.refs_2_ = f32[128,256]{1,0:T(8,128)S(1)} collective-permute-done((f32[128,256]{1,0:T(8,128)S(1)}, f32[128,256]{1,0:T(8,128)S(1)}, u32[]{:S(2)}, u32[]{:S(2)}) %collective-permute-start.17) | collective-permute-done | bytes 131104 | tf_op jit(solution)/shard_map/ppermute | solution.py:21
  82.2 1.5 %collective-permute-start.21 = (f32[128,256]{1,0:T(8,128)S(1)}, f32[128,256]{1,0:T(8,128)S(1)}, u32[]{:S(2)}, u32[]{:S(2)}) collective-permute-start(f32[128,256]{1,0:T(8,128)S(1)} %collective-permute-done.17.refs_2_), channel_id=1, source_target_pairs={{0,32},{32,0},{1,33},{33,1},{2,34},{34,2},{3,35},{35,3},{4,36},{36... | collective-permute-start | bytes 393224 | tf_op jit(solution)/shard_map/ppermute | solution.py:21
  83.7 0.0 collective-permute-start.20
  83.7 1.0 %collective-permute-done.21.refs_6_ = f32[128,256]{1,0:T(8,128)S(1)} collective-permute-done((f32[128,256]{1,0:T(8,128)S(1)}, f32[128,256]{1,0:T(8,128)S(1)}, u32[]{:S(2)}, u32[]{:S(2)}) %collective-permute-start.21) | collective-permute-done | bytes 131104 | tf_op jit(solution)/shard_map/ppermute | solution.py:21
  84.7 0.4 collective-permute-done.20.refs_5_
  85.0 1.1 %finish.1 = (f32[128,1792]{1,0:T(8,128)}, f32[1792]{0:T(1024)}) custom-call(f32[128,256]{1,0:T(8,128)S(1)} %get-tuple-element.26.refs_0_, f32[128,256]{1,0:T(8,128)S(1)} %collective-permute-done.16.refs_1_, f32[128,256]{1,0:T(8,128)S(1)} %collective-permute-done.17.refs_2_, f32[128,256]{1,0:T(8,128)S(1)} %collective-permute-done.18.refs_3_, ...), custom_call_target="tpu_custom_call" | custom-call | tf_op jit(solution)/shard_map/finish/pallas_call | solution.py:223
  (18 shorter events, 0.1 us)
Async XLA Ops:
  0.6 0.9 %copy-start.2 = (bf16[56,1792]{1,0:T(8,128)(2,1)S(1)}, bf16[56,1792]{1,0:T(8,128)(2,1)}, u32[]{:S(2)}) copy-start(bf16[56,1792]{1,0:T(8,128)(2,1)} %weight_ref.1) | copy-start | bytes 602116
  2.3 12.8 %all-to-all-start = ((bf16[8,56,256]{2,1,0:T(8,128)(2,1)}), bf16[8,56,256]{2,1,0:T(8,128)(2,1)S(1)}, u32[]{:S(2)}, u32[]{:S(2)}) async-start(bf16[8,56,256]{2,1,0:T(8,128)(2,1)} %windows.1), calls=%async_computation | async-start | bytes 458752 | tf_op jit(solution)/shard_map/all_to_all | solution.py:173
  11.4 28.9 %copy-start.1 = (bf16[128,3584]{1,0:T(8,128)(2,1)S(1)}, bf16[128,3584]{1,0:T(8,128)(2,1)}, u32[]{:S(2)}) copy-start(bf16[128,3584]{1,0:T(8,128)(2,1)} %drive.1.refs_0_) | copy-start | bytes 2752516
  11.4 43.1 %copy-start.3 = (f32[1792]{0:T(1024)S(1)}, f32[1792]{0:T(1024)}, u32[]{:S(2)}) copy-start(f32[1792]{0:T(1024)} %param.7) | copy-start | bytes 21508
  15.0 21.1 %collective-permute-start.3 = (bf16[128,3584]{1,0:T(8,128)(2,1)}, bf16[128,3584]{1,0:T(8,128)(2,1)S(1)}, u32[]{:S(2)}, u32[]{:S(2)}) collective-permute-start(bf16[128,3584]{1,0:T(8,128)(2,1)} %drive.1.refs_0_), channel_id=1, source_target_pairs={{0,192},{64,0},{128,64},{192,128},{1,193},{65,1},{129,65},{193,129... | collective-permute-start | bytes 2752520 | tf_op jit(solution)/shard_map/ppermute | solution.py:21
  15.9 22.1 %collective-permute-start.1 = (bf16[128,3584]{1,0:T(8,128)(2,1)}, bf16[128,3584]{1,0:T(8,128)(2,1)S(1)}, u32[]{:S(2)}, u32[]{:S(2)}) collective-permute-start(bf16[128,3584]{1,0:T(8,128)(2,1)} %drive.1.refs_0_), channel_id=1, source_target_pairs={{0,64},{64,128},{128,192},{192,0},{1,65},{65,129},{129,193},{193,1... | collective-permute-start | bytes 2752520 | tf_op jit(solution)/shard_map/ppermute | solution.py:21
  16.5 9.0 %collective-permute-start.10 = (bf16[8,56,256]{2,1,0:T(8,128)(2,1)S(1)}, bf16[8,56,256]{2,1,0:T(8,128)(2,1)S(1)}, u32[]{:S(2)}, u32[]{:S(2)}) collective-permute-start(bf16[8,56,256]{2,1,0:T(8,128)(2,1)S(1)} %all-to-all-done.refs_0_), channel_id=1, source_target_pairs={{0,1},{1,2},{2,3},{3,0},{4,5},{5,6},{6,7},{7,4},{8,9},{9,10},{10,1... | collective-permute-start | bytes 688136 | tf_op jit(solution)/shard_map/ppermute | solution.py:21
  17.1 9.9 %collective-permute-start.9 = (bf16[8,56,256]{2,1,0:T(8,128)(2,1)S(1)}, bf16[8,56,256]{2,1,0:T(8,128)(2,1)S(1)}, u32[]{:S(2)}, u32[]{:S(2)}) collective-permute-start(bf16[8,56,256]{2,1,0:T(8,128)(2,1)S(1)} %all-to-all-done.refs_0_), channel_id=1, source_target_pairs={{0,3},{1,0},{2,1},{3,2},{4,7},{5,4},{6,5},{7,6},{8,11},{9,8},{10,9... | collective-permute-start | bytes 688136 | tf_op jit(solution)/shard_map/ppermute | solution.py:21
  19.2 10.1 %collective-permute-start.8 = (bf16[8,56,256]{2,1,0:T(8,128)(2,1)S(1)}, bf16[8,56,256]{2,1,0:T(8,128)(2,1)S(1)}, u32[]{:S(2)}, u32[]{:S(2)}) collective-permute-start(bf16[8,56,256]{2,1,0:T(8,128)(2,1)S(1)} %all-to-all-done.refs_0_), channel_id=1, source_target_pairs={{0,4},{4,0},{1,5},{5,1},{2,6},{6,2},{3,7},{7,3},{8,12},{12,8},{9,1... | collective-permute-start | bytes 688136 | tf_op jit(solution)/shard_map/ppermute | solution.py:21
  25.5 14.7 %collective-permute-start.7 = (bf16[8,56,256]{2,1,0:T(8,128)(2,1)S(1)}, bf16[8,56,256]{2,1,0:T(8,128)(2,1)S(1)}, u32[]{:S(2)}, u32[]{:S(2)}) collective-permute-start(bf16[8,56,256]{2,1,0:T(8,128)(2,1)S(1)} %all-to-all-done.refs_0_), channel_id=1, source_target_pairs={{0,2},{1,3},{2,0},{3,1},{4,6},{5,7},{6,4},{7,5},{8,10},{9,11},{10,... | collective-permute-start | bytes 688136 | tf_op jit(solution)/shard_map/ppermute | solution.py:21
  29.3 11.0 %collective-permute-start.13 = (bf16[8,56,256]{2,1,0:T(8,128)(2,1)S(1)}, bf16[8,56,256]{2,1,0:T(8,128)(2,1)S(1)}, u32[]{:S(2)}, u32[]{:S(2)}) collective-permute-start(bf16[8,56,256]{2,1,0:T(8,128)(2,1)S(1)} %collective-permute-done.8.refs_4_), channel_id=1, source_target_pairs={{0,1},{1,2},{2,3},{3,0},{4,5},{5,6},{6,7},{7,4},{8,9},{9,10},{10,1... | collective-permute-start | bytes 688136 | tf_op jit(solution)/shard_map/ppermute | solution.py:21
  29.3 16.1 %collective-permute-start.12 = (bf16[8,56,256]{2,1,0:T(8,128)(2,1)S(1)}, bf16[8,56,256]{2,1,0:T(8,128)(2,1)S(1)}, u32[]{:S(2)}, u32[]{:S(2)}) collective-permute-start(bf16[8,56,256]{2,1,0:T(8,128)(2,1)S(1)} %collective-permute-done.8.refs_4_), channel_id=1, source_target_pairs={{0,2},{1,3},{2,0},{3,1},{4,6},{5,7},{6,4},{7,5},{8,10},{9,11},{10,... | collective-permute-start | bytes 688136 | tf_op jit(solution)/shard_map/ppermute | solution.py:21
  36.1 9.4 %collective-permute-start.11 = (bf16[8,56,256]{2,1,0:T(8,128)(2,1)S(1)}, bf16[8,56,256]{2,1,0:T(8,128)(2,1)S(1)}, u32[]{:S(2)}, u32[]{:S(2)}) collective-permute-start(bf16[8,56,256]{2,1,0:T(8,128)(2,1)S(1)} %collective-permute-done.8.refs_4_), channel_id=1, source_target_pairs={{0,3},{1,0},{2,1},{3,2},{4,7},{5,4},{6,5},{7,6},{8,11},{9,8},{10,9... | collective-permute-start | bytes 688136 | tf_op jit(solution)/shard_map/ppermute | solution.py:21
  38.0 9.9 %collective-permute-start.6 = (bf16[64,3584]{1,0:T(8,128)(2,1)S(1)}, bf16[64,3584]{1,0:T(8,128)(2,1)S(1)}, u32[]{:S(2)}, u32[]{:S(2)}) collective-permute-start(bf16[64,3584]{1,0:T(8,128)(2,1)S(1)} %slice.9), channel_id=1, source_target_pairs={{0,192},{64,0},{128,64},{192,128},{1,193},{65,1},{129,65},{193,129... | collective-permute-start | bytes 1376264 | tf_op jit(solution)/shard_map/ppermute | solution.py:21
  40.2 10.8 %collective-permute-start.5 = (bf16[64,3584]{1,0:T(8,128)(2,1)S(1)}, bf16[64,3584]{1,0:T(8,128)(2,1)S(1)}, u32[]{:S(2)}, u32[]{:S(2)}) collective-permute-start(bf16[64,3584]{1,0:T(8,128)(2,1)S(1)} %slice.8), channel_id=1, source_target_pairs={{0,64},{64,128},{128,192},{192,0},{1,65},{65,129},{129,193},{193,1... | collective-permute-start | bytes 1376264 | tf_op jit(solution)/shard_map/ppermute | solution.py:21
  40.3 14.3 %collective-permute-start = (bf16[128,3584]{1,0:T(8,128)(2,1)S(1)}, bf16[128,3584]{1,0:T(8,128)(2,1)S(1)}, u32[]{:S(2)}, u32[]{:S(2)}) collective-permute-start(bf16[128,3584]{1,0:T(8,128)(2,1)S(1)} %copy-done.1), channel_id=1, source_target_pairs={{0,32},{32,0},{1,33},{33,1},{2,34},{34,2},{3,35},{35,3},{4,36},{36... | collective-permute-start | bytes 2752520 | tf_op jit(solution)/shard_map/ppermute | solution.py:21
  45.4 9.2 %collective-permute-start.4 = (bf16[128,3584]{1,0:T(8,128)(2,1)S(1)}, bf16[128,3584]{1,0:T(8,128)(2,1)S(1)}, u32[]{:S(2)}, u32[]{:S(2)}) collective-permute-start(bf16[128,3584]{1,0:T(8,128)(2,1)S(1)} %collective-permute-done.3.refs_4_), channel_id=1, source_target_pairs={{0,32},{32,0},{1,33},{33,1},{2,34},{34,2},{3,35},{35,3},{4,36},{36... | collective-permute-start | bytes 2752520 | tf_op jit(solution)/shard_map/ppermute | solution.py:21
  45.5 11.1 %collective-permute-start.2 = (bf16[128,3584]{1,0:T(8,128)(2,1)S(1)}, bf16[128,3584]{1,0:T(8,128)(2,1)S(1)}, u32[]{:S(2)}, u32[]{:S(2)}) collective-permute-start(bf16[128,3584]{1,0:T(8,128)(2,1)S(1)} %collective-permute-done.1.refs_2_), channel_id=1, source_target_pairs={{0,32},{32,0},{1,33},{33,1},{2,34},{34,2},{3,35},{35,3},{4,36},{36... | collective-permute-start | bytes 2752520 | tf_op jit(solution)/shard_map/ppermute | solution.py:21
  51.1 4.8 %collective-permute-start.14 = (bf16[64,3584]{1,0:T(8,128)(2,1)S(1)}, bf16[64,3584]{1,0:T(8,128)(2,1)S(1)}, u32[]{:S(2)}, u32[]{:S(2)}) collective-permute-start(bf16[64,3584]{1,0:T(8,128)(2,1)S(1)} %collective-permute-done.5.refs_6_), channel_id=1, source_target_pairs={{0,32},{32,0},{1,33},{33,1},{2,34},{34,2},{3,35},{35,3},{4,36},{36... | collective-permute-start | bytes 1376264 | tf_op jit(solution)/shard_map/ppermute | solution.py:21
  54.5 2.1 %collective-permute-start.15 = (bf16[64,3584]{1,0:T(8,128)(2,1)S(1)}, bf16[64,3584]{1,0:T(8,128)(2,1)S(1)}, u32[]{:S(2)}, u32[]{:S(2)}) collective-permute-start(bf16[64,3584]{1,0:T(8,128)(2,1)S(1)} %collective-permute-done.6.refs_8_), channel_id=1, source_target_pairs={{0,32},{32,0},{1,33},{33,1},{2,34},{34,2},{3,35},{35,3},{4,36},{36... | collective-permute-start | bytes 1376264 | tf_op jit(solution)/shard_map/ppermute | solution.py:21
  54.5 2.1 %copy-start = (bf16[128,3584]{1,0:T(8,128)(2,1)S(1)}, bf16[128,3584]{1,0:T(8,128)(2,1)}, u32[]{:S(2)}) copy-start(bf16[128,3584]{1,0:T(8,128)(2,1)} %refs_10_.1) | copy-start | bytes 2752516
  60.5 24.5 %all-to-all-start.1 = ((f32[64,8,128]{2,1,0:T(8,128)}), f32[64,8,128]{2,1,0:T(8,128)S(1)}, u32[]{:S(2)}, u32[]{:S(2)}) async-start(f32[64,8,128]{2,1,0:T(8,128)} %get-tuple-element.27), calls=%async_computation.1 | async-start | bytes 524288 | tf_op jit(solution)/shard_map/all_to_all | solution.py:220
  70.2 7.9 %collective-permute-start.18 = (f32[128,256]{1,0:T(8,128)S(1)}, f32[128,256]{1,0:T(8,128)S(1)}, u32[]{:S(2)}, u32[]{:S(2)}) collective-permute-start(f32[128,256]{1,0:T(8,128)S(1)} %get-tuple-element.26.refs_0_), channel_id=1, source_target_pairs={{0,64},{64,128},{128,192},{192,0},{1,65},{65,129},{129,193},{193,1... | collective-permute-start | bytes 393224 | tf_op jit(solution)/shard_map/ppermute | solution.py:21
  71.7 10.5 %collective-permute-start.17 = (f32[128,256]{1,0:T(8,128)S(1)}, f32[128,256]{1,0:T(8,128)S(1)}, u32[]{:S(2)}, u32[]{:S(2)}) collective-permute-start(f32[128,256]{1,0:T(8,128)S(1)} %get-tuple-element.26.refs_0_), channel_id=1, source_target_pairs={{0,128},{64,192},{128,0},{192,64},{1,129},{65,193},{129,1},{193,65... | collective-permute-start | bytes 393224 | tf_op jit(solution)/shard_map/ppermute | solution.py:21
  74.3 9.4 %collective-permute-start.16 = (f32[128,256]{1,0:T(8,128)S(1)}, f32[128,256]{1,0:T(8,128)S(1)}, u32[]{:S(2)}, u32[]{:S(2)}) collective-permute-start(f32[128,256]{1,0:T(8,128)S(1)} %get-tuple-element.26.refs_0_), channel_id=1, source_target_pairs={{0,192},{64,0},{128,64},{192,128},{1,193},{65,1},{129,65},{193,129... | collective-permute-start | bytes 393224 | tf_op jit(solution)/shard_map/ppermute | solution.py:21
  75.3 8.3 %collective-permute-start.19 = (f32[128,256]{1,0:T(8,128)S(1)}, f32[128,256]{1,0:T(8,128)S(1)}, u32[]{:S(2)}, u32[]{:S(2)}) collective-permute-start(f32[128,256]{1,0:T(8,128)S(1)} %get-tuple-element.26.refs_0_), channel_id=1, source_target_pairs={{0,32},{32,0},{1,33},{33,1},{2,34},{34,2},{3,35},{35,3},{4,36},{36... | collective-permute-start | bytes 393224 | tf_op jit(solution)/shard_map/ppermute | solution.py:21
  78.1 5.6 %collective-permute-start.22 = (f32[128,256]{1,0:T(8,128)S(1)}, f32[128,256]{1,0:T(8,128)S(1)}, u32[]{:S(2)}, u32[]{:S(2)}) collective-permute-start(f32[128,256]{1,0:T(8,128)S(1)} %collective-permute-done.18.refs_3_), channel_id=1, source_target_pairs={{0,32},{32,0},{1,33},{33,1},{2,34},{34,2},{3,35},{35,3},{4,36},{36... | collective-permute-start | bytes 393224 | tf_op jit(solution)/shard_map/ppermute | solution.py:21
  82.2 2.5 %collective-permute-start.21 = (f32[128,256]{1,0:T(8,128)S(1)}, f32[128,256]{1,0:T(8,128)S(1)}, u32[]{:S(2)}, u32[]{:S(2)}) collective-permute-start(f32[128,256]{1,0:T(8,128)S(1)} %collective-permute-done.17.refs_2_), channel_id=1, source_target_pairs={{0,32},{32,0},{1,33},{33,1},{2,34},{34,2},{3,35},{35,3},{4,36},{36... | collective-permute-start | bytes 393224 | tf_op jit(solution)/shard_map/ppermute | solution.py:21
  83.7 1.3 %collective-permute-start.20 = (f32[128,256]{1,0:T(8,128)S(1)}, f32[128,256]{1,0:T(8,128)S(1)}, u32[]{:S(2)}, u32[]{:S(2)}) collective-permute-start(f32[128,256]{1,0:T(8,128)S(1)} %collective-permute-done.16.refs_1_), channel_id=1, source_target_pairs={{0,32},{32,0},{1,33},{33,1},{2,34},{34,2},{3,35},{35,3},{4,36},{36... | collective-permute-start | bytes 393224 | tf_op jit(solution)/shard_map/ppermute | solution.py:21

commit v7 on v5

--- a/solution.py
+++ b/solution.py
@@ -12,7 +12,7 @@
 Y, CORE, Z, X = 4, 2, 2, 4
 STEPS = Y * CORE
 MIB = 1024 * 1024
-GROUPS = ((0, 24), (24, 48), (48, 64))
+GROUPS = ((0, 16), (16, 32), (32, 48), (48, 64))
 
 
 def around(x, axis, by):
@@ -68,14 +68,19 @@
     pieces, (features_ref, weight_ref, threshold_ref, rates_ref, grad_ref, current_ref) = refs[:count], refs[count:]
     rows = features_ref.shape[0]
     core, y = lax.axis_index("core"), lax.axis_index("y")
-    left = jnp.concatenate([p[...] for p in pieces] + [features_ref[...]], axis=0)
-    total = jnp.dot(left, weight_ref[...], preferred_element_type=jnp.float32)
-    at = 0
-    for dy, dc, first, tall in spans:
-        step = (y + dy) % Y * CORE + (core + dc) % CORE
-        current_ref[step, first : first + tall, :] = total[at : at + tall]
-        at += tall
-    current_ref[STEPS] = total[at:]
+    cut = 4
+    for part in (range(cut), range(cut, count)):
+        last = part.stop == count
+        held = [pieces[i][...] for i in part] + ([features_ref[...]] if last else [])
+        total = jnp.dot(jnp.concatenate(held, axis=0), weight_ref[...], preferred_element_type=jnp.float32)
+        at = 0
+        for i in part:
+            dy, dc, first, tall = spans[i]
+            step = (y + dy) % Y * CORE + (core + dc) % CORE
+            current_ref[step, first : first + tall, :] = total[at : at + tall]
+            at += tall
+        if last:
+            current_ref[STEPS] = total[at:]
     threshold = threshold_ref[:, pl.ds(start_of(y, core), WIDE)]
     tall = GROUPS[-1][1]
 
@@ -93,19 +98,24 @@
         rates_ref[at, :] = rates
         v = current_ref[STEPS, at, :]
         error = (rates - v * jax.nn.sigmoid(v)) / tokens_all
+        share = error / STEPS
         cotangent = jnp.zeros((tall, WIDE), jnp.float32)
         for t in reversed(range(STEPS)):
             fired = current_ref[t, at, :]
-            dspike = error * threshold / STEPS - threshold * cotangent
-            dwide = dspike * SHARP * fired * (1.0 - fired)
-            grad_sum = grad_sum + (-dwide - fired * cotangent + error * fired / STEPS)
+            pull = share - cotangent
+            dwide = pull * (SHARP * threshold) * (fired * (1.0 - fired))
+            grad_sum = grad_sum + (fired * pull - dwide)
             cotangent = cotangent + dwide
         return grad_sum
 
     grad_sum = lax.fori_loop(0, rows // tall, strip, jnp.zeros((tall, WIDE), jnp.float32))
     for i, (first, last) in enumerate(GROUPS):
         part = jnp.sum(grad_sum[first:last], axis=0, keepdims=True)
-        grad_ref[:, :, i * WIDE : (i + 1) * WIDE] = jnp.broadcast_to(part[None], (grad_ref.shape[0], 1, WIDE))
+        grad_ref[:, i * WIDE : (i + 1) * WIDE] = part
+
+
+def both_kernel(mine_ref, far_ref, out_ref):
+    out_ref[...] = jnp.broadcast_to((mine_ref[...] + far_ref[...])[None], out_ref.shape)
 
 
 def finish_kernel(*refs):
@@ -196,12 +206,12 @@
     )(near_w, *near_x, far_w, *far_x)
     weight = weight.reshape(deep, WIDE)
 
-    peers = STEPS * Z * X
+    peers = STEPS * X
     rates, grad = pl.pallas_call(
         functools.partial(student_kernel, tokens_all=tokens_all, spans=spans),
         out_shape=(
             jax.ShapeDtypeStruct((rows, WIDE), jnp.float32),
-            jax.ShapeDtypeStruct((peers, 1, len(GROUPS) * WIDE), jnp.float32),
+            jax.ShapeDtypeStruct((1, len(GROUPS) * WIDE), jnp.float32),
         ),
         in_specs=[vmem] * (len(steps) + 3),
         out_specs=(vmem, vmem),
@@ -214,7 +224,15 @@
     )(*steps, features, weight, threshold[None])
 
     rates_y = [around(rates, "y", -1), around(rates, "y", 2), around(rates, "y", 1)]
-    grads = lax.all_to_all(grad, ("y", "core", "z", "x"), 0, 0, tiled=True)
+    grad = pl.pallas_call(
+        both_kernel,
+        out_shape=jax.ShapeDtypeStruct((peers, 1, len(GROUPS) * WIDE), jnp.float32),
+        in_specs=[vmem] * 2,
+        out_specs=vmem,
+        compiler_params=pltpu.CompilerParams(vmem_limit_bytes=4 * MIB),
+        name="both",
+    )(grad, around(grad, "z", 1))
+    grads = lax.all_to_all(grad, ("y", "core", "x"), 0, 0, tiled=True)
     pieces = [rates] + rates_y
     other = [around(v, "core", 1) for v in pieces]
     return pl.pallas_call(

time: 86.1 us -> 85.7 us (level)
  blocking collectives: 0 us -> 13 us
  starting transfers between devices: 53.1 us -> 46.3 us
  waiting for transfers between devices: 22.2 us -> 16.6 us
  Pallas kernels: 8.68 us -> 7.73 us
    all_to_all x0 -> x1, blocking collectives: none -> 13 us  [on_device(): grads = lax.all_to_all(grad, ('y', 'core', 'x'), 0, 0, tiled=True)]
    all_to_all x1 -> x0, starting transfers between devices: 9.66 us -> none  [on_device(): grads = lax.all_to_all(grad, ('y', 'core', 'z', 'x'), 0, 0, tiled=True)]
    ppermute x23 -> x24, waiting for transfers between devices: 18.6 us -> 13 us  [around(): return lax.ppermute(x, axis, [(i, (i + by) % n) for i in range(n)])]
    ppermute x23 -> x24, starting transfers between devices: 36.9 us -> 39.7 us  [around(): return lax.ppermute(x, axis, [(i, (i + by) % n) for i in range(n)])]
    pallas_call x1, Pallas kernels: 4.06 us -> 3.09 us  [on_device(): pl.pallas_call(functools.partial(student_kernel, tokens_all=tokens_all, s...]
  transfers between devices with their start and end apart: 25 -> 25, of which waited for: 11 -> 7; matrix products, arithmetic and copies ran while one was open for 0% -> 0% of each run, Pallas kernels for 3% -> 3%
where the time goes in v7:
time: 85.7 us; the launch traced here: 85.4 us
  starting transfers between devices  46.3 us (54%)
  waiting for transfers between devices  16.6 us (19%)
  blocking collectives  13 us (15%)
  Pallas kernels  7.73 us (9%)
  local copies, waits for them, and re-layouts  1.01 us (1%)
    ppermute x24, starting transfers between devices, around(): return lax.ppermute(x, axis, [(i, (i + by) % n) for i in range(n)])  39.7 us
    ppermute x24, waiting for transfers between devices, around(): return lax.ppermute(x, axis, [(i, (i + by) % n) for i in range(n)])  13 us
    all_to_all x1, blocking collectives, on_device(): grads = lax.all_to_all(grad, ('y', 'core', 'x'), 0, 0, tiled=True)  13 us
    all_to_all x1, starting transfers between devices, on_device(): near_w = lax.all_to_all(payload, ('y', 'core'), 0, 0, tiled=True)  6.54 us
    all_to_all x1, waiting for transfers between devices, on_device(): near_w = lax.all_to_all(payload, ('y', 'core'), 0, 0, tiled=True)  3.6 us
    pallas_call x1, Pallas kernels, on_device(): pl.pallas_call(functools.partial(student_kernel, tokens_all=tokens_all, s...  3.09 us
    pallas_call x1, Pallas kernels, on_device(): pl.pallas_call(drive_kernel, out_shape=jax.ShapeDtypeStruct((rows, deep),...  2.58 us
  transfers between devices with their start and end apart: 25, of which 7 were waited for; matrix products, arithmetic and copies ran while one was open for 0% of the time, Pallas kernels for 3%

profile of v7, /device:TPU:1, one launch (start us, length us, event | category | flops | bytes accessed | tf_op | source)
XLA Modules:
  0.0 85.4 jit_solution(9998346082869329344)
XLA Ops:
  0.6 0.9 %copy-done.2 = bf16[56,1792]{1,0:T(8,128)(2,1)S(1)} copy-done((bf16[56,1792]{1,0:T(8,128)(2,1)S(1)}, bf16[56,1792]{1,0:T(8,128)(2,1)}, u32[]{:S(2)}) %copy-start.2) | copy-done | bytes 200728
  1.6 0.7 windows.1
  2.3 6.5 %all-to-all-start = ((bf16[8,56,256]{2,1,0:T(8,128)(2,1)}), bf16[8,56,256]{2,1,0:T(8,128)(2,1)S(1)}, u32[]{:S(2)}, u32[]{:S(2)}) async-start(bf16[8,56,256]{2,1,0:T(8,128)(2,1)} %windows.1), calls=%async_computation | async-start | bytes 458752 | tf_op jit(solution)/shard_map/all_to_all | solution.py:180
  8.8 2.6 %drive.1.refs_0_ = bf16[128,3584]{1,0:T(8,128)(2,1)} custom-call(s32[1,128,3584]{2,1,0:T(8,128)} %mask_hbm.1, bf16[128,3584]{1,0:T(8,128)(2,1)} %refs_10_.1), custom_call_target="tpu_custom_call" | custom-call | tf_op jit(solution)/shard_map/drive/pallas_call | solution.py:157
  11.4 0.0 copy-start.1
  11.4 0.0 copy-start.3
  11.4 3.6 %all-to-all-done.refs_0_ = bf16[8,56,256]{2,1,0:T(8,128)(2,1)S(1)} async-done(((bf16[8,56,256]{2,1,0:T(8,128)(2,1)}), bf16[8,56,256]{2,1,0:T(8,128)(2,1)S(1)}, u32[]{:S(2)}, u32[]{:S(2)}) %all-to-all-start) | async-done | bytes 229408 | tf_op jit(solution)/shard_map/all_to_all | solution.py:180
  15.0 0.9 %collective-permute-start.3 = (bf16[128,3584]{1,0:T(8,128)(2,1)}, bf16[128,3584]{1,0:T(8,128)(2,1)S(1)}, u32[]{:S(2)}, u32[]{:S(2)}) collective-permute-start(bf16[128,3584]{1,0:T(8,128)(2,1)} %drive.1.refs_0_), channel_id=1, source_target_pairs={{0,192},{64,0},{128,64},{192,128},{1,193},{65,1},{129,65},{193,129... | collective-permute-start | bytes 2752520 | tf_op jit(solution)/shard_map/ppermute | solution.py:20
  15.9 0.6 collective-permute-start.1
  16.5 0.6 collective-permute-start.10
  17.1 2.1 %collective-permute-start.9 = (bf16[8,56,256]{2,1,0:T(8,128)(2,1)S(1)}, bf16[8,56,256]{2,1,0:T(8,128)(2,1)S(1)}, u32[]{:S(2)}, u32[]{:S(2)}) collective-permute-start(bf16[8,56,256]{2,1,0:T(8,128)(2,1)S(1)} %all-to-all-done.refs_0_), channel_id=1, source_target_pairs={{0,3},{1,0},{2,1},{3,2},{4,7},{5,4},{6,5},{7,6},{8,11},{9,8},{10,9... | collective-permute-start | bytes 688136 | tf_op jit(solution)/shard_map/ppermute | solution.py:20
  19.2 6.3 %collective-permute-start.8 = (bf16[8,56,256]{2,1,0:T(8,128)(2,1)S(1)}, bf16[8,56,256]{2,1,0:T(8,128)(2,1)S(1)}, u32[]{:S(2)}, u32[]{:S(2)}) collective-permute-start(bf16[8,56,256]{2,1,0:T(8,128)(2,1)S(1)} %all-to-all-done.refs_0_), channel_id=1, source_target_pairs={{0,4},{4,0},{1,5},{5,1},{2,6},{6,2},{3,7},{7,3},{8,12},{12,8},{9,1... | collective-permute-start | bytes 688136 | tf_op jit(solution)/shard_map/ppermute | solution.py:20
  25.5 1.5 %collective-permute-start.7 = (bf16[8,56,256]{2,1,0:T(8,128)(2,1)S(1)}, bf16[8,56,256]{2,1,0:T(8,128)(2,1)S(1)}, u32[]{:S(2)}, u32[]{:S(2)}) collective-permute-start(bf16[8,56,256]{2,1,0:T(8,128)(2,1)S(1)} %all-to-all-done.refs_0_), channel_id=1, source_target_pairs={{0,2},{1,3},{2,0},{3,1},{4,6},{5,7},{6,4},{7,5},{8,10},{9,11},{10,... | collective-permute-start | bytes 688136 | tf_op jit(solution)/shard_map/ppermute | solution.py:20
  27.0 0.0 collective-permute-done.9.refs_1_
  27.0 2.3 %collective-permute-done.8.refs_4_ = bf16[8,56,256]{2,1,0:T(8,128)(2,1)S(1)} collective-permute-done((bf16[8,56,256]{2,1,0:T(8,128)(2,1)S(1)}, bf16[8,56,256]{2,1,0:T(8,128)(2,1)S(1)}, u32[]{:S(2)}, u32[]{:S(2)}) %collective-permute-start.8) | collective-permute-done | bytes 229408 | tf_op jit(solution)/shard_map/ppermute | solution.py:20
  29.3 2.4 %collective-permute-start.12 = (bf16[8,56,256]{2,1,0:T(8,128)(2,1)S(1)}, bf16[8,56,256]{2,1,0:T(8,128)(2,1)S(1)}, u32[]{:S(2)}, u32[]{:S(2)}) collective-permute-start(bf16[8,56,256]{2,1,0:T(8,128)(2,1)S(1)} %collective-permute-done.8.refs_4_), channel_id=1, source_target_pairs={{0,2},{1,3},{2,0},{3,1},{4,6},{5,7},{6,4},{7,5},{8,10},{9,11},{10,... | collective-permute-start | bytes 688136 | tf_op jit(solution)/shard_map/ppermute | solution.py:20
  31.7 4.4 %collective-permute-done.3.refs_4_ = bf16[128,3584]{1,0:T(8,128)(2,1)S(1)} collective-permute-done((bf16[128,3584]{1,0:T(8,128)(2,1)}, bf16[128,3584]{1,0:T(8,128)(2,1)S(1)}, u32[]{:S(2)}, u32[]{:S(2)}) %collective-permute-start.3) | collective-permute-done | bytes 917536 | tf_op jit(solution)/shard_map/ppermute | solution.py:20
  36.1 1.9 %collective-permute-start.11 = (bf16[8,56,256]{2,1,0:T(8,128)(2,1)S(1)}, bf16[8,56,256]{2,1,0:T(8,128)(2,1)S(1)}, u32[]{:S(2)}, u32[]{:S(2)}) collective-permute-start(bf16[8,56,256]{2,1,0:T(8,128)(2,1)S(1)} %collective-permute-done.8.refs_4_), channel_id=1, source_target_pairs={{0,3},{1,0},{2,1},{3,2},{4,7},{5,4},{6,5},{7,6},{8,11},{9,8},{10,9... | collective-permute-start | bytes 688136 | tf_op jit(solution)/shard_map/ppermute | solution.py:20
  38.0 0.0 collective-permute-done.1.refs_2_
  38.0 2.2 %collective-permute-start.6 = (bf16[64,3584]{1,0:T(8,128)(2,1)S(1)}, bf16[64,3584]{1,0:T(8,128)(2,1)S(1)}, u32[]{:S(2)}, u32[]{:S(2)}) collective-permute-start(bf16[64,3584]{1,0:T(8,128)(2,1)S(1)} %slice.9), channel_id=1, source_target_pairs={{0,192},{64,0},{128,64},{192,128},{1,193},{65,1},{129,65},{193,129... | collective-permute-start | bytes 1376264 | tf_op jit(solution)/shard_map/ppermute | solution.py:20
  40.2 0.0 collective-permute-done.7.refs_2_
  40.2 0.1 collective-permute-start.5
  40.3 0.0 collective-permute-done.13.refs_7_
  40.3 5.1 %collective-permute-start = (bf16[128,3584]{1,0:T(8,128)(2,1)S(1)}, bf16[128,3584]{1,0:T(8,128)(2,1)S(1)}, u32[]{:S(2)}, u32[]{:S(2)}) collective-permute-start(bf16[128,3584]{1,0:T(8,128)(2,1)S(1)} %copy-done.1), channel_id=1, source_target_pairs={{0,32},{32,0},{1,33},{33,1},{2,34},{34,2},{3,35},{35,3},{4,36},{36... | collective-permute-start | bytes 2752520 | tf_op jit(solution)/shard_map/ppermute | solution.py:20
  45.4 0.1 collective-permute-start.4
  45.5 0.0 collective-permute-done.11.refs_5_
  45.5 1.1 %collective-permute-start.2 = (bf16[128,3584]{1,0:T(8,128)(2,1)S(1)}, bf16[128,3584]{1,0:T(8,128)(2,1)S(1)}, u32[]{:S(2)}, u32[]{:S(2)}) collective-permute-start(bf16[128,3584]{1,0:T(8,128)(2,1)S(1)} %collective-permute-done.1.refs_2_), channel_id=1, source_target_pairs={{0,32},{32,0},{1,33},{33,1},{2,34},{34,2},{3,35},{35,3},{4,36},{36... | collective-permute-start | bytes 2752520 | tf_op jit(solution)/shard_map/ppermute | solution.py:20
  46.6 1.3 %collective-permute-done.6.refs_8_ = bf16[64,3584]{1,0:T(8,128)(2,1)S(1)} collective-permute-done((bf16[64,3584]{1,0:T(8,128)(2,1)S(1)}, bf16[64,3584]{1,0:T(8,128)(2,1)S(1)}, u32[]{:S(2)}, u32[]{:S(2)}) %collective-permute-start.6) | collective-permute-done | bytes 458784 | tf_op jit(solution)/shard_map/ppermute | solution.py:20
  47.9 3.2 %collective-permute-done.5.refs_6_ = bf16[64,3584]{1,0:T(8,128)(2,1)S(1)} collective-permute-done((bf16[64,3584]{1,0:T(8,128)(2,1)S(1)}, bf16[64,3584]{1,0:T(8,128)(2,1)S(1)}, u32[]{:S(2)}, u32[]{:S(2)}) %collective-permute-start.5) | collective-permute-done | bytes 458784 | tf_op jit(solution)/shard_map/ppermute | solution.py:20
  51.1 3.4 %collective-permute-start.14 = (bf16[64,3584]{1,0:T(8,128)(2,1)S(1)}, bf16[64,3584]{1,0:T(8,128)(2,1)S(1)}, u32[]{:S(2)}, u32[]{:S(2)}) collective-permute-start(bf16[64,3584]{1,0:T(8,128)(2,1)S(1)} %collective-permute-done.5.refs_6_), channel_id=1, source_target_pairs={{0,32},{32,0},{1,33},{33,1},{2,34},{34,2},{3,35},{35,3},{4,36},{36... | collective-permute-start | bytes 1376264 | tf_op jit(solution)/shard_map/ppermute | solution.py:20
  54.5 0.0 collective-permute-start.15
  54.5 0.0 copy-start
  54.5 0.1 assemble.1
  54.6 0.0 collective-permute-done.4.refs_5_
  54.7 1.2 %collective-permute-done.14.refs_7_ = bf16[64,3584]{1,0:T(8,128)(2,1)S(1)} collective-permute-done((bf16[64,3584]{1,0:T(8,128)(2,1)S(1)}, bf16[64,3584]{1,0:T(8,128)(2,1)S(1)}, u32[]{:S(2)}, u32[]{:S(2)}) %collective-permute-start.14) | collective-permute-done | bytes 458784 | tf_op jit(solution)/shard_map/ppermute | solution.py:20
  55.9 0.7 collective-permute-done.15.refs_9_
  56.6 3.1 %student.1 = (f32[128,256]{1,0:T(8,128)S(1)}, f32[1,1024]{1,0:T(1,128)S(1)}) custom-call(bf16[128,3584]{1,0:T(8,128)(2,1)S(1)} %copy-done.1, bf16[128,3584]{1,0:T(8,128)(2,1)S(1)} %collective-permute-done.refs_1_, bf16[128,3584]{1,0:T(8,128)(2,1)S(1)} %collective-permute-done.1.refs_2_, bf16[128,3584]{1,0:T(8,128)(2,1)S(1)} %collective-permute-done.2.refs_3_, ...), custom_call_target="tpu_custom_call" | custom-call | flops 2113929216 | bytes 8388608 | tf_op jit(solution)/shard_map/student/pallas_call | solution.py:210
  59.7 0.1 collective-permute-start.18
  59.7 1.1 %collective-permute-start.17 = (f32[128,256]{1,0:T(8,128)S(1)}, f32[128,256]{1,0:T(8,128)S(1)}, u32[]{:S(2)}, u32[]{:S(2)}) collective-permute-start(f32[128,256]{1,0:T(8,128)S(1)} %get-tuple-element.26.refs_0_), channel_id=1, source_target_pairs={{0,128},{64,192},{128,0},{192,64},{1,129},{65,193},{129,1},{193,65... | collective-permute-start | bytes 393224 | tf_op jit(solution)/shard_map/ppermute | solution.py:20
  60.8 1.6 %collective-permute-start.16 = (f32[128,256]{1,0:T(8,128)S(1)}, f32[128,256]{1,0:T(8,128)S(1)}, u32[]{:S(2)}, u32[]{:S(2)}) collective-permute-start(f32[128,256]{1,0:T(8,128)S(1)} %get-tuple-element.26.refs_0_), channel_id=1, source_target_pairs={{0,192},{64,0},{128,64},{192,128},{1,193},{65,1},{129,65},{193,129... | collective-permute-start | bytes 393224 | tf_op jit(solution)/shard_map/ppermute | solution.py:20
  62.4 6.9 %collective-permute-start.23 = (f32[1,1024]{1,0:T(1,128)S(1)}, f32[1,1024]{1,0:T(1,128)S(1)}, u32[]{:S(2)}, u32[]{:S(2)}) collective-permute-start(f32[1,1024]{1,0:T(1,128)S(1)} %get-tuple-element.27.mine_ref), channel_id=1, source_target_pairs={{0,4},{4,0},{1,5},{5,1},{2,6},{6,2},{3,7},{7,3},{8,12},{12,8},{9,1... | collective-permute-start | bytes 12296 | tf_op jit(solution)/shard_map/ppermute | solution.py:20
  69.3 1.2 %collective-permute-start.19 = (f32[128,256]{1,0:T(8,128)S(1)}, f32[128,256]{1,0:T(8,128)S(1)}, u32[]{:S(2)}, u32[]{:S(2)}) collective-permute-start(f32[128,256]{1,0:T(8,128)S(1)} %get-tuple-element.26.refs_0_), channel_id=1, source_target_pairs={{0,32},{32,0},{1,33},{33,1},{2,34},{34,2},{3,35},{35,3},{4,36},{36... | collective-permute-start | bytes 393224 | tf_op jit(solution)/shard_map/ppermute | solution.py:20
  70.5 0.0 collective-permute-done.18.refs_3_
  70.5 0.0 collective-permute-start.22
  70.6 0.5 collective-permute-start.21
  71.1 0.1 collective-permute-start.20
  71.2 13.0 %all_to_all.10.refs_8_ = f32[32,1,1024]{2,1,0:T(1,128)S(1)} all-to-all(f32[32,1,1024]{2,1,0:T(1,128)S(1)} %both.1), channel_id=1, replica_groups=mesh['y'=4,'core'=2,'mp'=4,'z'=2,'x'=4] {'y','core','x'}, dimensions={0} | all-to-all | bytes 262144 | tf_op jit(solution)/shard_map/all_to_all | solution.py:235
  84.2 1.2 %finish.1 = (f32[128,1792]{1,0:T(8,128)}, f32[1792]{0:T(1024)}) custom-call(f32[128,256]{1,0:T(8,128)S(1)} %get-tuple-element.26.refs_0_, f32[128,256]{1,0:T(8,128)S(1)} %collective-permute-done.16.refs_1_, f32[128,256]{1,0:T(8,128)S(1)} %collective-permute-done.17.refs_2_, f32[128,256]{1,0:T(8,128)S(1)} %collective-permute-done.18.refs_3_, ...), custom_call_target="tpu_custom_call" | custom-call | tf_op jit(solution)/shard_map/finish/pallas_call | solution.py:238
  (20 shorter events, 0.1 us)
Async XLA Ops:
  0.6 0.9 %copy-start.2 = (bf16[56,1792]{1,0:T(8,128)(2,1)S(1)}, bf16[56,1792]{1,0:T(8,128)(2,1)}, u32[]{:S(2)}) copy-start(bf16[56,1792]{1,0:T(8,128)(2,1)} %weight_ref.1) | copy-start | bytes 602116
  2.3 12.8 %all-to-all-start = ((bf16[8,56,256]{2,1,0:T(8,128)(2,1)}), bf16[8,56,256]{2,1,0:T(8,128)(2,1)S(1)}, u32[]{:S(2)}, u32[]{:S(2)}) async-start(bf16[8,56,256]{2,1,0:T(8,128)(2,1)} %windows.1), calls=%async_computation | async-start | bytes 458752 | tf_op jit(solution)/shard_map/all_to_all | solution.py:180
  11.4 28.9 %copy-start.1 = (bf16[128,3584]{1,0:T(8,128)(2,1)S(1)}, bf16[128,3584]{1,0:T(8,128)(2,1)}, u32[]{:S(2)}) copy-start(bf16[128,3584]{1,0:T(8,128)(2,1)} %drive.1.refs_0_) | copy-start | bytes 2752516
  11.4 43.1 %copy-start.3 = (f32[1792]{0:T(1024)S(1)}, f32[1792]{0:T(1024)}, u32[]{:S(2)}) copy-start(f32[1792]{0:T(1024)} %param.7) | copy-start | bytes 21508
  15.0 21.1 %collective-permute-start.3 = (bf16[128,3584]{1,0:T(8,128)(2,1)}, bf16[128,3584]{1,0:T(8,128)(2,1)S(1)}, u32[]{:S(2)}, u32[]{:S(2)}) collective-permute-start(bf16[128,3584]{1,0:T(8,128)(2,1)} %drive.1.refs_0_), channel_id=1, source_target_pairs={{0,192},{64,0},{128,64},{192,128},{1,193},{65,1},{129,65},{193,129... | collective-permute-start | bytes 2752520 | tf_op jit(solution)/shard_map/ppermute | solution.py:20
  15.9 22.1 %collective-permute-start.1 = (bf16[128,3584]{1,0:T(8,128)(2,1)}, bf16[128,3584]{1,0:T(8,128)(2,1)S(1)}, u32[]{:S(2)}, u32[]{:S(2)}) collective-permute-start(bf16[128,3584]{1,0:T(8,128)(2,1)} %drive.1.refs_0_), channel_id=1, source_target_pairs={{0,64},{64,128},{128,192},{192,0},{1,65},{65,129},{129,193},{193,1... | collective-permute-start | bytes 2752520 | tf_op jit(solution)/shard_map/ppermute | solution.py:20
  16.5 9.0 %collective-permute-start.10 = (bf16[8,56,256]{2,1,0:T(8,128)(2,1)S(1)}, bf16[8,56,256]{2,1,0:T(8,128)(2,1)S(1)}, u32[]{:S(2)}, u32[]{:S(2)}) collective-permute-start(bf16[8,56,256]{2,1,0:T(8,128)(2,1)S(1)} %all-to-all-done.refs_0_), channel_id=1, source_target_pairs={{0,1},{1,2},{2,3},{3,0},{4,5},{5,6},{6,7},{7,4},{8,9},{9,10},{10,1... | collective-permute-start | bytes 688136 | tf_op jit(solution)/shard_map/ppermute | solution.py:20
  17.1 9.9 %collective-permute-start.9 = (bf16[8,56,256]{2,1,0:T(8,128)(2,1)S(1)}, bf16[8,56,256]{2,1,0:T(8,128)(2,1)S(1)}, u32[]{:S(2)}, u32[]{:S(2)}) collective-permute-start(bf16[8,56,256]{2,1,0:T(8,128)(2,1)S(1)} %all-to-all-done.refs_0_), channel_id=1, source_target_pairs={{0,3},{1,0},{2,1},{3,2},{4,7},{5,4},{6,5},{7,6},{8,11},{9,8},{10,9... | collective-permute-start | bytes 688136 | tf_op jit(solution)/shard_map/ppermute | solution.py:20
  19.2 10.1 %collective-permute-start.8 = (bf16[8,56,256]{2,1,0:T(8,128)(2,1)S(1)}, bf16[8,56,256]{2,1,0:T(8,128)(2,1)S(1)}, u32[]{:S(2)}, u32[]{:S(2)}) collective-permute-start(bf16[8,56,256]{2,1,0:T(8,128)(2,1)S(1)} %all-to-all-done.refs_0_), channel_id=1, source_target_pairs={{0,4},{4,0},{1,5},{5,1},{2,6},{6,2},{3,7},{7,3},{8,12},{12,8},{9,1... | collective-permute-start | bytes 688136 | tf_op jit(solution)/shard_map/ppermute | solution.py:20
  25.5 14.7 %collective-permute-start.7 = (bf16[8,56,256]{2,1,0:T(8,128)(2,1)S(1)}, bf16[8,56,256]{2,1,0:T(8,128)(2,1)S(1)}, u32[]{:S(2)}, u32[]{:S(2)}) collective-permute-start(bf16[8,56,256]{2,1,0:T(8,128)(2,1)S(1)} %all-to-all-done.refs_0_), channel_id=1, source_target_pairs={{0,2},{1,3},{2,0},{3,1},{4,6},{5,7},{6,4},{7,5},{8,10},{9,11},{10,... | collective-permute-start | bytes 688136 | tf_op jit(solution)/shard_map/ppermute | solution.py:20
  29.3 11.0 %collective-permute-start.13 = (bf16[8,56,256]{2,1,0:T(8,128)(2,1)S(1)}, bf16[8,56,256]{2,1,0:T(8,128)(2,1)S(1)}, u32[]{:S(2)}, u32[]{:S(2)}) collective-permute-start(bf16[8,56,256]{2,1,0:T(8,128)(2,1)S(1)} %collective-permute-done.8.refs_4_), channel_id=1, source_target_pairs={{0,1},{1,2},{2,3},{3,0},{4,5},{5,6},{6,7},{7,4},{8,9},{9,10},{10,1... | collective-permute-start | bytes 688136 | tf_op jit(solution)/shard_map/ppermute | solution.py:20
  29.3 16.1 %collective-permute-start.12 = (bf16[8,56,256]{2,1,0:T(8,128)(2,1)S(1)}, bf16[8,56,256]{2,1,0:T(8,128)(2,1)S(1)}, u32[]{:S(2)}, u32[]{:S(2)}) collective-permute-start(bf16[8,56,256]{2,1,0:T(8,128)(2,1)S(1)} %collective-permute-done.8.refs_4_), channel_id=1, source_target_pairs={{0,2},{1,3},{2,0},{3,1},{4,6},{5,7},{6,4},{7,5},{8,10},{9,11},{10,... | collective-permute-start | bytes 688136 | tf_op jit(solution)/shard_map/ppermute | solution.py:20
  36.1 9.4 %collective-permute-start.11 = (bf16[8,56,256]{2,1,0:T(8,128)(2,1)S(1)}, bf16[8,56,256]{2,1,0:T(8,128)(2,1)S(1)}, u32[]{:S(2)}, u32[]{:S(2)}) collective-permute-start(bf16[8,56,256]{2,1,0:T(8,128)(2,1)S(1)} %collective-permute-done.8.refs_4_), channel_id=1, source_target_pairs={{0,3},{1,0},{2,1},{3,2},{4,7},{5,4},{6,5},{7,6},{8,11},{9,8},{10,9... | collective-permute-start | bytes 688136 | tf_op jit(solution)/shard_map/ppermute | solution.py:20
  38.0 9.9 %collective-permute-start.6 = (bf16[64,3584]{1,0:T(8,128)(2,1)S(1)}, bf16[64,3584]{1,0:T(8,128)(2,1)S(1)}, u32[]{:S(2)}, u32[]{:S(2)}) collective-permute-start(bf16[64,3584]{1,0:T(8,128)(2,1)S(1)} %slice.9), channel_id=1, source_target_pairs={{0,192},{64,0},{128,64},{192,128},{1,193},{65,1},{129,65},{193,129... | collective-permute-start | bytes 1376264 | tf_op jit(solution)/shard_map/ppermute | solution.py:20
  40.2 10.8 %collective-permute-start.5 = (bf16[64,3584]{1,0:T(8,128)(2,1)S(1)}, bf16[64,3584]{1,0:T(8,128)(2,1)S(1)}, u32[]{:S(2)}, u32[]{:S(2)}) collective-permute-start(bf16[64,3584]{1,0:T(8,128)(2,1)S(1)} %slice.8), channel_id=1, source_target_pairs={{0,64},{64,128},{128,192},{192,0},{1,65},{65,129},{129,193},{193,1... | collective-permute-start | bytes 1376264 | tf_op jit(solution)/shard_map/ppermute | solution.py:20
  40.3 14.3 %collective-permute-start = (bf16[128,3584]{1,0:T(8,128)(2,1)S(1)}, bf16[128,3584]{1,0:T(8,128)(2,1)S(1)}, u32[]{:S(2)}, u32[]{:S(2)}) collective-permute-start(bf16[128,3584]{1,0:T(8,128)(2,1)S(1)} %copy-done.1), channel_id=1, source_target_pairs={{0,32},{32,0},{1,33},{33,1},{2,34},{34,2},{3,35},{35,3},{4,36},{36... | collective-permute-start | bytes 2752520 | tf_op jit(solution)/shard_map/ppermute | solution.py:20
  45.4 9.2 %collective-permute-start.4 = (bf16[128,3584]{1,0:T(8,128)(2,1)S(1)}, bf16[128,3584]{1,0:T(8,128)(2,1)S(1)}, u32[]{:S(2)}, u32[]{:S(2)}) collective-permute-start(bf16[128,3584]{1,0:T(8,128)(2,1)S(1)} %collective-permute-done.3.refs_4_), channel_id=1, source_target_pairs={{0,32},{32,0},{1,33},{33,1},{2,34},{34,2},{3,35},{35,3},{4,36},{36... | collective-permute-start | bytes 2752520 | tf_op jit(solution)/shard_map/ppermute | solution.py:20
  45.5 11.1 %collective-permute-start.2 = (bf16[128,3584]{1,0:T(8,128)(2,1)S(1)}, bf16[128,3584]{1,0:T(8,128)(2,1)S(1)}, u32[]{:S(2)}, u32[]{:S(2)}) collective-permute-start(bf16[128,3584]{1,0:T(8,128)(2,1)S(1)} %collective-permute-done.1.refs_2_), channel_id=1, source_target_pairs={{0,32},{32,0},{1,33},{33,1},{2,34},{34,2},{3,35},{35,3},{4,36},{36... | collective-permute-start | bytes 2752520 | tf_op jit(solution)/shard_map/ppermute | solution.py:20
  51.1 4.8 %collective-permute-start.14 = (bf16[64,3584]{1,0:T(8,128)(2,1)S(1)}, bf16[64,3584]{1,0:T(8,128)(2,1)S(1)}, u32[]{:S(2)}, u32[]{:S(2)}) collective-permute-start(bf16[64,3584]{1,0:T(8,128)(2,1)S(1)} %collective-permute-done.5.refs_6_), channel_id=1, source_target_pairs={{0,32},{32,0},{1,33},{33,1},{2,34},{34,2},{3,35},{35,3},{4,36},{36... | collective-permute-start | bytes 1376264 | tf_op jit(solution)/shard_map/ppermute | solution.py:20
  54.5 2.1 %collective-permute-start.15 = (bf16[64,3584]{1,0:T(8,128)(2,1)S(1)}, bf16[64,3584]{1,0:T(8,128)(2,1)S(1)}, u32[]{:S(2)}, u32[]{:S(2)}) collective-permute-start(bf16[64,3584]{1,0:T(8,128)(2,1)S(1)} %collective-permute-done.6.refs_8_), channel_id=1, source_target_pairs={{0,32},{32,0},{1,33},{33,1},{2,34},{34,2},{3,35},{35,3},{4,36},{36... | collective-permute-start | bytes 1376264 | tf_op jit(solution)/shard_map/ppermute | solution.py:20
  54.5 2.1 %copy-start = (bf16[128,3584]{1,0:T(8,128)(2,1)S(1)}, bf16[128,3584]{1,0:T(8,128)(2,1)}, u32[]{:S(2)}) copy-start(bf16[128,3584]{1,0:T(8,128)(2,1)} %refs_10_.1) | copy-start | bytes 2752516
  59.7 10.9 %collective-permute-start.18 = (f32[128,256]{1,0:T(8,128)S(1)}, f32[128,256]{1,0:T(8,128)S(1)}, u32[]{:S(2)}, u32[]{:S(2)}) collective-permute-start(f32[128,256]{1,0:T(8,128)S(1)} %get-tuple-element.26.refs_0_), channel_id=1, source_target_pairs={{0,64},{64,128},{128,192},{192,0},{1,65},{65,129},{129,193},{193,1... | collective-permute-start | bytes 393224 | tf_op jit(solution)/shard_map/ppermute | solution.py:20
  59.7 10.8 %collective-permute-start.17 = (f32[128,256]{1,0:T(8,128)S(1)}, f32[128,256]{1,0:T(8,128)S(1)}, u32[]{:S(2)}, u32[]{:S(2)}) collective-permute-start(f32[128,256]{1,0:T(8,128)S(1)} %get-tuple-element.26.refs_0_), channel_id=1, source_target_pairs={{0,128},{64,192},{128,0},{192,64},{1,129},{65,193},{129,1},{193,65... | collective-permute-start | bytes 393224 | tf_op jit(solution)/shard_map/ppermute | solution.py:20
  60.8 10.3 %collective-permute-start.16 = (f32[128,256]{1,0:T(8,128)S(1)}, f32[128,256]{1,0:T(8,128)S(1)}, u32[]{:S(2)}, u32[]{:S(2)}) collective-permute-start(f32[128,256]{1,0:T(8,128)S(1)} %get-tuple-element.26.refs_0_), channel_id=1, source_target_pairs={{0,192},{64,0},{128,64},{192,128},{1,193},{65,1},{129,65},{193,129... | collective-permute-start | bytes 393224 | tf_op jit(solution)/shard_map/ppermute | solution.py:20
  62.4 8.7 %collective-permute-start.23 = (f32[1,1024]{1,0:T(1,128)S(1)}, f32[1,1024]{1,0:T(1,128)S(1)}, u32[]{:S(2)}, u32[]{:S(2)}) collective-permute-start(f32[1,1024]{1,0:T(1,128)S(1)} %get-tuple-element.27.mine_ref), channel_id=1, source_target_pairs={{0,4},{4,0},{1,5},{5,1},{2,6},{6,2},{3,7},{7,3},{8,12},{12,8},{9,1... | collective-permute-start | bytes 12296 | tf_op jit(solution)/shard_map/ppermute | solution.py:20
  69.3 14.9 %collective-permute-start.19 = (f32[128,256]{1,0:T(8,128)S(1)}, f32[128,256]{1,0:T(8,128)S(1)}, u32[]{:S(2)}, u32[]{:S(2)}) collective-permute-start(f32[128,256]{1,0:T(8,128)S(1)} %get-tuple-element.26.refs_0_), channel_id=1, source_target_pairs={{0,32},{32,0},{1,33},{33,1},{2,34},{34,2},{3,35},{35,3},{4,36},{36... | collective-permute-start | bytes 393224 | tf_op jit(solution)/shard_map/ppermute | solution.py:20
  70.5 13.6 %collective-permute-start.22 = (f32[128,256]{1,0:T(8,128)S(1)}, f32[128,256]{1,0:T(8,128)S(1)}, u32[]{:S(2)}, u32[]{:S(2)}) collective-permute-start(f32[128,256]{1,0:T(8,128)S(1)} %collective-permute-done.18.refs_3_), channel_id=1, source_target_pairs={{0,32},{32,0},{1,33},{33,1},{2,34},{34,2},{3,35},{35,3},{4,36},{36... | collective-permute-start | bytes 393224 | tf_op jit(solution)/shard_map/ppermute | solution.py:20
  70.6 13.6 %collective-permute-start.21 = (f32[128,256]{1,0:T(8,128)S(1)}, f32[128,256]{1,0:T(8,128)S(1)}, u32[]{:S(2)}, u32[]{:S(2)}) collective-permute-start(f32[128,256]{1,0:T(8,128)S(1)} %collective-permute-done.17.refs_2_), channel_id=1, source_target_pairs={{0,32},{32,0},{1,33},{33,1},{2,34},{34,2},{3,35},{35,3},{4,36},{36... | collective-permute-start | bytes 393224 | tf_op jit(solution)/shard_map/ppermute | solution.py:20
  71.1 13.1 %collective-permute-start.20 = (f32[128,256]{1,0:T(8,128)S(1)}, f32[128,256]{1,0:T(8,128)S(1)}, u32[]{:S(2)}, u32[]{:S(2)}) collective-permute-start(f32[128,256]{1,0:T(8,128)S(1)} %collective-permute-done.16.refs_1_), channel_id=1, source_target_pairs={{0,32},{32,0},{1,33},{33,1},{2,34},{34,2},{3,35},{35,3},{4,36},{36... | collective-permute-start | bytes 393224 | tf_op jit(solution)/shard_map/ppermute | solution.py:20

commit v8 on v7

--- a/solution.py
+++ b/solution.py
@@ -12,7 +12,7 @@
 Y, CORE, Z, X = 4, 2, 2, 4
 STEPS = Y * CORE
 MIB = 1024 * 1024
-GROUPS = ((0, 16), (16, 32), (32, 48), (48, 64))
+GROUPS = ((0, 32), (32, 64), (64, 96), (96, 128))
 
 
 def around(x, axis, by):

time: 85.7 us -> 85.8 us (level)
  no operation moved by 1% of the time
where the time goes in v8:
time: 85.8 us; the launch traced here: 85.6 us
  starting transfers between devices  46.3 us (54%)
  waiting for transfers between devices  16.6 us (19%)
  blocking collectives  13 us (15%)
  Pallas kernels  7.9 us (9%)
  local copies, waits for them, and re-layouts  1.01 us (1%)
    ppermute x24, starting transfers between devices, around(): return lax.ppermute(x, axis, [(i, (i + by) % n) for i in range(n)])  39.7 us
    ppermute x24, waiting for transfers between devices, around(): return lax.ppermute(x, axis, [(i, (i + by) % n) for i in range(n)])  13 us
    all_to_all x1, blocking collectives, on_device(): grads = lax.all_to_all(grad, ('y', 'core', 'x'), 0, 0, tiled=True)  13 us
    all_to_all x1, starting transfers between devices, on_device(): near_w = lax.all_to_all(payload, ('y', 'core'), 0, 0, tiled=True)  6.54 us
    all_to_all x1, waiting for transfers between devices, on_device(): near_w = lax.all_to_all(payload, ('y', 'core'), 0, 0, tiled=True)  3.6 us
    pallas_call x1, Pallas kernels, on_device(): pl.pallas_call(functools.partial(student_kernel, tokens_all=tokens_all, s...  3.25 us
    pallas_call x1, Pallas kernels, on_device(): pl.pallas_call(drive_kernel, out_shape=jax.ShapeDtypeStruct((rows, deep),...  2.58 us
  transfers between devices with their start and end apart: 25, of which 7 were waited for; matrix products, arithmetic and copies ran while one was open for 0% of the time, Pallas kernels for 3%

profile of v8, /device:TPU:1, one launch (start us, length us, event | category | flops | bytes accessed | tf_op | source)
XLA Modules:
  0.0 85.6 jit_solution(10658215080181112920)
XLA Ops:
  0.6 0.9 %copy-done.2 = bf16[56,1792]{1,0:T(8,128)(2,1)S(1)} copy-done((bf16[56,1792]{1,0:T(8,128)(2,1)S(1)}, bf16[56,1792]{1,0:T(8,128)(2,1)}, u32[]{:S(2)}) %copy-start.2) | copy-done | bytes 200728
  1.6 0.7 windows.1
  2.3 6.5 %all-to-all-start = ((bf16[8,56,256]{2,1,0:T(8,128)(2,1)}), bf16[8,56,256]{2,1,0:T(8,128)(2,1)S(1)}, u32[]{:S(2)}, u32[]{:S(2)}) async-start(bf16[8,56,256]{2,1,0:T(8,128)(2,1)} %windows.1), calls=%async_computation | async-start | bytes 458752 | tf_op jit(solution)/shard_map/all_to_all | solution.py:180
  8.8 2.6 %drive.1.refs_0_ = bf16[128,3584]{1,0:T(8,128)(2,1)} custom-call(s32[1,128,3584]{2,1,0:T(8,128)} %mask_hbm.1, bf16[128,3584]{1,0:T(8,128)(2,1)} %refs_10_.1), custom_call_target="tpu_custom_call" | custom-call | tf_op jit(solution)/shard_map/drive/pallas_call | solution.py:157
  11.4 0.0 copy-start.1
  11.4 0.0 copy-start.3
  11.4 3.6 %all-to-all-done.refs_0_ = bf16[8,56,256]{2,1,0:T(8,128)(2,1)S(1)} async-done(((bf16[8,56,256]{2,1,0:T(8,128)(2,1)}), bf16[8,56,256]{2,1,0:T(8,128)(2,1)S(1)}, u32[]{:S(2)}, u32[]{:S(2)}) %all-to-all-start) | async-done | bytes 229408 | tf_op jit(solution)/shard_map/all_to_all | solution.py:180
  15.0 0.9 %collective-permute-start.3 = (bf16[128,3584]{1,0:T(8,128)(2,1)}, bf16[128,3584]{1,0:T(8,128)(2,1)S(1)}, u32[]{:S(2)}, u32[]{:S(2)}) collective-permute-start(bf16[128,3584]{1,0:T(8,128)(2,1)} %drive.1.refs_0_), channel_id=1, source_target_pairs={{0,192},{64,0},{128,64},{192,128},{1,193},{65,1},{129,65},{193,129... | collective-permute-start | bytes 2752520 | tf_op jit(solution)/shard_map/ppermute | solution.py:20
  15.9 0.6 collective-permute-start.1
  16.5 0.6 collective-permute-start.10
  17.1 2.1 %collective-permute-start.9 = (bf16[8,56,256]{2,1,0:T(8,128)(2,1)S(1)}, bf16[8,56,256]{2,1,0:T(8,128)(2,1)S(1)}, u32[]{:S(2)}, u32[]{:S(2)}) collective-permute-start(bf16[8,56,256]{2,1,0:T(8,128)(2,1)S(1)} %all-to-all-done.refs_0_), channel_id=1, source_target_pairs={{0,3},{1,0},{2,1},{3,2},{4,7},{5,4},{6,5},{7,6},{8,11},{9,8},{10,9... | collective-permute-start | bytes 688136 | tf_op jit(solution)/shard_map/ppermute | solution.py:20
  19.2 6.3 %collective-permute-start.8 = (bf16[8,56,256]{2,1,0:T(8,128)(2,1)S(1)}, bf16[8,56,256]{2,1,0:T(8,128)(2,1)S(1)}, u32[]{:S(2)}, u32[]{:S(2)}) collective-permute-start(bf16[8,56,256]{2,1,0:T(8,128)(2,1)S(1)} %all-to-all-done.refs_0_), channel_id=1, source_target_pairs={{0,4},{4,0},{1,5},{5,1},{2,6},{6,2},{3,7},{7,3},{8,12},{12,8},{9,1... | collective-permute-start | bytes 688136 | tf_op jit(solution)/shard_map/ppermute | solution.py:20
  25.5 0.0 collective-permute-done.10.refs_3_
  25.5 1.5 %collective-permute-start.7 = (bf16[8,56,256]{2,1,0:T(8,128)(2,1)S(1)}, bf16[8,56,256]{2,1,0:T(8,128)(2,1)S(1)}, u32[]{:S(2)}, u32[]{:S(2)}) collective-permute-start(bf16[8,56,256]{2,1,0:T(8,128)(2,1)S(1)} %all-to-all-done.refs_0_), channel_id=1, source_target_pairs={{0,2},{1,3},{2,0},{3,1},{4,6},{5,7},{6,4},{7,5},{8,10},{9,11},{10,... | collective-permute-start | bytes 688136 | tf_op jit(solution)/shard_map/ppermute | solution.py:20
  27.0 2.3 %collective-permute-done.8.refs_4_ = bf16[8,56,256]{2,1,0:T(8,128)(2,1)S(1)} collective-permute-done((bf16[8,56,256]{2,1,0:T(8,128)(2,1)S(1)}, bf16[8,56,256]{2,1,0:T(8,128)(2,1)S(1)}, u32[]{:S(2)}, u32[]{:S(2)}) %collective-permute-start.8) | collective-permute-done | bytes 229408 | tf_op jit(solution)/shard_map/ppermute | solution.py:20
  29.3 2.4 %collective-permute-start.12 = (bf16[8,56,256]{2,1,0:T(8,128)(2,1)S(1)}, bf16[8,56,256]{2,1,0:T(8,128)(2,1)S(1)}, u32[]{:S(2)}, u32[]{:S(2)}) collective-permute-start(bf16[8,56,256]{2,1,0:T(8,128)(2,1)S(1)} %collective-permute-done.8.refs_4_), channel_id=1, source_target_pairs={{0,2},{1,3},{2,0},{3,1},{4,6},{5,7},{6,4},{7,5},{8,10},{9,11},{10,... | collective-permute-start | bytes 688136 | tf_op jit(solution)/shard_map/ppermute | solution.py:20
  31.7 4.4 %collective-permute-done.3.refs_4_ = bf16[128,3584]{1,0:T(8,128)(2,1)S(1)} collective-permute-done((bf16[128,3584]{1,0:T(8,128)(2,1)}, bf16[128,3584]{1,0:T(8,128)(2,1)S(1)}, u32[]{:S(2)}, u32[]{:S(2)}) %collective-permute-start.3) | collective-permute-done | bytes 917536 | tf_op jit(solution)/shard_map/ppermute | solution.py:20
  36.1 1.9 %collective-permute-start.11 = (bf16[8,56,256]{2,1,0:T(8,128)(2,1)S(1)}, bf16[8,56,256]{2,1,0:T(8,128)(2,1)S(1)}, u32[]{:S(2)}, u32[]{:S(2)}) collective-permute-start(bf16[8,56,256]{2,1,0:T(8,128)(2,1)S(1)} %collective-permute-done.8.refs_4_), channel_id=1, source_target_pairs={{0,3},{1,0},{2,1},{3,2},{4,7},{5,4},{6,5},{7,6},{8,11},{9,8},{10,9... | collective-permute-start | bytes 688136 | tf_op jit(solution)/shard_map/ppermute | solution.py:20
  38.0 2.2 %collective-permute-start.6 = (bf16[64,3584]{1,0:T(8,128)(2,1)S(1)}, bf16[64,3584]{1,0:T(8,128)(2,1)S(1)}, u32[]{:S(2)}, u32[]{:S(2)}) collective-permute-start(bf16[64,3584]{1,0:T(8,128)(2,1)S(1)} %slice.9), channel_id=1, source_target_pairs={{0,192},{64,0},{128,64},{192,128},{1,193},{65,1},{129,65},{193,129... | collective-permute-start | bytes 1376264 | tf_op jit(solution)/shard_map/ppermute | solution.py:20
  40.2 0.1 collective-permute-start.5
  40.3 5.1 %collective-permute-start = (bf16[128,3584]{1,0:T(8,128)(2,1)S(1)}, bf16[128,3584]{1,0:T(8,128)(2,1)S(1)}, u32[]{:S(2)}, u32[]{:S(2)}) collective-permute-start(bf16[128,3584]{1,0:T(8,128)(2,1)S(1)} %copy-done.1), channel_id=1, source_target_pairs={{0,32},{32,0},{1,33},{33,1},{2,34},{34,2},{3,35},{35,3},{4,36},{36... | collective-permute-start | bytes 2752520 | tf_op jit(solution)/shard_map/ppermute | solution.py:20
  45.4 0.0 collective-permute-done.12.refs_6_
  45.4 0.1 collective-permute-start.4
  45.5 0.0 collective-permute-done.11.refs_5_
  45.5 1.1 %collective-permute-start.2 = (bf16[128,3584]{1,0:T(8,128)(2,1)S(1)}, bf16[128,3584]{1,0:T(8,128)(2,1)S(1)}, u32[]{:S(2)}, u32[]{:S(2)}) collective-permute-start(bf16[128,3584]{1,0:T(8,128)(2,1)S(1)} %collective-permute-done.1.refs_2_), channel_id=1, source_target_pairs={{0,32},{32,0},{1,33},{33,1},{2,34},{34,2},{3,35},{35,3},{4,36},{36... | collective-permute-start | bytes 2752520 | tf_op jit(solution)/shard_map/ppermute | solution.py:20
  46.6 1.3 %collective-permute-done.6.refs_8_ = bf16[64,3584]{1,0:T(8,128)(2,1)S(1)} collective-permute-done((bf16[64,3584]{1,0:T(8,128)(2,1)S(1)}, bf16[64,3584]{1,0:T(8,128)(2,1)S(1)}, u32[]{:S(2)}, u32[]{:S(2)}) %collective-permute-start.6) | collective-permute-done | bytes 458784 | tf_op jit(solution)/shard_map/ppermute | solution.py:20
  47.9 3.2 %collective-permute-done.5.refs_6_ = bf16[64,3584]{1,0:T(8,128)(2,1)S(1)} collective-permute-done((bf16[64,3584]{1,0:T(8,128)(2,1)S(1)}, bf16[64,3584]{1,0:T(8,128)(2,1)S(1)}, u32[]{:S(2)}, u32[]{:S(2)}) %collective-permute-start.5) | collective-permute-done | bytes 458784 | tf_op jit(solution)/shard_map/ppermute | solution.py:20
  51.1 3.4 %collective-permute-start.14 = (bf16[64,3584]{1,0:T(8,128)(2,1)S(1)}, bf16[64,3584]{1,0:T(8,128)(2,1)S(1)}, u32[]{:S(2)}, u32[]{:S(2)}) collective-permute-start(bf16[64,3584]{1,0:T(8,128)(2,1)S(1)} %collective-permute-done.5.refs_6_), channel_id=1, source_target_pairs={{0,32},{32,0},{1,33},{33,1},{2,34},{34,2},{3,35},{35,3},{4,36},{36... | collective-permute-start | bytes 1376264 | tf_op jit(solution)/shard_map/ppermute | solution.py:20
  54.5 0.0 collective-permute-start.15
  54.5 0.0 copy-start
  54.5 0.1 assemble.1
  54.6 0.0 collective-permute-done.refs_1_
  54.6 0.0 collective-permute-done.4.refs_5_
  54.7 1.2 %collective-permute-done.14.refs_7_ = bf16[64,3584]{1,0:T(8,128)(2,1)S(1)} collective-permute-done((bf16[64,3584]{1,0:T(8,128)(2,1)S(1)}, bf16[64,3584]{1,0:T(8,128)(2,1)S(1)}, u32[]{:S(2)}, u32[]{:S(2)}) %collective-permute-start.14) | collective-permute-done | bytes 458784 | tf_op jit(solution)/shard_map/ppermute | solution.py:20
  55.9 0.7 collective-permute-done.15.refs_9_
  56.6 0.0 collective-permute-done.2.refs_3_
  56.6 3.3 %student.1 = (f32[128,256]{1,0:T(8,128)S(1)}, f32[1,1024]{1,0:T(1,128)S(1)}) custom-call(bf16[128,3584]{1,0:T(8,128)(2,1)S(1)} %copy-done.1, bf16[128,3584]{1,0:T(8,128)(2,1)S(1)} %collective-permute-done.refs_1_, bf16[128,3584]{1,0:T(8,128)(2,1)S(1)} %collective-permute-done.1.refs_2_, bf16[128,3584]{1,0:T(8,128)(2,1)S(1)} %collective-permute-done.2.refs_3_, ...), custom_call_target="tpu_custom_call" | custom-call | flops 2113929216 | bytes 8388608 | tf_op jit(solution)/shard_map/student/pallas_call | solution.py:210
  59.8 0.1 collective-permute-start.18
  59.9 1.1 %collective-permute-start.17 = (f32[128,256]{1,0:T(8,128)S(1)}, f32[128,256]{1,0:T(8,128)S(1)}, u32[]{:S(2)}, u32[]{:S(2)}) collective-permute-start(f32[128,256]{1,0:T(8,128)S(1)} %get-tuple-element.26.refs_0_), channel_id=1, source_target_pairs={{0,128},{64,192},{128,0},{192,64},{1,129},{65,193},{129,1},{193,65... | collective-permute-start | bytes 393224 | tf_op jit(solution)/shard_map/ppermute | solution.py:20
  61.0 1.6 %collective-permute-start.16 = (f32[128,256]{1,0:T(8,128)S(1)}, f32[128,256]{1,0:T(8,128)S(1)}, u32[]{:S(2)}, u32[]{:S(2)}) collective-permute-start(f32[128,256]{1,0:T(8,128)S(1)} %get-tuple-element.26.refs_0_), channel_id=1, source_target_pairs={{0,192},{64,0},{128,64},{192,128},{1,193},{65,1},{129,65},{193,129... | collective-permute-start | bytes 393224 | tf_op jit(solution)/shard_map/ppermute | solution.py:20
  62.6 6.9 %collective-permute-start.23 = (f32[1,1024]{1,0:T(1,128)S(1)}, f32[1,1024]{1,0:T(1,128)S(1)}, u32[]{:S(2)}, u32[]{:S(2)}) collective-permute-start(f32[1,1024]{1,0:T(1,128)S(1)} %get-tuple-element.27.mine_ref), channel_id=1, source_target_pairs={{0,4},{4,0},{1,5},{5,1},{2,6},{6,2},{3,7},{7,3},{8,12},{12,8},{9,1... | collective-permute-start | bytes 12296 | tf_op jit(solution)/shard_map/ppermute | solution.py:20
  69.5 1.2 %collective-permute-start.19 = (f32[128,256]{1,0:T(8,128)S(1)}, f32[128,256]{1,0:T(8,128)S(1)}, u32[]{:S(2)}, u32[]{:S(2)}) collective-permute-start(f32[128,256]{1,0:T(8,128)S(1)} %get-tuple-element.26.refs_0_), channel_id=1, source_target_pairs={{0,32},{32,0},{1,33},{33,1},{2,34},{34,2},{3,35},{35,3},{4,36},{36... | collective-permute-start | bytes 393224 | tf_op jit(solution)/shard_map/ppermute | solution.py:20
  70.7 0.0 collective-permute-done.18.refs_3_
  70.7 0.0 collective-permute-start.22
  70.7 0.5 collective-permute-start.21
  71.2 0.1 collective-permute-start.20
  71.3 13.0 %all_to_all.10.refs_8_ = f32[32,1,1024]{2,1,0:T(1,128)S(1)} all-to-all(f32[32,1,1024]{2,1,0:T(1,128)S(1)} %both.1), channel_id=1, replica_groups=mesh['y'=4,'core'=2,'mp'=4,'z'=2,'x'=4] {'y','core','x'}, dimensions={0} | all-to-all | bytes 262144 | tf_op jit(solution)/shard_map/all_to_all | solution.py:235
  84.4 1.2 %finish.1 = (f32[128,1792]{1,0:T(8,128)}, f32[1792]{0:T(1024)}) custom-call(f32[128,256]{1,0:T(8,128)S(1)} %get-tuple-element.26.refs_0_, f32[128,256]{1,0:T(8,128)S(1)} %collective-permute-done.16.refs_1_, f32[128,256]{1,0:T(8,128)S(1)} %collective-permute-done.17.refs_2_, f32[128,256]{1,0:T(8,128)S(1)} %collective-permute-done.18.refs_3_, ...), custom_call_target="tpu_custom_call" | custom-call | tf_op jit(solution)/shard_map/finish/pallas_call | solution.py:238
  (20 shorter events, 0.1 us)
Async XLA Ops:
  0.6 0.9 %copy-start.2 = (bf16[56,1792]{1,0:T(8,128)(2,1)S(1)}, bf16[56,1792]{1,0:T(8,128)(2,1)}, u32[]{:S(2)}) copy-start(bf16[56,1792]{1,0:T(8,128)(2,1)} %weight_ref.1) | copy-start | bytes 602116
  2.3 12.8 %all-to-all-start = ((bf16[8,56,256]{2,1,0:T(8,128)(2,1)}), bf16[8,56,256]{2,1,0:T(8,128)(2,1)S(1)}, u32[]{:S(2)}, u32[]{:S(2)}) async-start(bf16[8,56,256]{2,1,0:T(8,128)(2,1)} %windows.1), calls=%async_computation | async-start | bytes 458752 | tf_op jit(solution)/shard_map/all_to_all | solution.py:180
  11.4 28.9 %copy-start.1 = (bf16[128,3584]{1,0:T(8,128)(2,1)S(1)}, bf16[128,3584]{1,0:T(8,128)(2,1)}, u32[]{:S(2)}) copy-start(bf16[128,3584]{1,0:T(8,128)(2,1)} %drive.1.refs_0_) | copy-start | bytes 2752516
  11.4 43.1 %copy-start.3 = (f32[1792]{0:T(1024)S(1)}, f32[1792]{0:T(1024)}, u32[]{:S(2)}) copy-start(f32[1792]{0:T(1024)} %param.7) | copy-start | bytes 21508
  15.0 21.1 %collective-permute-start.3 = (bf16[128,3584]{1,0:T(8,128)(2,1)}, bf16[128,3584]{1,0:T(8,128)(2,1)S(1)}, u32[]{:S(2)}, u32[]{:S(2)}) collective-permute-start(bf16[128,3584]{1,0:T(8,128)(2,1)} %drive.1.refs_0_), channel_id=1, source_target_pairs={{0,192},{64,0},{128,64},{192,128},{1,193},{65,1},{129,65},{193,129... | collective-permute-start | bytes 2752520 | tf_op jit(solution)/shard_map/ppermute | solution.py:20
  15.9 22.1 %collective-permute-start.1 = (bf16[128,3584]{1,0:T(8,128)(2,1)}, bf16[128,3584]{1,0:T(8,128)(2,1)S(1)}, u32[]{:S(2)}, u32[]{:S(2)}) collective-permute-start(bf16[128,3584]{1,0:T(8,128)(2,1)} %drive.1.refs_0_), channel_id=1, source_target_pairs={{0,64},{64,128},{128,192},{192,0},{1,65},{65,129},{129,193},{193,1... | collective-permute-start | bytes 2752520 | tf_op jit(solution)/shard_map/ppermute | solution.py:20
  16.5 9.0 %collective-permute-start.10 = (bf16[8,56,256]{2,1,0:T(8,128)(2,1)S(1)}, bf16[8,56,256]{2,1,0:T(8,128)(2,1)S(1)}, u32[]{:S(2)}, u32[]{:S(2)}) collective-permute-start(bf16[8,56,256]{2,1,0:T(8,128)(2,1)S(1)} %all-to-all-done.refs_0_), channel_id=1, source_target_pairs={{0,1},{1,2},{2,3},{3,0},{4,5},{5,6},{6,7},{7,4},{8,9},{9,10},{10,1... | collective-permute-start | bytes 688136 | tf_op jit(solution)/shard_map/ppermute | solution.py:20
  17.1 9.9 %collective-permute-start.9 = (bf16[8,56,256]{2,1,0:T(8,128)(2,1)S(1)}, bf16[8,56,256]{2,1,0:T(8,128)(2,1)S(1)}, u32[]{:S(2)}, u32[]{:S(2)}) collective-permute-start(bf16[8,56,256]{2,1,0:T(8,128)(2,1)S(1)} %all-to-all-done.refs_0_), channel_id=1, source_target_pairs={{0,3},{1,0},{2,1},{3,2},{4,7},{5,4},{6,5},{7,6},{8,11},{9,8},{10,9... | collective-permute-start | bytes 688136 | tf_op jit(solution)/shard_map/ppermute | solution.py:20
  19.2 10.1 %collective-permute-start.8 = (bf16[8,56,256]{2,1,0:T(8,128)(2,1)S(1)}, bf16[8,56,256]{2,1,0:T(8,128)(2,1)S(1)}, u32[]{:S(2)}, u32[]{:S(2)}) collective-permute-start(bf16[8,56,256]{2,1,0:T(8,128)(2,1)S(1)} %all-to-all-done.refs_0_), channel_id=1, source_target_pairs={{0,4},{4,0},{1,5},{5,1},{2,6},{6,2},{3,7},{7,3},{8,12},{12,8},{9,1... | collective-permute-start | bytes 688136 | tf_op jit(solution)/shard_map/ppermute | solution.py:20
  25.5 14.7 %collective-permute-start.7 = (bf16[8,56,256]{2,1,0:T(8,128)(2,1)S(1)}, bf16[8,56,256]{2,1,0:T(8,128)(2,1)S(1)}, u32[]{:S(2)}, u32[]{:S(2)}) collective-permute-start(bf16[8,56,256]{2,1,0:T(8,128)(2,1)S(1)} %all-to-all-done.refs_0_), channel_id=1, source_target_pairs={{0,2},{1,3},{2,0},{3,1},{4,6},{5,7},{6,4},{7,5},{8,10},{9,11},{10,... | collective-permute-start | bytes 688136 | tf_op jit(solution)/shard_map/ppermute | solution.py:20
  29.3 11.0 %collective-permute-start.13 = (bf16[8,56,256]{2,1,0:T(8,128)(2,1)S(1)}, bf16[8,56,256]{2,1,0:T(8,128)(2,1)S(1)}, u32[]{:S(2)}, u32[]{:S(2)}) collective-permute-start(bf16[8,56,256]{2,1,0:T(8,128)(2,1)S(1)} %collective-permute-done.8.refs_4_), channel_id=1, source_target_pairs={{0,1},{1,2},{2,3},{3,0},{4,5},{5,6},{6,7},{7,4},{8,9},{9,10},{10,1... | collective-permute-start | bytes 688136 | tf_op jit(solution)/shard_map/ppermute | solution.py:20
  29.3 16.1 %collective-permute-start.12 = (bf16[8,56,256]{2,1,0:T(8,128)(2,1)S(1)}, bf16[8,56,256]{2,1,0:T(8,128)(2,1)S(1)}, u32[]{:S(2)}, u32[]{:S(2)}) collective-permute-start(bf16[8,56,256]{2,1,0:T(8,128)(2,1)S(1)} %collective-permute-done.8.refs_4_), channel_id=1, source_target_pairs={{0,2},{1,3},{2,0},{3,1},{4,6},{5,7},{6,4},{7,5},{8,10},{9,11},{10,... | collective-permute-start | bytes 688136 | tf_op jit(solution)/shard_map/ppermute | solution.py:20
  36.1 9.4 %collective-permute-start.11 = (bf16[8,56,256]{2,1,0:T(8,128)(2,1)S(1)}, bf16[8,56,256]{2,1,0:T(8,128)(2,1)S(1)}, u32[]{:S(2)}, u32[]{:S(2)}) collective-permute-start(bf16[8,56,256]{2,1,0:T(8,128)(2,1)S(1)} %collective-permute-done.8.refs_4_), channel_id=1, source_target_pairs={{0,3},{1,0},{2,1},{3,2},{4,7},{5,4},{6,5},{7,6},{8,11},{9,8},{10,9... | collective-permute-start | bytes 688136 | tf_op jit(solution)/shard_map/ppermute | solution.py:20
  38.0 9.9 %collective-permute-start.6 = (bf16[64,3584]{1,0:T(8,128)(2,1)S(1)}, bf16[64,3584]{1,0:T(8,128)(2,1)S(1)}, u32[]{:S(2)}, u32[]{:S(2)}) collective-permute-start(bf16[64,3584]{1,0:T(8,128)(2,1)S(1)} %slice.9), channel_id=1, source_target_pairs={{0,192},{64,0},{128,64},{192,128},{1,193},{65,1},{129,65},{193,129... | collective-permute-start | bytes 1376264 | tf_op jit(solution)/shard_map/ppermute | solution.py:20
  40.2 10.8 %collective-permute-start.5 = (bf16[64,3584]{1,0:T(8,128)(2,1)S(1)}, bf16[64,3584]{1,0:T(8,128)(2,1)S(1)}, u32[]{:S(2)}, u32[]{:S(2)}) collective-permute-start(bf16[64,3584]{1,0:T(8,128)(2,1)S(1)} %slice.8), channel_id=1, source_target_pairs={{0,64},{64,128},{128,192},{192,0},{1,65},{65,129},{129,193},{193,1... | collective-permute-start | bytes 1376264 | tf_op jit(solution)/shard_map/ppermute | solution.py:20
  40.3 14.3 %collective-permute-start = (bf16[128,3584]{1,0:T(8,128)(2,1)S(1)}, bf16[128,3584]{1,0:T(8,128)(2,1)S(1)}, u32[]{:S(2)}, u32[]{:S(2)}) collective-permute-start(bf16[128,3584]{1,0:T(8,128)(2,1)S(1)} %copy-done.1), channel_id=1, source_target_pairs={{0,32},{32,0},{1,33},{33,1},{2,34},{34,2},{3,35},{35,3},{4,36},{36... | collective-permute-start | bytes 2752520 | tf_op jit(solution)/shard_map/ppermute | solution.py:20
  45.4 9.2 %collective-permute-start.4 = (bf16[128,3584]{1,0:T(8,128)(2,1)S(1)}, bf16[128,3584]{1,0:T(8,128)(2,1)S(1)}, u32[]{:S(2)}, u32[]{:S(2)}) collective-permute-start(bf16[128,3584]{1,0:T(8,128)(2,1)S(1)} %collective-permute-done.3.refs_4_), channel_id=1, source_target_pairs={{0,32},{32,0},{1,33},{33,1},{2,34},{34,2},{3,35},{35,3},{4,36},{36... | collective-permute-start | bytes 2752520 | tf_op jit(solution)/shard_map/ppermute | solution.py:20
  45.5 11.1 %collective-permute-start.2 = (bf16[128,3584]{1,0:T(8,128)(2,1)S(1)}, bf16[128,3584]{1,0:T(8,128)(2,1)S(1)}, u32[]{:S(2)}, u32[]{:S(2)}) collective-permute-start(bf16[128,3584]{1,0:T(8,128)(2,1)S(1)} %collective-permute-done.1.refs_2_), channel_id=1, source_target_pairs={{0,32},{32,0},{1,33},{33,1},{2,34},{34,2},{3,35},{35,3},{4,36},{36... | collective-permute-start | bytes 2752520 | tf_op jit(solution)/shard_map/ppermute | solution.py:20
  51.1 4.8 %collective-permute-start.14 = (bf16[64,3584]{1,0:T(8,128)(2,1)S(1)}, bf16[64,3584]{1,0:T(8,128)(2,1)S(1)}, u32[]{:S(2)}, u32[]{:S(2)}) collective-permute-start(bf16[64,3584]{1,0:T(8,128)(2,1)S(1)} %collective-permute-done.5.refs_6_), channel_id=1, source_target_pairs={{0,32},{32,0},{1,33},{33,1},{2,34},{34,2},{3,35},{35,3},{4,36},{36... | collective-permute-start | bytes 1376264 | tf_op jit(solution)/shard_map/ppermute | solution.py:20
  54.5 2.1 %collective-permute-start.15 = (bf16[64,3584]{1,0:T(8,128)(2,1)S(1)}, bf16[64,3584]{1,0:T(8,128)(2,1)S(1)}, u32[]{:S(2)}, u32[]{:S(2)}) collective-permute-start(bf16[64,3584]{1,0:T(8,128)(2,1)S(1)} %collective-permute-done.6.refs_8_), channel_id=1, source_target_pairs={{0,32},{32,0},{1,33},{33,1},{2,34},{34,2},{3,35},{35,3},{4,36},{36... | collective-permute-start | bytes 1376264 | tf_op jit(solution)/shard_map/ppermute | solution.py:20
  54.5 2.1 %copy-start = (bf16[128,3584]{1,0:T(8,128)(2,1)S(1)}, bf16[128,3584]{1,0:T(8,128)(2,1)}, u32[]{:S(2)}) copy-start(bf16[128,3584]{1,0:T(8,128)(2,1)} %refs_10_.1) | copy-start | bytes 2752516
  59.8 10.9 %collective-permute-start.18 = (f32[128,256]{1,0:T(8,128)S(1)}, f32[128,256]{1,0:T(8,128)S(1)}, u32[]{:S(2)}, u32[]{:S(2)}) collective-permute-start(f32[128,256]{1,0:T(8,128)S(1)} %get-tuple-element.26.refs_0_), channel_id=1, source_target_pairs={{0,64},{64,128},{128,192},{192,0},{1,65},{65,129},{129,193},{193,1... | collective-permute-start | bytes 393224 | tf_op jit(solution)/shard_map/ppermute | solution.py:20
  59.9 10.8 %collective-permute-start.17 = (f32[128,256]{1,0:T(8,128)S(1)}, f32[128,256]{1,0:T(8,128)S(1)}, u32[]{:S(2)}, u32[]{:S(2)}) collective-permute-start(f32[128,256]{1,0:T(8,128)S(1)} %get-tuple-element.26.refs_0_), channel_id=1, source_target_pairs={{0,128},{64,192},{128,0},{192,64},{1,129},{65,193},{129,1},{193,65... | collective-permute-start | bytes 393224 | tf_op jit(solution)/shard_map/ppermute | solution.py:20
  61.0 10.3 %collective-permute-start.16 = (f32[128,256]{1,0:T(8,128)S(1)}, f32[128,256]{1,0:T(8,128)S(1)}, u32[]{:S(2)}, u32[]{:S(2)}) collective-permute-start(f32[128,256]{1,0:T(8,128)S(1)} %get-tuple-element.26.refs_0_), channel_id=1, source_target_pairs={{0,192},{64,0},{128,64},{192,128},{1,193},{65,1},{129,65},{193,129... | collective-permute-start | bytes 393224 | tf_op jit(solution)/shard_map/ppermute | solution.py:20
  62.6 8.7 %collective-permute-start.23 = (f32[1,1024]{1,0:T(1,128)S(1)}, f32[1,1024]{1,0:T(1,128)S(1)}, u32[]{:S(2)}, u32[]{:S(2)}) collective-permute-start(f32[1,1024]{1,0:T(1,128)S(1)} %get-tuple-element.27.mine_ref), channel_id=1, source_target_pairs={{0,4},{4,0},{1,5},{5,1},{2,6},{6,2},{3,7},{7,3},{8,12},{12,8},{9,1... | collective-permute-start | bytes 12296 | tf_op jit(solution)/shard_map/ppermute | solution.py:20
  69.5 14.9 %collective-permute-start.19 = (f32[128,256]{1,0:T(8,128)S(1)}, f32[128,256]{1,0:T(8,128)S(1)}, u32[]{:S(2)}, u32[]{:S(2)}) collective-permute-start(f32[128,256]{1,0:T(8,128)S(1)} %get-tuple-element.26.refs_0_), channel_id=1, source_target_pairs={{0,32},{32,0},{1,33},{33,1},{2,34},{34,2},{3,35},{35,3},{4,36},{36... | collective-permute-start | bytes 393224 | tf_op jit(solution)/shard_map/ppermute | solution.py:20
  70.7 13.6 %collective-permute-start.22 = (f32[128,256]{1,0:T(8,128)S(1)}, f32[128,256]{1,0:T(8,128)S(1)}, u32[]{:S(2)}, u32[]{:S(2)}) collective-permute-start(f32[128,256]{1,0:T(8,128)S(1)} %collective-permute-done.18.refs_3_), channel_id=1, source_target_pairs={{0,32},{32,0},{1,33},{33,1},{2,34},{34,2},{3,35},{35,3},{4,36},{36... | collective-permute-start | bytes 393224 | tf_op jit(solution)/shard_map/ppermute | solution.py:20
  70.7 13.6 %collective-permute-start.21 = (f32[128,256]{1,0:T(8,128)S(1)}, f32[128,256]{1,0:T(8,128)S(1)}, u32[]{:S(2)}, u32[]{:S(2)}) collective-permute-start(f32[128,256]{1,0:T(8,128)S(1)} %collective-permute-done.17.refs_2_), channel_id=1, source_target_pairs={{0,32},{32,0},{1,33},{33,1},{2,34},{34,2},{3,35},{35,3},{4,36},{36... | collective-permute-start | bytes 393224 | tf_op jit(solution)/shard_map/ppermute | solution.py:20
  71.2 13.1 %collective-permute-start.20 = (f32[128,256]{1,0:T(8,128)S(1)}, f32[128,256]{1,0:T(8,128)S(1)}, u32[]{:S(2)}, u32[]{:S(2)}) collective-permute-start(f32[128,256]{1,0:T(8,128)S(1)} %collective-permute-done.16.refs_1_), channel_id=1, source_target_pairs={{0,32},{32,0},{1,33},{33,1},{2,34},{34,2},{3,35},{35,3},{4,36},{36... | collective-permute-start | bytes 393224 | tf_op jit(solution)/shard_map/ppermute | solution.py:20
